TPU v7x, 32 devices: a whole 2x2x4 slice. The times are simulated.
32 devices in a mesh: win: 2 (over y), gz: 4 (over z), gy: 2 (over x), gx: 2 (over core).
Axes of the slice: x: 2, y: 2, z: 4, core: 2. Of those that a mesh axis runs over, the one named last changes fastest.
Arguments:
- noisy: float32 [32, 16, 256], P(('win', 'gz'), 'gy', 'gx'), parts along dimension 0, may hold values from -6 to 6
- first_weight: float32 [32, 1, 27], replicated, may hold values from -1.25 to 1.25
- first_bias: float32 [16], replicated, may hold values from -8 to -3
- second_weight: float32 [32, 16, 27], replicated, may hold values from -0.3125 to 0.3125
- second_bias: float32 [16], replicated, may hold values from -8 to -3
- head_weight: float32 [16], replicated, may hold values from -18 to 18
- seg_weight_in: float32 [16, 1, 27], replicated, may hold values from -1.25 to 1.25
- seg_bias_in: float32 [16], replicated, may hold values from -3 to 3
- seg_weight_out: float32 [16, 16, 27], replicated, may hold values from -0.3125 to 0.3125
- seg_bias_out: float32 [16], replicated, may hold values from -3 to 3
Outputs:
- denoised: float32 [32, 16, 256], P(('win', 'gz'), 'gy', 'gx'), parts along dimension 0
- segmented: float32 [16, 32, 16, 256], P(None, ('win', 'gz'), 'gy', 'gx'), parts along dimension 1
There are 2 independent parts, one for each index of `win`. A program takes and returns all parts, laid end to end along the dimension named above; an argument that names none is the same for every part. Nothing has to cross between parts.
All inputs are finite; a program needn't handle non-finite values.
Results may differ from a plain program's by a relative error of at most 0.00029.
Values sent between devices are 32-bit elements; how exact they have to be, the bound alone decides.
No kernel may reach another device: no remote copies, remote signals or barrier semaphores. Data moves between devices by JAX's collectives and lax.ppermute only.
A program may use at most 64 MiB of HBM per device.

v0:
```python
import jax
import jax.numpy as jnp
from jax import lax
from jax.sharding import PartitionSpec as P


def shifted(value, axis, steps):
    count = lax.axis_size(axis)
    first, last = (max(0, -steps), min(count, count - steps))
    return lax.ppermute(value, axis, [(source, source + steps) for source in range(first, last)])


def with_halo(block, sides, width):
    for axis, dim in sides:
        count = lax.axis_size(axis)
        forward = [(i, i + 1) for i in range(count - 1)]
        backward = [(target, source) for source, target in forward]
        low = lax.ppermute(
            lax.slice_in_dim(block, block.shape[dim] - width, None, axis=dim), axis, forward
        )
        high = lax.ppermute(lax.slice_in_dim(block, 0, width, axis=dim), axis, backward)
        block = jnp.concatenate([low, block, high], axis=dim)
    return block


def convolve(padded, weight):
    depth = padded.shape[1] - 2
    height = padded.shape[2] - 2
    width = padded.shape[3] - 2
    total = jnp.zeros((weight.shape[0], depth, height, width), jnp.float32)
    for tap in range(27):
        step_z = tap // 9
        step_y = tap // 3 % 3
        step_x = tap % 3
        piece = padded[
            :, step_z : step_z + depth, step_y : step_y + height, step_x : step_x + width
        ]
        total = total + jnp.einsum(
            "oc,czyx->ozyx", weight[:, :, tap], piece, precision=lax.Precision.HIGHEST
        )
    return total


def affine(earlier, later):
    return (earlier[0] * later[0], later[0] * earlier[1] + later[1])


def recurrent(padded, weight, bias, backward):
    channels = bias.shape[0]
    pre = convolve(padded, weight)
    cand = jnp.tanh(pre[:channels])
    keep = jax.nn.sigmoid(-(pre[channels:] + bias[:, None, None, None]))
    inject = (1.0 - keep) * cand
    if backward:
        keep = jnp.flip(keep, 1)
        inject = jnp.flip(inject, 1)
    cum_keep, cum_inject = lax.associative_scan(affine, (keep, inject), axis=1)
    total_keep = cum_keep[:, -1]
    total_inject = cum_inject[:, -1]
    offset = -1 if backward else 1

    def relay(turn, carry):
        return shifted(total_keep * carry + total_inject, "gz", offset)

    carry = lax.fori_loop(0, lax.axis_size("gz") - 1, relay, jnp.zeros_like(total_inject))
    hidden = cum_keep * carry[:, None] + cum_inject
    if backward:
        hidden = jnp.flip(hidden, 1)
    return hidden


def inside_mask(length, where, count):
    places = jnp.arange(length + 2)
    outside = (places == 0) & (where == 0) | (places == length + 1) & (where == count - 1)
    return jnp.where(outside, 0.0, 1.0).astype(jnp.float32)


def body(
    noisy,
    first_weight,
    first_bias,
    second_weight,
    second_bias,
    head_weight,
    seg_weight_in,
    seg_bias_in,
    seg_weight_out,
    seg_bias_out,
):
    noisy_pad = with_halo(noisy[None], (("gz", 1), ("gy", 2), ("gx", 3)), 1)
    first_hidden = recurrent(noisy_pad, first_weight, first_bias, False)
    hidden_pad = with_halo(first_hidden, (("gz", 1), ("gy", 2), ("gx", 3)), 1)
    second_hidden = recurrent(hidden_pad, second_weight, second_bias, True)
    denoised = noisy + jnp.einsum(
        "c,czyx->zyx", head_weight, second_hidden, precision=lax.Precision.HIGHEST
    )
    deep_pad = with_halo(denoised[None], (("gz", 1), ("gy", 2), ("gx", 3)), 2)
    grown = jnp.maximum(convolve(deep_pad, seg_weight_in) + seg_bias_in[:, None, None, None], 0.0)
    mask_z = inside_mask(denoised.shape[0], lax.axis_index("gz"), lax.axis_size("gz"))
    mask_y = inside_mask(denoised.shape[1], lax.axis_index("gy"), lax.axis_size("gy"))
    mask_x = inside_mask(denoised.shape[2], lax.axis_index("gx"), lax.axis_size("gx"))
    feature_pad = (
        grown * (mask_z[:, None, None] * mask_y[None, :, None] * mask_x[None, None, :])[None]
    )
    segmented = convolve(feature_pad, seg_weight_out) + seg_bias_out[:, None, None, None]
    return (denoised, segmented)


def solution(mesh):
    in_specs = (P(("win", "gz"), "gy", "gx"), P(), P(), P(), P(), P(), P(), P(), P(), P())
    out_specs = (P(("win", "gz"), "gy", "gx"), P(None, ("win", "gz"), "gy", "gx"))
    return jax.shard_map(body, mesh=mesh, in_specs=in_specs, out_specs=out_specs, check_vma=False)
```

profile of v0, /device:TPU:1, one launch (start us, length us, event | category | flops | bytes accessed | tf_op | source)
XLA Modules:
  0.0 146.8 jit_solution(1202628407863394762)
XLA Ops:
  1.4 4.0 %collective-permute-start.2 = (f32[1,1,8,128]{3,2,1,0:T(8,128)S(1)}, f32[1,1,8,128]{3,2,1,0:T(8,128)S(1)}, u32[]{:S(2)}, u32[]{:S(2)}) collective-permute-start(f32[1,1,8,128]{3,2,1,0:T(8,128)S(1)} %get-tuple-element.241), channel_id=1, source_target_pairs={{0,4},{4,8},{8,12},{1,5},{5,9},{9,13},{2,6},{6,10},{10,14},{3,7},{... | collective-permute-start | bytes 12296 | tf_op jit(solution)/shard_map/ppermute | solution.py:18
  6.7 2.8 %fusion.224 = (f32[16,16,1]{2,1,0:T(8,128)}, f32[16,16,1]{2,1,0:T(8,128)}, f32[16,16,1]{2,1,0:T(8,128)}, f32[16,16,1]{2,1,0:T(8,128)}, f32[16,16,1]{2,1,0:T(8,12...) fusion(f32[16,16,27]{2,1,0:T(8,128)} %param.22), kind=kLoop, calls=%fused_computation.456 | loop fusion | bytes 16384 | tf_op jit(solution)/shard_map/slice | solution.py:39
  9.5 1.5 %fusion.223 = (f32[16,16,1]{2,1,0:T(8,128)S(1)}, f32[16,16,1]{2,1,0:T(8,128)S(1)}, f32[16,16,1]{2,1,0:T(8,128)S(1)}, f32[16,16,1]{2,1,0:T(8,128)S(1)}, f32[16,16...) fusion(f32[16,16,27]{2,1,0:T(8,128)S(1)} %copy-done.1), kind=kLoop, calls=%fused_computation.455 | loop fusion | bytes 38912 | tf_op jit(solution)/shard_map/slice | solution.py:39
  11.8 3.1 %collective-permute-start.4 = (f32[1,6,1,128]{3,2,1,0:T(1,128)S(1)}, f32[1,6,1,128]{3,2,1,0:T(1,128)S(1)}, u32[]{:S(2)}, u32[]{:S(2)}) collective-permute-start(f32[1,6,1,128]{3,2,1,0:T(1,128)S(1)} %get-tuple-element.235), channel_id=1, source_target_pairs={{0,2},{1,3},{4,6},{5,7},{8,10},{9,11},{12,14},{13,15},{16,18},{17,... | collective-permute-start | bytes 9224 | tf_op jit(solution)/shard_map/ppermute | solution.py:18
  16.3 3.0 %collective-permute-done.5 = f32[1,6,1,128]{3,2,1,0:T(1,128)S(1)} collective-permute-done((f32[1,6,1,128]{3,2,1,0:T(1,128)S(1)}, f32[1,6,1,128]{3,2,1,0:T(1,128)S(1)}, u32[]{:S(2)}, u32[]{:S(2)}) %collective-permute-start.5) | collective-permute-done | bytes 3104 | tf_op jit(solution)/shard_map/ppermute | solution.py:21
  20.7 4.3 %collective-permute-start.7 = (f32[1,6,10,1]{3,2,1,0:T(8,128)S(1)}, f32[1,6,10,1]{3,2,1,0:T(8,128)S(1)}, u32[]{:S(2)}, u32[]{:S(2)}) collective-permute-start(f32[1,6,10,1]{3,2,1,0:T(8,128)S(1)} %get-tuple-element.228), channel_id=1, source_target_pairs={{1,0},{3,2},{5,4},{7,6},{9,8},{11,10},{13,12},{15,14},{17,16},{19,... | collective-permute-start | bytes 728 | tf_op jit(solution)/shard_map/ppermute | solution.py:21
  28.3 15.7 %while.20 = (s32[]{:T(128)}, f32[16,8,128]{2,1,0:T(8,128)S(1)}, f32[16,8,128]{2,1,0:T(8,128)S(1)}, f32[16,8,128]{2,1,0:T(8,128)S(1)}, s32[]{:T(128)}) while((s32[]{:T(128)}, f32[16,8,128]{2,1,0:T(8,128)S(1)}, f32[16,8,128]{2,1,0:T(8,128)S(1)}, f32[16,8,128]{2,1,0:T(8,128)S(1)}, s32[]{:T(128)}) %tuple.203), condition=%wide.region_1.0_spmd, body=%wide.region_0.0_spmd.sunk | while | flops 32770 | bytes 524389 | solution.py:65
  28.3 4.3 %collective-permute-start = (f32[16,8,128]{2,1,0:T(8,128)S(1)}, f32[16,8,128]{2,1,0:T(8,128)S(1)}, u32[]{:S(2)}, u32[]{:S(2)}) collective-permute-start(f32[16,8,128]{2,1,0:T(8,128)S(1)} %multiply_add_fusion.6), channel_id=1, source_target_pairs={{0,4},{4,8},{8,12},{1,5},{5,9},{9,13},{2,6},{6,10},{10,14},{3,7},{... | collective-permute-start | bytes 196616 | tf_op jit(solution)/shard_map/while/body/eval_jaxpr/ppermute | solution.py:10
  33.9 3.7 %collective-permute-start = (f32[16,8,128]{2,1,0:T(8,128)S(1)}, f32[16,8,128]{2,1,0:T(8,128)S(1)}, u32[]{:S(2)}, u32[]{:S(2)}) collective-permute-start(f32[16,8,128]{2,1,0:T(8,128)S(1)} %multiply_add_fusion.6), channel_id=1, source_target_pairs={{0,4},{4,8},{8,12},{1,5},{5,9},{9,13},{2,6},{6,10},{10,14},{3,7},{... | collective-permute-start | bytes 196616 | tf_op jit(solution)/shard_map/while/body/eval_jaxpr/ppermute | solution.py:10
  39.0 3.7 %collective-permute-start = (f32[16,8,128]{2,1,0:T(8,128)S(1)}, f32[16,8,128]{2,1,0:T(8,128)S(1)}, u32[]{:S(2)}, u32[]{:S(2)}) collective-permute-start(f32[16,8,128]{2,1,0:T(8,128)S(1)} %multiply_add_fusion.6), channel_id=1, source_target_pairs={{0,4},{4,8},{8,12},{1,5},{5,9},{9,13},{2,6},{6,10},{10,14},{3,7},{... | collective-permute-start | bytes 196616 | tf_op jit(solution)/shard_map/while/body/eval_jaxpr/ppermute | solution.py:10
  44.1 3.8 %collective-permute-start.8 = (f32[16,1,8,128]{3,0,2,1:T(8,128)S(1)}, f32[16,1,8,128]{3,0,2,1:T(8,128)S(1)}, u32[]{:S(2)}, u32[]{:S(2)}) collective-permute-start(f32[16,1,8,128]{3,0,2,1:T(8,128)S(1)} %get-tuple-element.129), channel_id=1, source_target_pairs={{0,4},{4,8},{8,12},{1,5},{5,9},{9,13},{2,6},{6,10},{10,14},{3,7},{... | collective-permute-start | bytes 196616 | tf_op jit(solution)/shard_map/ppermute | solution.py:18
  49.9 3.1 %collective-permute-done.9 = f32[16,1,8,128]{3,0,2,1:T(8,128)S(1)} collective-permute-done((f32[16,1,8,128]{3,0,2,1:T(8,128)S(1)}, f32[16,1,8,128]{3,0,2,1:T(8,128)S(1)}, u32[]{:S(2)}, u32[]{:S(2)}) %collective-permute-start.9) | collective-permute-done | bytes 65568 | tf_op jit(solution)/shard_map/ppermute | solution.py:21
  53.0 1.4 collective-permute-start.10
  56.9 2.3 %collective-permute-done.11 = f32[16,6,1,128]{3,0,2,1:T(8,128)S(1)} collective-permute-done((f32[16,6,1,128]{3,0,2,1:T(8,128)S(1)}, f32[16,6,1,128]{3,0,2,1:T(8,128)S(1)}, u32[]{:S(2)}, u32[]{:S(2)}) %collective-permute-start.11) | collective-permute-done | bytes 49184 | tf_op jit(solution)/shard_map/ppermute | solution.py:21
  60.7 8.8 %collective-permute-start.13 = (f32[16,6,10,1]{3,0,2,1:T(8,128)S(1)}, f32[16,6,10,1]{3,0,2,1:T(8,128)S(1)}, u32[]{:S(2)}, u32[]{:S(2)}) collective-permute-start(f32[16,6,10,1]{3,0,2,1:T(8,128)S(1)} %get-tuple-element.118), channel_id=1, source_target_pairs={{1,0},{3,2},{5,4},{7,6},{9,8},{11,10},{13,12},{15,14},{17,16},{19,... | collective-permute-start | bytes 11528 | tf_op jit(solution)/shard_map/ppermute | solution.py:21
  87.3 15.7 %while.21 = (s32[]{:T(128)}, f32[16,8,128]{2,1,0:T(8,128)S(1)}, f32[16,8,128]{2,1,0:T(8,128)S(1)}, f32[16,8,128]{2,1,0:T(8,128)S(1)}, s32[]{:T(128)}) while((s32[]{:T(128)}, f32[16,8,128]{2,1,0:T(8,128)S(1)}, f32[16,8,128]{2,1,0:T(8,128)S(1)}, f32[16,8,128]{2,1,0:T(8,128)S(1)}, s32[]{:T(128)}) %tuple.206), condition=%wide.region_3.4_spmd, body=%wide.region_2.3_spmd.sunk | while | flops 32770 | bytes 524389 | solution.py:65
  88.7 4.3 %collective-permute-done.1 = f32[16,8,128]{2,1,0:T(8,128)S(1)} collective-permute-done((f32[16,8,128]{2,1,0:T(8,128)S(1)}, f32[16,8,128]{2,1,0:T(8,128)S(1)}, u32[]{:S(2)}, u32[]{:S(2)}) %collective-permute-start.1) | collective-permute-done | bytes 65568 | tf_op jit(solution)/shard_map/while/body/eval_jaxpr/ppermute | solution.py:10
  94.3 3.7 %collective-permute-done.1 = f32[16,8,128]{2,1,0:T(8,128)S(1)} collective-permute-done((f32[16,8,128]{2,1,0:T(8,128)S(1)}, f32[16,8,128]{2,1,0:T(8,128)S(1)}, u32[]{:S(2)}, u32[]{:S(2)}) %collective-permute-start.1) | collective-permute-done | bytes 65568 | tf_op jit(solution)/shard_map/while/body/eval_jaxpr/ppermute | solution.py:10
  99.3 3.7 %collective-permute-done.1 = f32[16,8,128]{2,1,0:T(8,128)S(1)} collective-permute-done((f32[16,8,128]{2,1,0:T(8,128)S(1)}, f32[16,8,128]{2,1,0:T(8,128)S(1)}, u32[]{:S(2)}, u32[]{:S(2)}) %collective-permute-start.1) | collective-permute-done | bytes 65568 | tf_op jit(solution)/shard_map/while/body/eval_jaxpr/ppermute | solution.py:10
  103.5 3.2 %collective-permute-start.14 = (f32[1,2,8,128]{3,2,1,0:T(8,128)S(1)}, f32[1,2,8,128]{3,2,1,0:T(8,128)S(1)}, u32[]{:S(2)}, u32[]{:S(2)}) collective-permute-start(f32[1,2,8,128]{3,2,1,0:T(8,128)S(1)} %get-tuple-element.237), channel_id=1, source_target_pairs={{0,4},{4,8},{8,12},{1,5},{5,9},{9,13},{2,6},{6,10},{10,14},{3,7},{... | collective-permute-start | bytes 24584 | tf_op jit(solution)/shard_map/ppermute | solution.py:18
  106.8 1.4 collective-permute-start.15
  109.1 2.2 %collective-permute-done.15 = f32[1,2,8,128]{3,2,1,0:T(8,128)S(1)} collective-permute-done((f32[1,2,8,128]{3,2,1,0:T(8,128)S(1)}, f32[1,2,8,128]{3,2,1,0:T(8,128)S(1)}, u32[]{:S(2)}, u32[]{:S(2)}) %collective-permute-start.15) | collective-permute-done | bytes 8224 | tf_op jit(solution)/shard_map/ppermute | solution.py:21
  122.6 6.3 %collective-permute-start.19 = (f32[1,8,12,2]{3,2,1,0:T(8,128)S(1)}, f32[1,8,12,2]{3,2,1,0:T(8,128)S(1)}, u32[]{:S(2)}, u32[]{:S(2)}) collective-permute-start(f32[1,8,12,2]{3,2,1,0:T(8,128)S(1)} %get-tuple-element.218), channel_id=1, source_target_pairs={{1,0},{3,2},{5,4},{7,6},{9,8},{11,10},{13,12},{15,14},{17,16},{19,... | collective-permute-start | bytes 2312 | tf_op jit(solution)/shard_map/ppermute | solution.py:21
  131.5 3.0 %fusion.39 = f32[16,6,10,130]{3,0,2,1:T(8,128)S(1)} fusion(f32[6,10,130]{2,1,0:T(8,128)S(1)} %broadcast_multiply_fusion, f32[16]{0:T(128)S(1)} %copy-done.22, f32[16]{0:T(128)S(1)} %get-tuple-element.93, f32[6,10,130]{2,1,0:T(8,128)S(1)} %get-tuple-element.183, f32[16]{0:T(128)S(1)} %get-tuple-element.94, f32[6,10,130]{2,1,0:T(8,128)S(1)} %get-tuple-element.174, ...), kind=kLoop, calls=%fused_computation.82 | loop fusion | flops 6988800 | bytes 1374592 | tf_op jit(solution)/shard_map/mul | solution.py:103
  (241 shorter events, 67.2 us)
Async XLA Ops:
  1.4 9.9 %collective-permute-start.2 = (f32[1,1,8,128]{3,2,1,0:T(8,128)S(1)}, f32[1,1,8,128]{3,2,1,0:T(8,128)S(1)}, u32[]{:S(2)}, u32[]{:S(2)}) collective-permute-start(f32[1,1,8,128]{3,2,1,0:T(8,128)S(1)} %get-tuple-element.241), channel_id=1, source_target_pairs={{0,4},{4,8},{8,12},{1,5},{5,9},{9,13},{2,6},{6,10},{10,14},{3,7},{... | collective-permute-start | bytes 12296 | tf_op jit(solution)/shard_map/ppermute | solution.py:18
  5.4 5.8 %collective-permute-start.3 = (f32[1,1,8,128]{3,2,1,0:T(8,128)S(1)}, f32[1,1,8,128]{3,2,1,0:T(8,128)S(1)}, u32[]{:S(2)}, u32[]{:S(2)}) collective-permute-start(f32[1,1,8,128]{3,2,1,0:T(8,128)S(1)} %get-tuple-element.242), channel_id=1, source_target_pairs={{4,0},{8,4},{12,8},{5,1},{9,5},{13,9},{6,2},{10,6},{14,10},{7,3},{... | collective-permute-start | bytes 12296 | tf_op jit(solution)/shard_map/ppermute | solution.py:21
  11.8 4.4 %collective-permute-start.4 = (f32[1,6,1,128]{3,2,1,0:T(1,128)S(1)}, f32[1,6,1,128]{3,2,1,0:T(1,128)S(1)}, u32[]{:S(2)}, u32[]{:S(2)}) collective-permute-start(f32[1,6,1,128]{3,2,1,0:T(1,128)S(1)} %get-tuple-element.235), channel_id=1, source_target_pairs={{0,2},{1,3},{4,6},{5,7},{8,10},{9,11},{12,14},{13,15},{16,18},{17,... | collective-permute-start | bytes 9224 | tf_op jit(solution)/shard_map/ppermute | solution.py:18
  15.0 4.3 %collective-permute-start.5 = (f32[1,6,1,128]{3,2,1,0:T(1,128)S(1)}, f32[1,6,1,128]{3,2,1,0:T(1,128)S(1)}, u32[]{:S(2)}, u32[]{:S(2)}) collective-permute-start(f32[1,6,1,128]{3,2,1,0:T(1,128)S(1)} %get-tuple-element.236), channel_id=1, source_target_pairs={{2,0},{3,1},{6,4},{7,5},{10,8},{11,9},{14,12},{15,13},{18,16},{19,... | collective-permute-start | bytes 9224 | tf_op jit(solution)/shard_map/ppermute | solution.py:21
  19.4 5.6 %collective-permute-start.6 = (f32[1,6,10,1]{3,2,1,0:T(8,128)S(1)}, f32[1,6,10,1]{3,2,1,0:T(8,128)S(1)}, u32[]{:S(2)}, u32[]{:S(2)}) collective-permute-start(f32[1,6,10,1]{3,2,1,0:T(8,128)S(1)} %get-tuple-element.227), channel_id=1, source_target_pairs={{0,1},{2,3},{4,5},{6,7},{8,9},{10,11},{12,13},{14,15},{16,17},{18,... | collective-permute-start | bytes 728 | tf_op jit(solution)/shard_map/ppermute | solution.py:18
  20.7 5.2 %collective-permute-start.7 = (f32[1,6,10,1]{3,2,1,0:T(8,128)S(1)}, f32[1,6,10,1]{3,2,1,0:T(8,128)S(1)}, u32[]{:S(2)}, u32[]{:S(2)}) collective-permute-start(f32[1,6,10,1]{3,2,1,0:T(8,128)S(1)} %get-tuple-element.228), channel_id=1, source_target_pairs={{1,0},{3,2},{5,4},{7,6},{9,8},{11,10},{13,12},{15,14},{17,16},{19,... | collective-permute-start | bytes 728 | tf_op jit(solution)/shard_map/ppermute | solution.py:21
  28.3 5.6 %collective-permute-start = (f32[16,8,128]{2,1,0:T(8,128)S(1)}, f32[16,8,128]{2,1,0:T(8,128)S(1)}, u32[]{:S(2)}, u32[]{:S(2)}) collective-permute-start(f32[16,8,128]{2,1,0:T(8,128)S(1)} %multiply_add_fusion.6), channel_id=1, source_target_pairs={{0,4},{4,8},{8,12},{1,5},{5,9},{9,13},{2,6},{6,10},{10,14},{3,7},{... | collective-permute-start | bytes 196616 | tf_op jit(solution)/shard_map/while/body/eval_jaxpr/ppermute | solution.py:10
  33.9 5.0 %collective-permute-start = (f32[16,8,128]{2,1,0:T(8,128)S(1)}, f32[16,8,128]{2,1,0:T(8,128)S(1)}, u32[]{:S(2)}, u32[]{:S(2)}) collective-permute-start(f32[16,8,128]{2,1,0:T(8,128)S(1)} %multiply_add_fusion.6), channel_id=1, source_target_pairs={{0,4},{4,8},{8,12},{1,5},{5,9},{9,13},{2,6},{6,10},{10,14},{3,7},{... | collective-permute-start | bytes 196616 | tf_op jit(solution)/shard_map/while/body/eval_jaxpr/ppermute | solution.py:10
  39.0 5.0 %collective-permute-start = (f32[16,8,128]{2,1,0:T(8,128)S(1)}, f32[16,8,128]{2,1,0:T(8,128)S(1)}, u32[]{:S(2)}, u32[]{:S(2)}) collective-permute-start(f32[16,8,128]{2,1,0:T(8,128)S(1)} %multiply_add_fusion.6), channel_id=1, source_target_pairs={{0,4},{4,8},{8,12},{1,5},{5,9},{9,13},{2,6},{6,10},{10,14},{3,7},{... | collective-permute-start | bytes 196616 | tf_op jit(solution)/shard_map/while/body/eval_jaxpr/ppermute | solution.py:10
  44.1 5.8 %collective-permute-start.8 = (f32[16,1,8,128]{3,0,2,1:T(8,128)S(1)}, f32[16,1,8,128]{3,0,2,1:T(8,128)S(1)}, u32[]{:S(2)}, u32[]{:S(2)}) collective-permute-start(f32[16,1,8,128]{3,0,2,1:T(8,128)S(1)} %get-tuple-element.129), channel_id=1, source_target_pairs={{0,4},{4,8},{8,12},{1,5},{5,9},{9,13},{2,6},{6,10},{10,14},{3,7},{... | collective-permute-start | bytes 196616 | tf_op jit(solution)/shard_map/ppermute | solution.py:18
  47.9 5.0 %collective-permute-start.9 = (f32[16,1,8,128]{3,0,2,1:T(8,128)S(1)}, f32[16,1,8,128]{3,0,2,1:T(8,128)S(1)}, u32[]{:S(2)}, u32[]{:S(2)}) collective-permute-start(f32[16,1,8,128]{3,0,2,1:T(8,128)S(1)} %get-tuple-element.130), channel_id=1, source_target_pairs={{4,0},{8,4},{12,8},{5,1},{9,5},{13,9},{6,2},{10,6},{14,10},{7,3},{... | collective-permute-start | bytes 196616 | tf_op jit(solution)/shard_map/ppermute | solution.py:21
  53.0 3.9 %collective-permute-start.10 = (f32[16,6,1,128]{3,0,2,1:T(8,128)S(1)}, f32[16,6,1,128]{3,0,2,1:T(8,128)S(1)}, u32[]{:S(2)}, u32[]{:S(2)}) collective-permute-start(f32[16,6,1,128]{3,0,2,1:T(8,128)S(1)} %get-tuple-element.119), channel_id=1, source_target_pairs={{0,2},{1,3},{4,6},{5,7},{8,10},{9,11},{12,14},{13,15},{16,18},{17,... | collective-permute-start | bytes 147464 | tf_op jit(solution)/shard_map/ppermute | solution.py:18
  54.3 4.8 %collective-permute-start.11 = (f32[16,6,1,128]{3,0,2,1:T(8,128)S(1)}, f32[16,6,1,128]{3,0,2,1:T(8,128)S(1)}, u32[]{:S(2)}, u32[]{:S(2)}) collective-permute-start(f32[16,6,1,128]{3,0,2,1:T(8,128)S(1)} %get-tuple-element.120), channel_id=1, source_target_pairs={{2,0},{3,1},{6,4},{7,5},{10,8},{11,9},{14,12},{15,13},{18,16},{19,... | collective-permute-start | bytes 147464 | tf_op jit(solution)/shard_map/ppermute | solution.py:21
  59.4 13.8 %collective-permute-start.12 = (f32[16,6,10,1]{3,0,2,1:T(8,128)S(1)}, f32[16,6,10,1]{3,0,2,1:T(8,128)S(1)}, u32[]{:S(2)}, u32[]{:S(2)}) collective-permute-start(f32[16,6,10,1]{3,0,2,1:T(8,128)S(1)} %get-tuple-element.117), channel_id=1, source_target_pairs={{0,1},{2,3},{4,5},{6,7},{8,9},{10,11},{12,13},{14,15},{16,17},{18,... | collective-permute-start | bytes 11528 | tf_op jit(solution)/shard_map/ppermute | solution.py:18
  60.7 12.6 %collective-permute-start.13 = (f32[16,6,10,1]{3,0,2,1:T(8,128)S(1)}, f32[16,6,10,1]{3,0,2,1:T(8,128)S(1)}, u32[]{:S(2)}, u32[]{:S(2)}) collective-permute-start(f32[16,6,10,1]{3,0,2,1:T(8,128)S(1)} %get-tuple-element.118), channel_id=1, source_target_pairs={{1,0},{3,2},{5,4},{7,6},{9,8},{11,10},{13,12},{15,14},{17,16},{19,... | collective-permute-start | bytes 11528 | tf_op jit(solution)/shard_map/ppermute | solution.py:21
  87.4 5.6 %collective-permute-start.1 = (f32[16,8,128]{2,1,0:T(8,128)S(1)}, f32[16,8,128]{2,1,0:T(8,128)S(1)}, u32[]{:S(2)}, u32[]{:S(2)}) collective-permute-start(f32[16,8,128]{2,1,0:T(8,128)S(1)} %multiply_add_fusion.7), channel_id=1, source_target_pairs={{4,0},{8,4},{12,8},{5,1},{9,5},{13,9},{6,2},{10,6},{14,10},{7,3},{... | collective-permute-start | bytes 196616 | tf_op jit(solution)/shard_map/while/body/eval_jaxpr/ppermute | solution.py:10
  93.0 5.0 %collective-permute-start.1 = (f32[16,8,128]{2,1,0:T(8,128)S(1)}, f32[16,8,128]{2,1,0:T(8,128)S(1)}, u32[]{:S(2)}, u32[]{:S(2)}) collective-permute-start(f32[16,8,128]{2,1,0:T(8,128)S(1)} %multiply_add_fusion.7), channel_id=1, source_target_pairs={{4,0},{8,4},{12,8},{5,1},{9,5},{13,9},{6,2},{10,6},{14,10},{7,3},{... | collective-permute-start | bytes 196616 | tf_op jit(solution)/shard_map/while/body/eval_jaxpr/ppermute | solution.py:10
  98.0 5.0 %collective-permute-start.1 = (f32[16,8,128]{2,1,0:T(8,128)S(1)}, f32[16,8,128]{2,1,0:T(8,128)S(1)}, u32[]{:S(2)}, u32[]{:S(2)}) collective-permute-start(f32[16,8,128]{2,1,0:T(8,128)S(1)} %multiply_add_fusion.7), channel_id=1, source_target_pairs={{4,0},{8,4},{12,8},{5,1},{9,5},{13,9},{6,2},{10,6},{14,10},{7,3},{... | collective-permute-start | bytes 196616 | tf_op jit(solution)/shard_map/while/body/eval_jaxpr/ppermute | solution.py:10
  103.5 5.6 %collective-permute-start.14 = (f32[1,2,8,128]{3,2,1,0:T(8,128)S(1)}, f32[1,2,8,128]{3,2,1,0:T(8,128)S(1)}, u32[]{:S(2)}, u32[]{:S(2)}) collective-permute-start(f32[1,2,8,128]{3,2,1,0:T(8,128)S(1)} %get-tuple-element.237), channel_id=1, source_target_pairs={{0,4},{4,8},{8,12},{1,5},{5,9},{9,13},{2,6},{6,10},{10,14},{3,7},{... | collective-permute-start | bytes 24584 | tf_op jit(solution)/shard_map/ppermute | solution.py:18
  106.8 4.5 %collective-permute-start.15 = (f32[1,2,8,128]{3,2,1,0:T(8,128)S(1)}, f32[1,2,8,128]{3,2,1,0:T(8,128)S(1)}, u32[]{:S(2)}, u32[]{:S(2)}) collective-permute-start(f32[1,2,8,128]{3,2,1,0:T(8,128)S(1)} %get-tuple-element.238), channel_id=1, source_target_pairs={{4,0},{8,4},{12,8},{5,1},{9,5},{13,9},{6,2},{10,6},{14,10},{7,3},{... | collective-permute-start | bytes 24584 | tf_op jit(solution)/shard_map/ppermute | solution.py:21
  111.3 9.9 %collective-permute-start.16 = (f32[1,8,2,128]{3,2,1,0:T(2,128)S(1)}, f32[1,8,2,128]{3,2,1,0:T(2,128)S(1)}, u32[]{:S(2)}, u32[]{:S(2)}) collective-permute-start(f32[1,8,2,128]{3,2,1,0:T(2,128)S(1)} %get-tuple-element.229), channel_id=1, source_target_pairs={{0,2},{1,3},{4,6},{5,7},{8,10},{9,11},{12,14},{13,15},{16,18},{17,... | collective-permute-start | bytes 24584 | tf_op jit(solution)/shard_map/ppermute | solution.py:18
  112.6 8.6 %collective-permute-start.17 = (f32[1,8,2,128]{3,2,1,0:T(2,128)S(1)}, f32[1,8,2,128]{3,2,1,0:T(2,128)S(1)}, u32[]{:S(2)}, u32[]{:S(2)}) collective-permute-start(f32[1,8,2,128]{3,2,1,0:T(2,128)S(1)} %get-tuple-element.230), channel_id=1, source_target_pairs={{2,0},{3,1},{6,4},{7,5},{10,8},{11,9},{14,12},{15,13},{18,16},{19,... | collective-permute-start | bytes 24584 | tf_op jit(solution)/shard_map/ppermute | solution.py:21
  121.3 8.8 %collective-permute-start.18 = (f32[1,8,12,2]{3,2,1,0:T(8,128)S(1)}, f32[1,8,12,2]{3,2,1,0:T(8,128)S(1)}, u32[]{:S(2)}, u32[]{:S(2)}) collective-permute-start(f32[1,8,12,2]{3,2,1,0:T(8,128)S(1)} %get-tuple-element.217), channel_id=1, source_target_pairs={{0,1},{2,3},{4,5},{6,7},{8,9},{10,11},{12,13},{14,15},{16,17},{18,... | collective-permute-start | bytes 2312 | tf_op jit(solution)/shard_map/ppermute | solution.py:18
  122.6 7.5 %collective-permute-start.19 = (f32[1,8,12,2]{3,2,1,0:T(8,128)S(1)}, f32[1,8,12,2]{3,2,1,0:T(8,128)S(1)}, u32[]{:S(2)}, u32[]{:S(2)}) collective-permute-start(f32[1,8,12,2]{3,2,1,0:T(8,128)S(1)} %get-tuple-element.218), channel_id=1, source_target_pairs={{1,0},{3,2},{5,4},{7,6},{9,8},{11,10},{13,12},{15,14},{17,16},{19,... | collective-permute-start | bytes 2312 | tf_op jit(solution)/shard_map/ppermute | solution.py:21
  (24 other events, 170.8 us)
where the time goes:
time: 148 us; the launch traced here: 147 us
  starting transfers between devices  63.5 us (43%)
  matrix products  29.2 us (20%)
  waiting for transfers between devices  27 us (18%)
  local copies, waits for them, and re-layouts  19 us (13%)
  other arithmetic  5.94 us (4%)
  between operations  1.99 us (1%)
    dot_general x54, matrix products, convolve(): jnp.einsum('oc,czyx->ozyx', weight[:, :, tap], piece, precision=lax.Preci...  28.9 us
    ppermute x9, starting transfers between devices, with_halo(): lax.ppermute(lax.slice_in_dim(block, 0, width, axis=dim), axis, backward)  27.3 us
    ppermute x9, starting transfers between devices, with_halo(): lax.ppermute(lax.slice_in_dim(block, block.shape[dim] - width, None, axis...  20.7 us
    ppermute x6, waiting for transfers between devices, shifted(): lax.ppermute(value, axis, [(source, source + steps) for source in range(f...  15.7 us
    ppermute x6, starting transfers between devices, shifted(): lax.ppermute(value, axis, [(source, source + steps) for source in range(f...  15.5 us
    ppermute x9, waiting for transfers between devices, with_halo(): lax.ppermute(lax.slice_in_dim(block, 0, width, axis=dim), axis, backward)  11.4 us
    unnamed x76, local copies, waits for them, and re-layouts  10.2 us
    slice x4, local copies, waits for them, and re-layouts, convolve(): weight[:, :, tap]  5.59 us
  transfers between devices with their start and end apart: 24, of which 11 were waited for; matrix products, arithmetic and copies ran while one was open for 11% of the time, Pallas kernels for 0%

commit v1 on v0

--- a/solution.py
+++ b/solution.py
@@ -1,6 +1,11 @@
+import functools
+
 import jax
 import jax.numpy as jnp
+import numpy as np
 from jax import lax
+from jax.experimental import pallas as pl
+from jax.experimental.pallas import tpu as pltpu
 from jax.sharding import PartitionSpec as P
 
 
@@ -106,7 +111,278 @@
     return (denoised, segmented)
 
 
+HALO = 4
+LANES = 128
+
+
+def split(value):
+    high = value.astype(jnp.bfloat16)
+    return high, (value - high.astype(jnp.float32)).astype(jnp.bfloat16)
+
+
+def halves(value):
+    high = lax.reduce_precision(value, 8, 7)
+    return high.astype(jnp.bfloat16), (value - high).astype(jnp.bfloat16)
+
+
+def swapped(value, axis):
+    return lax.ppermute(value, axis, [(0, 1), (1, 0)])
+
+
+def gathered(noisy):
+    count = lax.axis_size("gz")
+    place = lax.axis_index("gz")
+    slabs = [
+        lax.ppermute(noisy, "gz", [(i, (i + s) % count) for i in range(count)])
+        for s in range(count - 1, 0, -1)
+    ] + [noisy]
+    turns = jnp.concatenate(slabs + slabs[:-1], axis=0)
+    depth = noisy.shape[0]
+    block = lax.dynamic_slice_in_dim(turns, (count - 1 - place) * depth, count * depth, 0)
+    for axis, dim in (("gy", 1), ("gx", 2)):
+        first = lax.axis_index(axis) == 0
+        size = block.shape[dim]
+        low = lax.slice_in_dim(block, 0, HALO, axis=dim)
+        high = lax.slice_in_dim(block, size - HALO, size, axis=dim)
+        other = swapped(jnp.where(first, high, low), axis)
+        block = jnp.where(
+            first,
+            jnp.concatenate([block, other], dim),
+            jnp.concatenate([other, block], dim),
+        )
+    return block
+
+
+def kernel(
+    geometry,
+    place_ref,
+    noisy_ref,
+    mask_ref,
+    w1_ref,
+    bias1_ref,
+    w2_ref,
+    bias2_ref,
+    head_ref,
+    w3_ref,
+    bias3_ref,
+    w4_ref,
+    bias4_ref,
+    den_ref,
+    seg_ref,
+    stage,
+    thin,
+    pre,
+    rows,
+    wide_hi,
+    wide_lo,
+):
+    deep, depth, channels, pitch, span, margin = geometry
+    mask = mask_ref[...]
+    shifts = [(b - 1) * pitch + (c - 1) for b in range(3) for c in range(3)]
+    f32 = jnp.float32
+
+    def shifted(slot, shift):
+        return stage[slot, :, pl.ds(margin + shift, span)]
+
+    def thin_columns(field):
+        high, low = split(field)
+        stage[0, :, pl.ds(margin, span)] = high
+        stage[1, :, pl.ds(margin, span)] = low
+        for t, s in enumerate(shifts):
+            h = shifted(0, s)
+            thin[pl.ds(t * deep, deep), :] = h
+            thin[pl.ds((9 + t) * deep, deep), :] = h
+            thin[pl.ds((18 + t) * deep, deep), :] = shifted(1, s)
+
+    def wide_columns(z, field):
+        high, low = split(field)
+        stage[0, :, pl.ds(margin, span)] = high
+        stage[1, :, pl.ds(margin, span)] = low
+        for t, s in enumerate(shifts):
+            at = pl.ds(pl.multiple_of((z * 9 + t) * channels, channels), channels)
+            wide_hi[at, :] = shifted(0, s)
+            wide_lo[at, :] = shifted(1, s)
+
+    def banded(w_ref, start, taps):
+        at = pl.ds(pl.multiple_of(start, channels), taps)
+        rows_of = w_ref.shape[0] // 2
+        wh = w_ref[:rows_of]
+        wl = w_ref[rows_of:]
+        h = wide_hi[at, :]
+        out = jnp.dot(wh, h, preferred_element_type=f32)
+        out = out + jnp.dot(wh, wide_lo[at, :], preferred_element_type=f32)
+        return out + jnp.dot(wl, h, preferred_element_type=f32)
+
+    def gate(at, bias, hidden):
+        cand = jnp.tanh(pre[pl.ds(pl.multiple_of(at, channels), channels), :])
+        up = pre[pl.ds(pl.multiple_of(at + channels, channels), channels), :] + bias
+        fresh = 1.0 / (1.0 + jnp.exp(-up))
+        return hidden + fresh * (cand - hidden)
+
+    stage[...] = jnp.zeros_like(stage)
+    noisy = noisy_ref[...]
+    thin_columns(noisy)
+    pre[...] = jnp.dot(w1_ref[...], thin[...], preferred_element_type=f32)
+    edge = 9 * channels
+    zeros = jnp.zeros((edge, span), jnp.bfloat16)
+    for wide in (wide_hi, wide_lo):
+        wide[pl.ds(0, edge), :] = zeros
+        wide[pl.ds((deep + 1) * edge, edge), :] = zeros
+
+    def first(z, hidden):
+        hidden = gate(z * 2 * channels, bias1_ref[...], hidden)
+        wide_columns(z + 1, hidden * mask)
+        return hidden
+
+    blank = jnp.zeros((channels, span), f32)
+    lax.fori_loop(0, deep, first, blank)
+
+    taps = (depth + 2) * edge
+    block_rows = depth * 2 * channels
+
+    def second(turn, hidden):
+        b = deep // depth - 1 - turn
+        pre[pl.ds(0, block_rows), :] = banded(w2_ref, b * depth * edge, taps)
+        for zo in range(depth - 1, -1, -1):
+            hidden = gate(zo * 2 * channels, bias2_ref[...], hidden)
+            rows[pl.ds(b * depth + zo, 1), :] = jnp.sum(
+                hidden * head_ref[...], axis=0, keepdims=True
+            )
+        return hidden
+
+    lax.fori_loop(0, deep // depth, second, blank)
+
+    rows[...] = (noisy + rows[...]) * mask
+    mine = rows[pl.ds(0, depth), :]
+    for b in range(1, deep // depth):
+        mine = jnp.where(place_ref[0] == b, rows[pl.ds(b * depth, depth), :], mine)
+    den_ref[...] = mine
+    thin_columns(rows[...])
+    grown = jnp.dot(w3_ref[...], thin[...], preferred_element_type=f32)
+    grown = jnp.maximum(grown + bias3_ref[...], 0.0) * mask
+    for z in range(depth + 2):
+        wide_columns(z, grown[z * channels : (z + 1) * channels])
+    seg_ref[...] = banded(w4_ref, 0, taps) + bias4_ref[...]
+
+
+def thin_select(deep):
+    out = np.zeros((deep + 2, 27, 9, deep), np.float32)
+    for z in range(deep):
+        for a in range(3):
+            if 0 <= z + a - 1 < deep:
+                for t in range(9):
+                    out[z + 1, a * 9 + t, t, z + a - 1] = 1.0
+    return out.reshape(deep + 2, 27, 9 * deep)
+
+
+def band(weight, depth):
+    out, inn = weight.shape[0], weight.shape[1]
+    flat = jnp.transpose(weight, (0, 2, 1)).reshape(out, 27 * inn)
+    step = 9 * inn
+    return jnp.stack(
+        [jnp.pad(flat, ((0, 0), (step * z, step * (depth - 1 - z)))) for z in range(depth)]
+    )
+
+
+def twice(matrix):
+    return jnp.concatenate(halves(matrix), 0)
+
+
+def local_body(
+    noisy,
+    first_weight,
+    first_bias,
+    second_weight,
+    second_bias,
+    head_weight,
+    seg_weight_in,
+    seg_bias_in,
+    seg_weight_out,
+    seg_bias_out,
+):
+    depth, height, width = noisy.shape
+    count = lax.axis_size("gz")
+    place = lax.axis_index("gz")
+    deep = count * depth
+    channels = first_bias.shape[0]
+    high, pitch = height + HALO, width + HALO + 1
+    span = -(-high * pitch // LANES) * LANES
+    margin = -(-(pitch + 1) // LANES) * LANES
+
+    window = gathered(noisy)
+    flat = jnp.pad(window, ((0, 0), (0, 0), (0, 1))).reshape(deep, high * pitch)
+    flat = jnp.pad(flat, ((0, 0), (0, span - high * pitch)))
+    inside = np.zeros((high, pitch), np.float32)
+    inside[:, : pitch - 1] = 1.0
+    mask = jnp.asarray(np.pad(inside.reshape(1, -1), ((0, 0), (0, span - high * pitch))))
+
+    select = jnp.asarray(thin_select(deep))
+    exact = lax.Precision.HIGHEST
+
+    def thin_matrix(weight, picked):
+        full = jnp.einsum("ok,zkj->zoj", weight[:, 0], picked, precision=exact)
+        h, l = halves(full.reshape(-1, full.shape[-1]))
+        return jnp.concatenate([h, l, h], 1)
+
+    w1 = thin_matrix(first_weight, select[1:-1])
+    w3 = thin_matrix(
+        seg_weight_in, lax.dynamic_slice_in_dim(select, place * depth, depth + 2, 0)
+    )
+    w2 = twice(band(second_weight, depth).reshape(depth * 2 * channels, -1))
+    w4 = twice(
+        jnp.transpose(band(seg_weight_out, depth), (1, 0, 2)).reshape(depth * channels, -1)
+    )
+    layers = place * depth - 1 + jnp.arange(depth + 2)
+    real = ((layers >= 0) & (layers < deep)).astype(jnp.float32)
+    bias3 = (real[:, None] * seg_bias_in[None, :]).reshape(-1, 1)
+    bias4 = jnp.repeat(seg_bias_out, depth).reshape(-1, 1)
+
+    vmem = pl.BlockSpec(memory_space=pltpu.VMEM)
+    bf16 = jnp.bfloat16
+    den, seg = pl.pallas_call(
+        functools.partial(kernel, (deep, depth, channels, pitch, span, margin)),
+        out_shape=(
+            jax.ShapeDtypeStruct((depth, span), jnp.float32),
+            jax.ShapeDtypeStruct((depth * channels, span), jnp.float32),
+        ),
+        in_specs=[pl.BlockSpec(memory_space=pltpu.SMEM)] + [vmem] * 11,
+        out_specs=(vmem, vmem),
+        scratch_shapes=[
+            pltpu.VMEM((2, channels, span + 2 * margin), bf16),
+            pltpu.VMEM((27 * deep, span), bf16),
+            pltpu.VMEM((deep * 2 * channels, span), jnp.float32),
+            pltpu.VMEM((deep, span), jnp.float32),
+            pltpu.VMEM(((deep + 2) * 9 * channels, span), bf16),
+            pltpu.VMEM(((deep + 2) * 9 * channels, span), bf16),
+        ],
+        compiler_params=pltpu.CompilerParams(vmem_limit_bytes=56 * 1024 * 1024),
+    )(
+        place.reshape(1),
+        flat,
+        mask,
+        w1,
+        first_bias.reshape(-1, 1),
+        w2,
+        second_bias.reshape(-1, 1),
+        head_weight.reshape(-1, 1),
+        w3,
+        bias3,
+        w4,
+        bias4,
+    )
+    top = lax.axis_index("gy") * HALO
+    left = lax.axis_index("gx") * HALO
+
+    def own(field):
+        field = field[:, : high * pitch].reshape(-1, high, pitch)
+        return lax.dynamic_slice(field, (0, top, left), (field.shape[0], height, width))
+
+    return own(den), own(seg).reshape(channels, depth, height, width)
+
+
 def solution(mesh):
     in_specs = (P(("win", "gz"), "gy", "gx"), P(), P(), P(), P(), P(), P(), P(), P(), P())
     out_specs = (P(("win", "gz"), "gy", "gx"), P(None, ("win", "gz"), "gy", "gx"))
-    return jax.shard_map(body, mesh=mesh, in_specs=in_specs, out_specs=out_specs, check_vma=False)
+    shallow = mesh.shape["gz"] <= 4 and mesh.shape["gy"] == 2 and mesh.shape["gx"] == 2
+    chosen = local_body if shallow else body
+    return jax.shard_map(chosen, mesh=mesh, in_specs=in_specs, out_specs=out_specs, check_vma=False)

time: 148 us -> 52.5 us (0.35)
  starting transfers between devices: 63.5 us -> 8.66 us
  matrix products: 29.2 us -> 2.78 us
  waiting for transfers between devices: 27 us -> 1.56 us
  Pallas kernels: 0 us -> 19.4 us
  local copies, waits for them, and re-layouts: 19 us -> 14.8 us
  other arithmetic: 5.94 us -> 3.93 us
    ppermute x24 -> x5, starting transfers between devices: 63.5 us -> 8.66 us  [the longest x3 4.66 us: gathered(): lax.ppermute(noisy, 'gz', [(i, (i + s) % count) for i in range(count)])]
    dot_general x55 -> x2, matrix products: 29.2 us -> 2.78 us  [thin_matrix(): full = jnp.einsum('ok,zkj->zoj', weight[:, 0], picked, precision=exact)]
    ppermute x24 -> x5, waiting for transfers between devices: 27 us -> 1.56 us  [the longest x2 1.55 us: swapped(): return lax.ppermute(value, axis, [(0, 1), (1, 0)])]
    pallas_call x0 -> x1, Pallas kernels: none -> 19.4 us  [local_body(): pl.pallas_call(functools.partial(kernel, (deep, depth, channels, pitch, s...]
    slice x11 -> x0, local copies, waits for them, and re-layouts: 6.69 us -> none  [the longest x4 5.59 us: convolve(): weight[:, :, tap]]
    unnamed x76 -> x24, local copies, waits for them, and re-layouts: 10.2 us -> 4.4 us
    reshape x1 -> x9, local copies, waits for them, and re-layouts: 0.01 us -> 5.39 us  [the longest x2 2.88 us: own(): field = field[:, :high * pitch].reshape(-1, high, pitch)]
    mul x7 -> x1, other arithmetic: 3.5 us -> 0.07 us  [local_body(): bias3 = (real[:, None] * seg_bias_in[None, :]).reshape(-1, 1)]
  transfers between devices with their start and end apart: 24 -> 5, of which waited for: 11 -> 1; matrix products, arithmetic and copies ran while one was open for 11% -> 22% of each run, Pallas kernels for 0% -> 0%
where the time goes in v1:
time: 52.5 us; the launch traced here: 51.9 us
  Pallas kernels  19.4 us (37%)
  local copies, waits for them, and re-layouts  14.8 us (28%)
  starting transfers between devices  8.66 us (16%)
  other arithmetic  3.93 us (7%)
  matrix products  2.78 us (5%)
  waiting for transfers between devices  1.56 us (3%)
  between operations  0.87 us (2%)
    pallas_call x1, Pallas kernels, local_body(): pl.pallas_call(functools.partial(kernel, (deep, depth, channels, pitch, s...  19.4 us
    ppermute x3, starting transfers between devices, gathered(): lax.ppermute(noisy, 'gz', [(i, (i + s) % count) for i in range(count)])  4.66 us
    unnamed x24, local copies, waits for them, and re-layouts  4.4 us
    ppermute x2, starting transfers between devices, swapped(): return lax.ppermute(value, axis, [(0, 1), (1, 0)])  4.01 us
    reshape x2, local copies, waits for them, and re-layouts, own(): field = field[:, :high * pitch].reshape(-1, high, pitch)  2.88 us
    dot_general x2, matrix products, thin_matrix(): full = jnp.einsum('ok,zkj->zoj', weight[:, 0], picked, precision=exact)  2.78 us
    concatenate x2, other arithmetic, thin_matrix(): return jnp.concatenate([h, l, h], 1)  1.81 us
    ppermute x2, waiting for transfers between devices, swapped(): return lax.ppermute(value, axis, [(0, 1), (1, 0)])  1.55 us
  transfers between devices with their start and end apart: 5, of which 1 were waited for; matrix products, arithmetic and copies ran while one was open for 22% of the time, Pallas kernels for 0%

profile of v1, /device:TPU:1, one launch (start us, length us, event | category | flops | bytes accessed | tf_op | source)
XLA Modules:
  0.0 51.9 jit_solution(8119533635621600042)
XLA Ops:
  0.6 4.2 %collective-permute-start = (f32[4,8,128]{2,1,0:T(8,128)}, f32[4,8,128]{2,1,0:T(8,128)S(1)}, u32[]{:S(2)}, u32[]{:S(2)}) collective-permute-start(f32[4,8,128]{2,1,0:T(8,128)} %param.12), channel_id=1, source_target_pairs={{0,12},{4,0},{8,4},{12,8},{1,13},{5,1},{9,5},{13,9},{2,14},{6,2},{... | collective-permute-start | bytes 49160 | tf_op jit(solution)/shard_map/ppermute | solution.py:136
  5.3 0.8 %copy.40 = f32[32,1,27]{2,0,1:T(8,128)S(1)} copy(f32[32,1,27]{0,1,2:T(1,128)} %param.13) | data formatting | bytes 6912 | tf_op jit(solution)/shard_map/squeeze | solution.py:323
  6.1 1.6 %fusion.6 = f32[16,144,32]{1,2,0:T(8,128)S(1)} fusion(f32[16,27,144]{2,1,0:T(8,128)} %constant.60, f32[32,1,27]{2,0,1:T(8,128)S(1)} %copy.40), kind=kOutput, calls=%fused_computation.39 | convolution fusion | flops 23887872 | bytes 547200 | tf_op jit(solution)/shard_map/ok,zkj->zoj/dot_general | solution.py:323
  7.8 0.9 %copy-done.1 = f32[32,16,27]{0,1,2:T(8,128)S(1)} copy-done((f32[32,16,27]{0,1,2:T(8,128)S(1)}, f32[32,16,27]{0,1,2:T(8,128)}, u32[]{:S(2)}) %copy-start.1) | copy-done | bytes 55320
  9.0 1.2 %fusion.3 = f32[6,144,16]{1,2,0:T(8,128)S(1)} fusion(f32[16,27,1]{1,0,2:T(8,128)S(1)} %bitcast.50, f32[18,27,144]{2,1,0:T(8,128)} %constant.38.clone, s32[]{:T(128)S(6)} %select_n.55), kind=kOutput, calls=%fused_computation.15 | convolution fusion | flops 4478976 | bytes 253636 | tf_op jit(solution)/shard_map/ok,zkj->zoj/dot_general | solution.py:323
  10.2 0.9 %copy-done.2 = f32[16,16,27]{2,1,0:T(8,128)S(1)} copy-done((f32[16,16,27]{2,1,0:T(8,128)S(1)}, f32[16,16,27]{2,1,0:T(8,128)}, u32[]{:S(2)}) %copy-start.2) | copy-done | bytes 27672
  11.8 1.1 %pad_maximum_fusion.w1_ref = bf16[512,432]{1,0:T(8,128)(2,1)} fusion(bf16[512,144]{1,0:T(8,128)(2,1)S(1)} %get-tuple-element.7, bf16[512,144]{1,0:T(8,128)(2,1)S(1)} %get-tuple-element.6), kind=kLoop, calls=%fused_computation.5 | loop fusion | flops 1327104 | bytes 737280 | tf_op jit(solution)/shard_map/concatenate | solution.py:325
  12.8 0.8 %pad_maximum_fusion.2.w2_ref = bf16[256,864]{1,0:T(8,128)(2,1)} fusion(bf16[128,864]{1,0:T(8,128)(2,1)S(1)} %get-tuple-element.9, bf16[128,864]{1,0:T(8,128)(2,1)S(1)} %get-tuple-element.8), kind=kLoop, calls=%fused_computation.8 | loop fusion | flops 884736 | bytes 884736 | tf_op jit(solution)/shard_map/concatenate | solution.py:288
  13.7 0.7 %pad_maximum_fusion.3.w4_ref = bf16[128,864]{1,0:T(8,128)(2,1)} fusion(bf16[64,864]{1,0:T(8,128)(2,1)S(1)} %get-tuple-element.11, bf16[64,864]{1,0:T(8,128)(2,1)S(1)} %get-tuple-element.10), kind=kLoop, calls=%fused_computation.14 | loop fusion | flops 442368 | bytes 442368 | tf_op jit(solution)/shard_map/concatenate | solution.py:288
  14.5 0.7 %copy-done.3 = f32[4,8,128]{2,1,0:T(8,128)S(1)} copy-done((f32[4,8,128]{2,1,0:T(8,128)S(1)}, f32[4,8,128]{2,1,0:T(8,128)}, u32[]{:S(2)}) %copy-start.3) | copy-done | bytes 16408
  15.2 1.3 %collective-permute-start.3 = (f32[16,4,128]{2,1,0:T(4,128)S(1)}, f32[16,4,128]{2,1,0:T(4,128)S(1)}, u32[]{:S(2)}, u32[]{:S(2)}) collective-permute-start(f32[16,4,128]{2,1,0:T(4,128)S(1)} %dynamic-slice_select_fusion), channel_id=1, source_target_pairs={{0,2},{2,0},{1,3},{3,1},{4,6},{6,4},{5,7},{7,5},{8,10},{10,8},{9,1... | collective-permute-start | bytes 98312 | tf_op jit(solution)/shard_map/ppermute | solution.py:129
  16.5 1.5 %collective-permute-done.3 = f32[16,4,128]{2,1,0:T(4,128)S(1)} collective-permute-done((f32[16,4,128]{2,1,0:T(4,128)S(1)}, f32[16,4,128]{2,1,0:T(4,128)S(1)}, u32[]{:S(2)}, u32[]{:S(2)}) %collective-permute-start.3) | collective-permute-done | bytes 32800 | tf_op jit(solution)/shard_map/ppermute | solution.py:129
  18.2 2.7 %collective-permute-start.4 = (f32[16,12,4]{2,1,0:T(8,128)S(1)}, f32[16,12,4]{2,1,0:T(8,128)S(1)}, u32[]{:S(2)}, u32[]{:S(2)}) collective-permute-start(f32[16,12,4]{2,1,0:T(8,128)S(1)} %slice_select_fusion), channel_id=1, source_target_pairs={{0,1},{1,0},{2,3},{3,2},{4,5},{5,4},{6,7},{7,6},{8,9},{9,8},{10,11... | collective-permute-start | bytes 9224 | tf_op jit(solution)/shard_map/ppermute | solution.py:129
  20.9 0.7 %pad_maximum_fusion.4.w3_ref = bf16[96,432]{1,0:T(8,128)(2,1)} fusion(bf16[96,144]{1,0:T(8,128)(2,1)S(1)} %get-tuple-element.13, bf16[96,144]{1,0:T(8,128)(2,1)S(1)} %get-tuple-element.12), kind=kLoop, calls=%fused_computation.26 | loop fusion | flops 248832 | bytes 138240 | tf_op jit(solution)/shard_map/concatenate | solution.py:325
  22.3 0.7 %copy.34.bias1_ref = f32[16,1]{1,0:T(8,128)} copy(f32[16,1]{0,1:T(1,128)S(1)} %bitcast.56) | data formatting | bytes 128 | tf_op jit(solution)/shard_map/reshape | solution.py:364
  23.6 0.7 %copy.35.bias2_ref = f32[16,1]{1,0:T(8,128)} copy(f32[16,1]{0,1:T(1,128)S(1)} %bitcast.57) | data formatting | bytes 128 | tf_op jit(solution)/shard_map/reshape | solution.py:366
  25.0 0.7 %copy.36.head_ref = f32[16,1]{1,0:T(8,128)} copy(f32[16,1]{0,1:T(1,128)S(1)} %bitcast.58) | data formatting | bytes 128 | tf_op jit(solution)/shard_map/reshape | solution.py:367
  25.7 0.7 %mul.44.bias3_ref = f32[96,1]{1,0:T(8,128)} reshape(f32[6,16]{1,0:T(8,128)S(1)} %broadcast_multiply_fusion) | data formatting | bytes 768 | tf_op jit(solution)/shard_map/mul | solution.py:337
  26.4 0.7 %reshape_reshape.4.bias4_ref = f32[64,1]{1,0:T(8,128)} reshape(f32[16,4]{1,0:T(8,128)S(1)} %broadcast_in_dim.2) | data formatting | bytes 512 | tf_op jit(solution)/shard_map/reshape;reshape | solution.py:338
  28.1 19.4 %shard_map.131 = (f32[4,1664]{1,0:T(4,128)}, f32[64,1664]{1,0:T(8,128)}) custom-call(s32[1]{0:T(128)} %bitcast.place_ref, f32[16,1664]{1,0:T(8,128)} %pad.41.noisy_ref, f32[1,1664]{1,0:T(1,128)} %constant.37.clone.mask_ref, bf16[512,432]{1,0:T(8,128)(2,1)} %pad_maximum_fusion.w1_ref, f32[16,1]{1,0:T(8,128)} %copy.34.bias1_ref, ...), custom_call_target="tpu_custom_call" | custom-call | tf_op jit(solution)/shard_map/pallas_call | solution.py:342
  47.5 0.8 %reshape.89 = f32[4,12,133]{2,1,0:T(8,128)S(1)} reshape(f32[4,1596]{1,0:T(4,128)} %bitcast.55) | data formatting | bytes 51072 | tf_op jit(solution)/shard_map/reshape | solution.py:377
  48.3 2.0 %reshape.90 = f32[64,12,133]{2,1,0:T(8,128)S(1)} reshape(f32[64,1596]{1,0:T(8,128)} %bitcast.51) | data formatting | bytes 817152 | tf_op jit(solution)/shard_map/reshape | solution.py:377
  50.4 0.7 %constant_dynamic-slice_fusion.1 = f32[4,8,128]{2,1,0:T(8,128)} fusion(f32[4,12,133]{2,1,0:T(8,128)S(1)} %reshape.89, s32[]{:T(128)S(6)} %select_n.56, s32[]{:T(128)S(6)} %select_n.57), kind=kLoop, calls=%fused_computation.44 | loop fusion | bytes 32776 | tf_op jit(solution)/shard_map/dynamic_slice | solution.py:378
  51.1 0.8 %constant_dynamic-slice_fusion = f32[64,8,128]{2,1,0:T(8,128)} fusion(f32[64,12,133]{2,1,0:T(8,128)S(1)} %reshape.90, s32[]{:T(128)S(6)} %select_n.56, s32[]{:T(128)S(6)} %select_n.57), kind=kLoop, calls=%fused_computation.43 | loop fusion | bytes 524296 | tf_op jit(solution)/shard_map/dynamic_slice | solution.py:378
  (52 shorter events, 4.8 us)
Async XLA Ops:
  0.6 8.4 %copy-start = (f32[16,1,27]{2,1,0:T(1,128)S(1)}, f32[16,1,27]{2,1,0:T(1,128)}, u32[]{:S(2)}) copy-start(f32[16,1,27]{2,1,0:T(1,128)} %param.18) | copy-start | bytes 5188
  0.6 13.8 %collective-permute-start = (f32[4,8,128]{2,1,0:T(8,128)}, f32[4,8,128]{2,1,0:T(8,128)S(1)}, u32[]{:S(2)}, u32[]{:S(2)}) collective-permute-start(f32[4,8,128]{2,1,0:T(8,128)} %param.12), channel_id=1, source_target_pairs={{0,12},{4,0},{8,4},{12,8},{1,13},{5,1},{9,5},{13,9},{2,14},{6,2},{... | collective-permute-start | bytes 49160 | tf_op jit(solution)/shard_map/ppermute | solution.py:136
  4.8 9.6 %collective-permute-start.1 = (f32[4,8,128]{2,1,0:T(8,128)}, f32[4,8,128]{2,1,0:T(8,128)S(1)}, u32[]{:S(2)}, u32[]{:S(2)}) collective-permute-start(f32[4,8,128]{2,1,0:T(8,128)} %param.12), channel_id=1, source_target_pairs={{0,8},{4,12},{8,0},{12,4},{1,9},{5,13},{9,1},{13,5},{2,10},{6,14},... | collective-permute-start | bytes 49160 | tf_op jit(solution)/shard_map/ppermute | solution.py:136
  4.9 9.6 %collective-permute-start.2 = (f32[4,8,128]{2,1,0:T(8,128)}, f32[4,8,128]{2,1,0:T(8,128)S(1)}, u32[]{:S(2)}, u32[]{:S(2)}) collective-permute-start(f32[4,8,128]{2,1,0:T(8,128)} %param.12), channel_id=1, source_target_pairs={{0,4},{4,8},{8,12},{12,0},{1,5},{5,9},{9,13},{13,1},{2,6},{6,10},{... | collective-permute-start | bytes 49160 | tf_op jit(solution)/shard_map/ppermute | solution.py:136
  7.7 0.9 %copy-start.1 = (f32[32,16,27]{0,1,2:T(8,128)S(1)}, f32[32,16,27]{0,1,2:T(8,128)}, u32[]{:S(2)}) copy-start(f32[32,16,27]{0,1,2:T(8,128)} %param.15) | copy-start | bytes 165892
  10.2 0.9 %copy-start.2 = (f32[16,16,27]{2,1,0:T(8,128)S(1)}, f32[16,16,27]{2,1,0:T(8,128)}, u32[]{:S(2)}) copy-start(f32[16,16,27]{2,1,0:T(8,128)} %param.20) | copy-start | bytes 82948
  12.8 0.8 %copy-start.4 = (f32[16]{0:T(128)S(1)}, f32[16]{0:T(128)}, u32[]{:S(2)}) copy-start(f32[16]{0:T(128)} %param.19) | copy-start | bytes 196
  14.5 0.7 %copy-start.3 = (f32[4,8,128]{2,1,0:T(8,128)S(1)}, f32[4,8,128]{2,1,0:T(8,128)}, u32[]{:S(2)}) copy-start(f32[4,8,128]{2,1,0:T(8,128)} %param.12) | copy-start | bytes 49156
  15.2 2.8 %collective-permute-start.3 = (f32[16,4,128]{2,1,0:T(4,128)S(1)}, f32[16,4,128]{2,1,0:T(4,128)S(1)}, u32[]{:S(2)}, u32[]{:S(2)}) collective-permute-start(f32[16,4,128]{2,1,0:T(4,128)S(1)} %dynamic-slice_select_fusion), channel_id=1, source_target_pairs={{0,2},{2,0},{1,3},{3,1},{4,6},{6,4},{5,7},{7,5},{8,10},{10,8},{9,1... | collective-permute-start | bytes 98312 | tf_op jit(solution)/shard_map/ppermute | solution.py:129
  18.2 8.9 %collective-permute-start.4 = (f32[16,12,4]{2,1,0:T(8,128)S(1)}, f32[16,12,4]{2,1,0:T(8,128)S(1)}, u32[]{:S(2)}, u32[]{:S(2)}) collective-permute-start(f32[16,12,4]{2,1,0:T(8,128)S(1)} %slice_select_fusion), channel_id=1, source_target_pairs={{0,1},{1,0},{2,3},{3,2},{4,5},{5,4},{6,7},{7,6},{8,9},{9,8},{10,11... | collective-permute-start | bytes 9224 | tf_op jit(solution)/shard_map/ppermute | solution.py:129
  21.7 0.7 %copy-start.5 = (f32[16]{0:T(128)S(1)}, f32[16]{0:T(128)}, u32[]{:S(2)}) copy-start(f32[16]{0:T(128)} %param.14) | copy-start | bytes 196
  23.0 0.7 %copy-start.6 = (f32[16]{0:T(128)S(1)}, f32[16]{0:T(128)}, u32[]{:S(2)}) copy-start(f32[16]{0:T(128)} %param.16) | copy-start | bytes 196
  24.3 0.7 %copy-start.7 = (f32[16]{0:T(128)S(1)}, f32[16]{0:T(128)}, u32[]{:S(2)}) copy-start(f32[16]{0:T(128)} %param.17) | copy-start | bytes 196
  25.7 0.7 %copy-start.8 = (f32[16]{0:T(128)S(1)}, f32[16]{0:T(128)}, u32[]{:S(2)}) copy-start(f32[16]{0:T(128)} %param.21) | copy-start | bytes 196

commit v2 on v1

--- a/solution.py
+++ b/solution.py
@@ -120,11 +120,6 @@
     return high, (value - high.astype(jnp.float32)).astype(jnp.bfloat16)
 
 
-def halves(value):
-    high = lax.reduce_precision(value, 8, 7)
-    return high.astype(jnp.bfloat16), (value - high).astype(jnp.bfloat16)
-
-
 def swapped(value, axis):
     return lax.ppermute(value, axis, [(0, 1), (1, 0)])
 
@@ -153,20 +148,91 @@
     return block
 
 
+def prepare(
+    geometry,
+    w1_ref,
+    b1_ref,
+    w2_ref,
+    b2_ref,
+    head_ref,
+    w3_ref,
+    b3_ref,
+    w4_ref,
+    b4_ref,
+    thin_lane_ref,
+    thin_sub_ref,
+    spread_ref,
+    keep_ref,
+    gather_ref,
+    w1_out,
+    w2_out,
+    w3_out,
+    w4_out,
+    columns_out,
+    band,
+):
+    deep, depth, channels = geometry
+    f32, bf16 = jnp.float32, jnp.bfloat16
+    place = lax.axis_index("gz") * depth
+
+    def dot(left, right):
+        return jnp.dot(left, right, preferred_element_type=f32)
+
+    tap_lane, z_lane, part_lane = (thin_lane_ref[i : i + 1, :] for i in range(3))
+    tap_sub, a_sub = (thin_sub_ref[:, i : i + 1] for i in range(2))
+    same = tap_lane == tap_sub
+    crossed = part_lane == 1
+    reach = z_lane - a_sub + 1
+
+    def thin_rows(halves, z):
+        hit = same & (reach == z)
+        high = jnp.where(hit & ~crossed, 1.0, 0.0).astype(bf16)
+        low = jnp.where(hit & crossed, 1.0, 0.0).astype(bf16)
+        return (dot(halves[0], high) + dot(halves[1], low)).astype(bf16)
+
+    first = split(w1_ref[:, 0, :])
+    out = 2 * channels
+    for z in range(deep):
+        w1_out[z * out : (z + 1) * out, :] = thin_rows(first, z)
+    grow = split(w3_ref[:, 0, :])
+    for i in range(depth + 2):
+        z = place + i - 1
+        inside = (z >= 0) & (z < deep)
+        w3_out[i * channels : (i + 1) * channels, :] = thin_rows(
+            grow, jnp.where(inside, z, -deep)
+        )
+
+    spread = spread_ref[...]
+    step = 9 * channels
+    for w_ref, w_out in ((w2_ref, w2_out), (w4_ref, w4_out)):
+        out = w_ref.shape[0] // channels
+        keep = jnp.concatenate([keep_ref[...]] * out, 0)
+        gather = gather_ref[:out, : out * channels]
+        for part, half in enumerate(split(w_ref[...])):
+            flat = dot(gather, (dot(half, spread) * keep).astype(bf16))
+            band[...] = jnp.zeros_like(band)
+            for z in range(depth):
+                band[z * out : (z + 1) * out, pl.ds(z * step, 3 * step)] = flat
+            rows = depth * out
+            w_out[part * rows : (part + 1) * rows, :] = band[:rows, :].astype(bf16)
+
+    at_row = lax.broadcasted_iota(jnp.int32, (channels, channels), 0)
+    at_lane = lax.broadcasted_iota(jnp.int32, (channels, channels), 1)
+    for i, ref in enumerate((b1_ref, b2_ref, head_ref, b3_ref, b4_ref)):
+        columns_out[:, i : i + 1] = jnp.sum(
+            jnp.where(at_row == at_lane, ref[...], 0.0), axis=1, keepdims=True
+        )
+
+
 def kernel(
     geometry,
-    place_ref,
     noisy_ref,
     mask_ref,
     w1_ref,
-    bias1_ref,
     w2_ref,
-    bias2_ref,
-    head_ref,
     w3_ref,
-    bias3_ref,
     w4_ref,
-    bias4_ref,
+    columns_ref,
     den_ref,
     seg_ref,
     stage,
@@ -178,6 +244,8 @@
 ):
     deep, depth, channels, pitch, span, margin = geometry
     mask = mask_ref[...]
+    place = lax.axis_index("gz")
+    bias1, bias2, head, bias3, bias4 = (columns_ref[:, i : i + 1] for i in range(5))
     shifts = [(b - 1) * pitch + (c - 1) for b in range(3) for c in range(3)]
     f32 = jnp.float32
 
@@ -230,7 +298,7 @@
         wide[pl.ds((deep + 1) * edge, edge), :] = zeros
 
     def first(z, hidden):
-        hidden = gate(z * 2 * channels, bias1_ref[...], hidden)
+        hidden = gate(z * 2 * channels, bias1, hidden)
         wide_columns(z + 1, hidden * mask)
         return hidden
 
@@ -244,48 +312,41 @@
         b = deep // depth - 1 - turn
         pre[pl.ds(0, block_rows), :] = banded(w2_ref, b * depth * edge, taps)
         for zo in range(depth - 1, -1, -1):
-            hidden = gate(zo * 2 * channels, bias2_ref[...], hidden)
+            hidden = gate(zo * 2 * channels, bias2, hidden)
             rows[pl.ds(b * depth + zo, 1), :] = jnp.sum(
-                hidden * head_ref[...], axis=0, keepdims=True
+                hidden * head, axis=0, keepdims=True
             )
         return hidden
 
     lax.fori_loop(0, deep // depth, second, blank)
 
     rows[...] = (noisy + rows[...]) * mask
-    mine = rows[pl.ds(0, depth), :]
-    for b in range(1, deep // depth):
-        mine = jnp.where(place_ref[0] == b, rows[pl.ds(b * depth, depth), :], mine)
-    den_ref[...] = mine
-    thin_columns(rows[...])
+    finished = rows[...]
+    thin_columns(finished)
     grown = jnp.dot(w3_ref[...], thin[...], preferred_element_type=f32)
-    grown = jnp.maximum(grown + bias3_ref[...], 0.0) * mask
-    for z in range(depth + 2):
-        wide_columns(z, grown[z * channels : (z + 1) * channels])
-    seg_ref[...] = banded(w4_ref, 0, taps) + bias4_ref[...]
-
-
-def thin_select(deep):
-    out = np.zeros((deep + 2, 27, 9, deep), np.float32)
-    for z in range(deep):
-        for a in range(3):
-            if 0 <= z + a - 1 < deep:
-                for t in range(9):
-                    out[z + 1, a * 9 + t, t, z + a - 1] = 1.0
-    return out.reshape(deep + 2, 27, 9 * deep)
-
-
-def band(weight, depth):
-    out, inn = weight.shape[0], weight.shape[1]
-    flat = jnp.transpose(weight, (0, 2, 1)).reshape(out, 27 * inn)
-    step = 9 * inn
-    return jnp.stack(
-        [jnp.pad(flat, ((0, 0), (step * z, step * (depth - 1 - z)))) for z in range(depth)]
-    )
-
-
-def twice(matrix):
-    return jnp.concatenate(halves(matrix), 0)
+    for i in range(depth + 2):
+        z = place * depth + i - 1
+        real = jnp.where((z >= 0) & (z < deep), 1.0, 0.0)
+        layer = grown[i * channels : (i + 1) * channels]
+        wide_columns(i, jnp.maximum(layer + bias3, 0.0) * (mask * real))
+    pre[pl.ds(0, depth * channels), :] = banded(w4_ref, 0, taps)
+
+    height, width = den_ref.shape[1:]
+    for y in range(2):
+        for x in range(2):
+
+            @pl.when((lax.axis_index("gy") == y) & (lax.axis_index("gx") == x))
+            def _():
+                for r in range(height):
+                    lanes = pl.ds((y * HALO + r) * pitch + x * HALO, width)
+                    mine = rows[pl.ds(0, depth), lanes]
+                    for b in range(1, deep // depth):
+                        mine = jnp.where(place == b, rows[pl.ds(b * depth, depth), lanes], mine)
+                    den_ref[:, r, :] = mine
+                    for z in range(depth):
+                        seg_ref[:, z, r, :] = (
+                            pre[pl.ds(z * channels, channels), lanes] + bias4
+                        )
 
 
 def local_body(
@@ -316,68 +377,71 @@
     inside[:, : pitch - 1] = 1.0
     mask = jnp.asarray(np.pad(inside.reshape(1, -1), ((0, 0), (0, span - high * pitch))))
 
-    select = jnp.asarray(thin_select(deep))
-    exact = lax.Precision.HIGHEST
-
-    def thin_matrix(weight, picked):
-        full = jnp.einsum("ok,zkj->zoj", weight[:, 0], picked, precision=exact)
-        h, l = halves(full.reshape(-1, full.shape[-1]))
-        return jnp.concatenate([h, l, h], 1)
-
-    w1 = thin_matrix(first_weight, select[1:-1])
-    w3 = thin_matrix(
-        seg_weight_in, lax.dynamic_slice_in_dim(select, place * depth, depth + 2, 0)
+    f32, bf16, int32 = jnp.float32, jnp.bfloat16, jnp.int32
+    lane = np.arange(27 * deep)
+    thin_lane = np.stack(
+        [lane // deep % 9, lane % deep, lane // (9 * deep)] + [lane * 0] * 5
+    ).astype(np.int32)
+    thin_sub = np.stack([np.arange(27) % 9, np.arange(27) // 9], 1).astype(np.int32)
+    lane = np.arange(27 * channels)
+    spread = (np.arange(27)[:, None] == lane[None] // channels).astype(bf16)
+    keep = (np.arange(channels)[:, None] == lane[None] % channels).astype(np.float32)
+    lane = np.arange(2 * channels * channels)
+    gather = (np.arange(2 * channels)[:, None] == lane[None] // channels).astype(bf16)
+
+    taps = (depth + 2) * 9 * channels
+    in_vmem = pl.BlockSpec(memory_space=pltpu.VMEM)
+    w1, w2, w3, w4, columns = pl.pallas_call(
+        functools.partial(prepare, (deep, depth, channels)),
+        out_shape=(
+            pltpu.VMEM((deep * 2 * channels, 27 * deep), bf16),
+            pltpu.VMEM((2 * depth * 2 * channels, taps), bf16),
+            pltpu.VMEM(((depth + 2) * channels, 27 * deep), bf16),
+            pltpu.VMEM((2 * depth * channels, taps), bf16),
+            pltpu.VMEM((channels, LANES), f32),
+        ),
+        in_specs=[in_vmem] * 14,
+        out_specs=(in_vmem,) * 5,
+        scratch_shapes=[pltpu.VMEM((depth * 2 * channels, taps), f32)],
+        compiler_params=pltpu.CompilerParams(vmem_limit_bytes=16 * 1024 * 1024),
+    )(
+        first_weight,
+        first_bias.reshape(1, -1),
+        second_weight.reshape(-1, 27),
+        second_bias.reshape(1, -1),
+        head_weight.reshape(1, -1),
+        seg_weight_in,
+        seg_bias_in.reshape(1, -1),
+        seg_weight_out.reshape(-1, 27),
+        seg_bias_out.reshape(1, -1),
+        jnp.asarray(thin_lane),
+        jnp.asarray(thin_sub),
+        jnp.asarray(spread),
+        jnp.asarray(keep),
+        jnp.asarray(gather),
     )
-    w2 = twice(band(second_weight, depth).reshape(depth * 2 * channels, -1))
-    w4 = twice(
-        jnp.transpose(band(seg_weight_out, depth), (1, 0, 2)).reshape(depth * channels, -1)
-    )
-    layers = place * depth - 1 + jnp.arange(depth + 2)
-    real = ((layers >= 0) & (layers < deep)).astype(jnp.float32)
-    bias3 = (real[:, None] * seg_bias_in[None, :]).reshape(-1, 1)
-    bias4 = jnp.repeat(seg_bias_out, depth).reshape(-1, 1)
-
-    vmem = pl.BlockSpec(memory_space=pltpu.VMEM)
-    bf16 = jnp.bfloat16
-    den, seg = pl.pallas_call(
+    operands = [
+        pltpu.with_memory_space_constraint(v, pltpu.VMEM)
+        for v in (flat, mask, w1, w2, w3, w4, columns)
+    ]
+    return pl.pallas_call(
         functools.partial(kernel, (deep, depth, channels, pitch, span, margin)),
         out_shape=(
-            jax.ShapeDtypeStruct((depth, span), jnp.float32),
-            jax.ShapeDtypeStruct((depth * channels, span), jnp.float32),
+            jax.ShapeDtypeStruct((depth, height, width), f32),
+            jax.ShapeDtypeStruct((channels, depth, height, width), f32),
         ),
-        in_specs=[pl.BlockSpec(memory_space=pltpu.SMEM)] + [vmem] * 11,
-        out_specs=(vmem, vmem),
+        in_specs=[in_vmem] * 7,
+        out_specs=(in_vmem,) * 2,
         scratch_shapes=[
             pltpu.VMEM((2, channels, span + 2 * margin), bf16),
             pltpu.VMEM((27 * deep, span), bf16),
-            pltpu.VMEM((deep * 2 * channels, span), jnp.float32),
-            pltpu.VMEM((deep, span), jnp.float32),
+            pltpu.VMEM((deep * 2 * channels, span), f32),
+            pltpu.VMEM((deep, span), f32),
             pltpu.VMEM(((deep + 2) * 9 * channels, span), bf16),
             pltpu.VMEM(((deep + 2) * 9 * channels, span), bf16),
         ],
-        compiler_params=pltpu.CompilerParams(vmem_limit_bytes=56 * 1024 * 1024),
-    )(
-        place.reshape(1),
-        flat,
-        mask,
-        w1,
-        first_bias.reshape(-1, 1),
-        w2,
-        second_bias.reshape(-1, 1),
-        head_weight.reshape(-1, 1),
-        w3,
-        bias3,
-        w4,
-        bias4,
-    )
-    top = lax.axis_index("gy") * HALO
-    left = lax.axis_index("gx") * HALO
-
-    def own(field):
-        field = field[:, : high * pitch].reshape(-1, high, pitch)
-        return lax.dynamic_slice(field, (0, top, left), (field.shape[0], height, width))
-
-    return own(den), own(seg).reshape(channels, depth, height, width)
+        compiler_params=pltpu.CompilerParams(vmem_limit_bytes=36 * 1024 * 1024),
+    )(*operands)
 
 
 def solution(mesh):

time: 52.5 us -> 39.6 us (0.75)
  local copies, waits for them, and re-layouts: 14.8 us -> 1.9 us
  waiting for transfers between devices: 1.56 us -> 5.69 us
  other arithmetic: 3.93 us -> 0.28 us
  matrix products: 2.78 us -> 0 us
  Pallas kernels: 19.4 us -> 20.9 us
  starting transfers between devices: 8.66 us -> 9.25 us
    reshape x8 -> x0, local copies, waits for them, and re-layouts: 5.24 us -> none  [the longest x2 2.88 us: own(): field = field[:, :high * pitch].reshape(-1, high, pitch)]
    ppermute x3, waiting for transfers between devices: 0.01 us -> 4.14 us  [gathered(): lax.ppermute(noisy, 'gz', [(i, (i + s) % count) for i in range(count)])]
    concatenate x4 -> x0, other arithmetic: 3.34 us -> none  [the longest x2 1.81 us: thin_matrix(): return jnp.concatenate([h, l, h], 1)]
    dot_general x2 -> x0, matrix products: 2.78 us -> none  [thin_matrix(): full = jnp.einsum('ok,zkj->zoj', weight[:, 0], picked, precision=exact)]
    unnamed x24 -> x40, local copies, waits for them, and re-layouts: 4.4 us -> 1.71 us
    pallas_call x0 -> x1, Pallas kernels: none -> 1.69 us  [local_body(): pl.pallas_call(functools.partial(prepare, (deep, depth, channels)), out_s...]
    dynamic_slice x2 -> x0, local copies, waits for them, and re-layouts: 1.54 us -> none  [own(): lax.dynamic_slice(field, (0, top, left), (field.shape[0], height, width))]
    another operation x3 -> x0, local copies, waits for them, and re-layouts: 0.92 us -> none  [the longest x1 0.69 us: local_body(): bias4 = jnp.repeat(seg_bias_out, depth).reshape(-1, 1)]
  transfers between devices with their start and end apart: 5 -> 5, of which waited for: 1 -> 4; matrix products, arithmetic and copies ran while one was open for 22% -> 1% of each run, Pallas kernels for 0% -> 4%
where the time goes in v2:
time: 39.6 us; the launch traced here: 38.8 us
  Pallas kernels  20.9 us (53%)
  starting transfers between devices  9.25 us (23%)
  waiting for transfers between devices  5.69 us (14%)
  local copies, waits for them, and re-layouts  1.9 us (5%)
  between operations  0.86 us (2%)
    pallas_call x1, Pallas kernels, local_body(): pl.pallas_call(functools.partial(kernel, (deep, depth, channels, pitch, s...  19.2 us
    ppermute x3, starting transfers between devices, gathered(): lax.ppermute(noisy, 'gz', [(i, (i + s) % count) for i in range(count)])  4.66 us
    ppermute x2, starting transfers between devices, swapped(): return lax.ppermute(value, axis, [(0, 1), (1, 0)])  4.6 us
    ppermute x3, waiting for transfers between devices, gathered(): lax.ppermute(noisy, 'gz', [(i, (i + s) % count) for i in range(count)])  4.14 us
    unnamed x40, local copies, waits for them, and re-layouts  1.71 us
    pallas_call x1, Pallas kernels, local_body(): pl.pallas_call(functools.partial(prepare, (deep, depth, channels)), out_s...  1.69 us
    ppermute x2, waiting for transfers between devices, swapped(): return lax.ppermute(value, axis, [(0, 1), (1, 0)])  1.55 us
  transfers between devices with their start and end apart: 5, of which 4 were waited for; matrix products, arithmetic and copies ran while one was open for 1% of the time, Pallas kernels for 4%

profile of v2, /device:TPU:1, one launch (start us, length us, event | category | flops | bytes accessed | tf_op | source)
XLA Modules:
  0.0 38.8 jit_solution(14775632763769337353)
XLA Ops:
  0.6 4.2 %collective-permute-start = (f32[4,8,128]{2,1,0:T(8,128)}, f32[4,8,128]{2,1,0:T(8,128)S(1)}, u32[]{:S(2)}, u32[]{:S(2)}) collective-permute-start(f32[4,8,128]{2,1,0:T(8,128)} %param.16), channel_id=1, source_target_pairs={{0,12},{4,0},{8,4},{12,8},{1,13},{5,1},{9,5},{13,9},{2,14},{6,2},{... | collective-permute-start | bytes 49160 | tf_op jit(solution)/shard_map/ppermute | solution.py:131
  4.8 0.5 %collective-permute-start.2 = (f32[4,8,128]{2,1,0:T(8,128)}, f32[4,8,128]{2,1,0:T(8,128)S(1)}, u32[]{:S(2)}, u32[]{:S(2)}) collective-permute-start(f32[4,8,128]{2,1,0:T(8,128)} %param.16), channel_id=1, source_target_pairs={{0,4},{4,8},{8,12},{12,0},{1,5},{5,9},{9,13},{13,1},{2,6},{6,10},{... | collective-permute-start | bytes 49160 | tf_op jit(solution)/shard_map/ppermute | solution.py:131
  5.3 0.6 %collective-permute-done = f32[4,8,128]{2,1,0:T(8,128)S(1)} collective-permute-done((f32[4,8,128]{2,1,0:T(8,128)}, f32[4,8,128]{2,1,0:T(8,128)S(1)}, u32[]{:S(2)}, u32[]{:S(2)}) %collective-permute-start) | collective-permute-done | bytes 16416 | tf_op jit(solution)/shard_map/ppermute | solution.py:131
  5.9 2.6 %collective-permute-done.1 = f32[4,8,128]{2,1,0:T(8,128)S(1)} collective-permute-done((f32[4,8,128]{2,1,0:T(8,128)}, f32[4,8,128]{2,1,0:T(8,128)S(1)}, u32[]{:S(2)}, u32[]{:S(2)}) %collective-permute-start.1) | collective-permute-done | bytes 16416 | tf_op jit(solution)/shard_map/ppermute | solution.py:131
  8.5 0.9 %collective-permute-done.2 = f32[4,8,128]{2,1,0:T(8,128)S(1)} collective-permute-done((f32[4,8,128]{2,1,0:T(8,128)}, f32[4,8,128]{2,1,0:T(8,128)S(1)}, u32[]{:S(2)}, u32[]{:S(2)}) %collective-permute-start.2) | collective-permute-done | bytes 16416 | tf_op jit(solution)/shard_map/ppermute | solution.py:131
  9.5 1.3 %collective-permute-start.3 = (f32[16,4,128]{2,1,0:T(4,128)S(1)}, f32[16,4,128]{2,1,0:T(4,128)S(1)}, u32[]{:S(2)}, u32[]{:S(2)}) collective-permute-start(f32[16,4,128]{2,1,0:T(4,128)S(1)} %dynamic-slice_select_fusion), channel_id=1, source_target_pairs={{0,2},{2,0},{1,3},{3,1},{4,6},{6,4},{5,7},{7,5},{8,10},{10,8},{9,1... | collective-permute-start | bytes 98312 | tf_op jit(solution)/shard_map/ppermute | solution.py:124
  10.8 1.5 %collective-permute-done.3 = f32[16,4,128]{2,1,0:T(4,128)S(1)} collective-permute-done((f32[16,4,128]{2,1,0:T(4,128)S(1)}, f32[16,4,128]{2,1,0:T(4,128)S(1)}, u32[]{:S(2)}, u32[]{:S(2)}) %collective-permute-start.3) | collective-permute-done | bytes 32800 | tf_op jit(solution)/shard_map/ppermute | solution.py:124
  12.4 0.0 copy-start.13
  12.4 0.1 slice_select_fusion
  12.5 3.3 %collective-permute-start.4 = (f32[16,12,4]{2,1,0:T(8,128)S(1)}, f32[16,12,4]{2,1,0:T(8,128)S(1)}, u32[]{:S(2)}, u32[]{:S(2)}) collective-permute-start(f32[16,12,4]{2,1,0:T(8,128)S(1)} %slice_select_fusion), channel_id=1, source_target_pairs={{0,1},{1,0},{2,3},{3,2},{4,5},{5,4},{6,7},{7,6},{8,9},{9,8},{10,11... | collective-permute-start | bytes 9224 | tf_op jit(solution)/shard_map/ppermute | solution.py:124
  15.8 0.1 copy.21.w1_ref
  15.9 0.0 copy-start.2
  15.9 0.0 copy-start.3
  15.9 0.0 copy-start.4
  15.9 0.0 copy-start.5
  16.0 0.2 copy.20
  16.2 0.6 %copy-done = f32[16,16,27]{2,1,0:T(8,128)S(1)} copy-done((f32[16,16,27]{2,1,0:T(8,128)S(1)}, f32[16,16,27]{2,1,0:T(8,128)}, u32[]{:S(2)}) %copy-start) | copy-done | bytes 27672
  16.9 0.1 copy-done.6
  16.9 1.7 %shard_map.167 = (bf16[512,432]{1,0:T(8,128)(2,1)S(1)}, bf16[256,864]{1,0:T(8,128)(2,1)S(1)}, bf16[96,432]{1,0:T(8,128)(2,1)S(1)}, bf16[128,864]{1,0:T(8,128)(2,1)S(1)}, f32[16,128]{1,0:T(8,128)S(1)}) custom-call(f32[32,1,27]{2,1,0:T(1,128)S(1)} %copy.21.w1_ref, f32[1,16]{1,0:T(1,128)S(1)} %bitcast.9, f32[512,27]{1,0:T(8,128)S(1)} %bitcast.7, ...), custom_call_target="tpu_custom_call" | custom-call | tf_op jit(solution)/shard_map/pallas_call | solution.py:394
  18.6 0.1 maximum_select_fusion
  18.8 0.1 reshape.28
  19.0 0.0 copy-start.7
  19.0 0.7 %copy-done.7 = f32[1,1664]{1,0:T(1,128)S(1)} copy-done((f32[1,1664]{1,0:T(1,128)S(1)}, f32[1,1664]{1,0:T(1,128)}, u32[]{:S(2)}) %copy-start.7) | copy-done | bytes 6680
  19.7 19.2 %shard_map.168 = (f32[4,8,128]{2,1,0:T(8,128)}, f32[16,4,8,128]{3,2,1,0:T(8,128)}) custom-call(f32[16,1664]{1,0:T(8,128)S(1)} %pad.9.noisy_ref, f32[1,1664]{1,0:T(1,128)S(1)} %copy-done.7, bf16[512,432]{1,0:T(8,128)(2,1)S(1)} %get-tuple-element.7.w1_ref, bf16[256,864]{1,0:T(8,128)(2,1)S(1)} %get-tuple-element.8.w2_ref, ...), custom_call_target="tpu_custom_call" | custom-call | tf_op jit(solution)/shard_map/pallas_call | solution.py:427
  (37 shorter events, 0.2 us)
Async XLA Ops:
  0.6 5.3 %collective-permute-start = (f32[4,8,128]{2,1,0:T(8,128)}, f32[4,8,128]{2,1,0:T(8,128)S(1)}, u32[]{:S(2)}, u32[]{:S(2)}) collective-permute-start(f32[4,8,128]{2,1,0:T(8,128)} %param.16), channel_id=1, source_target_pairs={{0,12},{4,0},{8,4},{12,8},{1,13},{5,1},{9,5},{13,9},{2,14},{6,2},{... | collective-permute-start | bytes 49160 | tf_op jit(solution)/shard_map/ppermute | solution.py:131
  4.8 3.7 %collective-permute-start.1 = (f32[4,8,128]{2,1,0:T(8,128)}, f32[4,8,128]{2,1,0:T(8,128)S(1)}, u32[]{:S(2)}, u32[]{:S(2)}) collective-permute-start(f32[4,8,128]{2,1,0:T(8,128)} %param.16), channel_id=1, source_target_pairs={{0,8},{4,12},{8,0},{12,4},{1,9},{5,13},{9,1},{13,5},{2,10},{6,14},... | collective-permute-start | bytes 49160 | tf_op jit(solution)/shard_map/ppermute | solution.py:131
  4.8 4.6 %collective-permute-start.2 = (f32[4,8,128]{2,1,0:T(8,128)}, f32[4,8,128]{2,1,0:T(8,128)S(1)}, u32[]{:S(2)}, u32[]{:S(2)}) collective-permute-start(f32[4,8,128]{2,1,0:T(8,128)} %param.16), channel_id=1, source_target_pairs={{0,4},{4,8},{8,12},{12,0},{1,5},{5,9},{9,13},{13,1},{2,6},{6,10},{... | collective-permute-start | bytes 49160 | tf_op jit(solution)/shard_map/ppermute | solution.py:131
  8.5 0.9 %copy-start.14 = (f32[4,8,128]{2,1,0:T(8,128)S(1)}, f32[4,8,128]{2,1,0:T(8,128)}, u32[]{:S(2)}) copy-start(f32[4,8,128]{2,1,0:T(8,128)} %param.16) | copy-start | bytes 49156
  9.5 2.8 %collective-permute-start.3 = (f32[16,4,128]{2,1,0:T(4,128)S(1)}, f32[16,4,128]{2,1,0:T(4,128)S(1)}, u32[]{:S(2)}, u32[]{:S(2)}) collective-permute-start(f32[16,4,128]{2,1,0:T(4,128)S(1)} %dynamic-slice_select_fusion), channel_id=1, source_target_pairs={{0,2},{2,0},{1,3},{3,1},{4,6},{6,4},{5,7},{7,5},{8,10},{10,8},{9,1... | collective-permute-start | bytes 98312 | tf_op jit(solution)/shard_map/ppermute | solution.py:124
  12.4 3.5 %copy-start.15 = (f32[32,1,27]{0,1,2:T(1,128)S(1)}, f32[32,1,27]{0,1,2:T(1,128)}, u32[]{:S(2)}) copy-start(f32[32,1,27]{0,1,2:T(1,128)} %param.17) | copy-start | bytes 10372
  12.4 3.5 %copy-start.13 = (f32[32,16,27]{0,1,2:T(8,128)S(1)}, f32[32,16,27]{0,1,2:T(8,128)}, u32[]{:S(2)}) copy-start(f32[32,16,27]{0,1,2:T(8,128)} %param.19) | copy-start | bytes 165892
  12.5 6.1 %collective-permute-start.4 = (f32[16,12,4]{2,1,0:T(8,128)S(1)}, f32[16,12,4]{2,1,0:T(8,128)S(1)}, u32[]{:S(2)}, u32[]{:S(2)}) collective-permute-start(f32[16,12,4]{2,1,0:T(8,128)S(1)} %slice_select_fusion), channel_id=1, source_target_pairs={{0,1},{1,0},{2,3},{3,2},{4,5},{5,4},{6,7},{7,6},{8,9},{9,8},{10,11... | collective-permute-start | bytes 9224 | tf_op jit(solution)/shard_map/ppermute | solution.py:124
  15.9 0.9 %copy-start = (f32[16,16,27]{2,1,0:T(8,128)S(1)}, f32[16,16,27]{2,1,0:T(8,128)}, u32[]{:S(2)}) copy-start(f32[16,16,27]{2,1,0:T(8,128)} %param.24) | copy-start | bytes 82948
  15.9 0.9 %copy-start.1 = (bf16[32,512]{1,0:T(8,128)(2,1)S(1)}, bf16[32,512]{1,0:T(8,128)(2,1)}, u32[]{:S(2)}) copy-start(bf16[32,512]{1,0:T(8,128)(2,1)} %constant.38.clone.gather_ref) | copy-start | bytes 98308
  15.9 0.9 %copy-start.2 = (f32[16,432]{1,0:T(8,128)S(1)}, f32[16,432]{1,0:T(8,128)}, u32[]{:S(2)}) copy-start(f32[16,432]{1,0:T(8,128)} %constant.37.clone.keep_ref) | copy-start | bytes 82948
  15.9 0.9 %copy-start.3 = (bf16[27,432]{1,0:T(8,128)(2,1)S(1)}, bf16[27,432]{1,0:T(8,128)(2,1)}, u32[]{:S(2)}) copy-start(bf16[27,432]{1,0:T(8,128)(2,1)} %constant.36.clone.spread_ref) | copy-start | bytes 69988
  15.9 0.9 %copy-start.4 = (s32[27,2]{1,0:T(8,128)S(1)}, s32[27,2]{1,0:T(8,128)}, u32[]{:S(2)}) copy-start(s32[27,2]{1,0:T(8,128)} %constant.35.clone.thin_sub_ref) | copy-start | bytes 652
  15.9 0.9 %copy-start.5 = (s32[8,432]{1,0:T(8,128)S(1)}, s32[8,432]{1,0:T(8,128)}, u32[]{:S(2)}) copy-start(s32[8,432]{1,0:T(8,128)} %constant.34.clone.thin_lane_ref) | copy-start | bytes 41476
  16.0 0.9 %copy-start.11 = (f32[16]{0:T(128)S(1)}, f32[16]{0:T(128)}, u32[]{:S(2)}) copy-start(f32[16]{0:T(128)} %param.23) | copy-start | bytes 196
  16.0 0.9 %copy-start.12 = (f32[16]{0:T(128)S(1)}, f32[16]{0:T(128)}, u32[]{:S(2)}) copy-start(f32[16]{0:T(128)} %param.25) | copy-start | bytes 196
  16.2 0.7 %copy-start.6 = (f32[16,1,27]{2,1,0:T(1,128)S(1)}, f32[16,1,27]{2,1,0:T(1,128)}, u32[]{:S(2)}) copy-start(f32[16,1,27]{2,1,0:T(1,128)} %w3_ref.1) | copy-start | bytes 5188
  16.2 0.7 %copy-start.8 = (f32[16]{0:T(128)S(1)}, f32[16]{0:T(128)}, u32[]{:S(2)}) copy-start(f32[16]{0:T(128)} %param.18) | copy-start | bytes 196
  16.2 0.7 %copy-start.9 = (f32[16]{0:T(128)S(1)}, f32[16]{0:T(128)}, u32[]{:S(2)}) copy-start(f32[16]{0:T(128)} %param.20) | copy-start | bytes 196
  16.2 0.7 %copy-start.10 = (f32[16]{0:T(128)S(1)}, f32[16]{0:T(128)}, u32[]{:S(2)}) copy-start(f32[16]{0:T(128)} %param.21) | copy-start | bytes 196
  19.0 0.7 %copy-start.7 = (f32[1,1664]{1,0:T(1,128)S(1)}, f32[1,1664]{1,0:T(1,128)}, u32[]{:S(2)}) copy-start(f32[1,1664]{1,0:T(1,128)} %constant.33.clone.mask_ref) | copy-start | bytes 19972

commit v3 on v2

--- a/solution.py
+++ b/solution.py
@@ -134,18 +134,17 @@
     turns = jnp.concatenate(slabs + slabs[:-1], axis=0)
     depth = noisy.shape[0]
     block = lax.dynamic_slice_in_dim(turns, (count - 1 - place) * depth, count * depth, 0)
-    for axis, dim in (("gy", 1), ("gx", 2)):
-        first = lax.axis_index(axis) == 0
-        size = block.shape[dim]
-        low = lax.slice_in_dim(block, 0, HALO, axis=dim)
-        high = lax.slice_in_dim(block, size - HALO, size, axis=dim)
-        other = swapped(jnp.where(first, high, low), axis)
-        block = jnp.where(
-            first,
-            jnp.concatenate([block, other], dim),
-            jnp.concatenate([other, block], dim),
-        )
-    return block
+    block = jnp.where(lax.axis_index("gy") == 0, block, jnp.flip(block, 1))
+    near = lax.slice_in_dim(block, block.shape[1] - HALO, None, axis=1)
+    block = jnp.concatenate([block, swapped(jnp.flip(near, 1), "gy")], 1)
+    first = lax.axis_index("gx") == 0
+    size = block.shape[2]
+    low = lax.slice_in_dim(block, 0, HALO, axis=2)
+    high = lax.slice_in_dim(block, size - HALO, size, axis=2)
+    other = swapped(jnp.where(first, high, low), "gx")
+    return jnp.where(
+        first, jnp.concatenate([block, other], 2), jnp.concatenate([other, block], 2)
+    )
 
 
 def prepare(
@@ -161,7 +160,7 @@
     b4_ref,
     thin_lane_ref,
     thin_sub_ref,
-    spread_ref,
+    wide_lane_ref,
     keep_ref,
     gather_ref,
     w1_out,
@@ -174,13 +173,14 @@
     deep, depth, channels = geometry
     f32, bf16 = jnp.float32, jnp.bfloat16
     place = lax.axis_index("gz") * depth
+    turned = lax.axis_index("gy") == 1
 
     def dot(left, right):
         return jnp.dot(left, right, preferred_element_type=f32)
 
     tap_lane, z_lane, part_lane = (thin_lane_ref[i : i + 1, :] for i in range(3))
-    tap_sub, a_sub = (thin_sub_ref[:, i : i + 1] for i in range(2))
-    same = tap_lane == tap_sub
+    a_sub, tap_ahead, tap_turned = (thin_sub_ref[:, i : i + 1] for i in range(3))
+    same = tap_lane == jnp.where(turned, tap_turned, tap_ahead)
     crossed = part_lane == 1
     reach = z_lane - a_sub + 1
 
@@ -202,19 +202,28 @@
             grow, jnp.where(inside, z, -deep)
         )
 
-    spread = spread_ref[...]
-    step = 9 * channels
+    taps = lax.broadcasted_iota(jnp.int32, (27, wide_lane_ref.shape[1]), 0)
+    spread = taps == jnp.where(turned, wide_lane_ref[1:2, :], wide_lane_ref[0:1, :])
+    spread = jnp.where(spread, 1.0, 0.0).astype(bf16)
+    step = 3 * channels
+    part = (depth + 2) * step
+    band[...] = jnp.zeros_like(band)
     for w_ref, w_out in ((w2_ref, w2_out), (w4_ref, w4_out)):
         out = w_ref.shape[0] // channels
         keep = jnp.concatenate([keep_ref[...]] * out, 0)
         gather = gather_ref[:out, : out * channels]
-        for part, half in enumerate(split(w_ref[...])):
-            flat = dot(gather, (dot(half, spread) * keep).astype(bf16))
-            band[...] = jnp.zeros_like(band)
-            for z in range(depth):
-                band[z * out : (z + 1) * out, pl.ds(z * step, 3 * step)] = flat
-            rows = depth * out
-            w_out[part * rows : (part + 1) * rows, :] = band[:rows, :].astype(bf16)
+        flats = [
+            dot(gather, (dot(half, spread) * keep).astype(bf16)) for half in split(w_ref[...])
+        ]
+        for b in range(3):
+            for i, half in enumerate((0, 0, 1)):
+                piece = flats[half][:, b * 3 * step : (b + 1) * 3 * step]
+                for z in range(depth):
+                    row = (b * depth + z) * out
+                    band[row : row + out, pl.ds(i * part + z * step, 3 * step)] = piece
+        w_out[...] = band[: w_out.shape[0], :].astype(bf16)
+        if w_ref is w2_ref:
+            band[: w4_out.shape[0], :] = jnp.zeros((w4_out.shape[0], 3 * part), f32)
 
     at_row = lax.broadcasted_iota(jnp.int32, (channels, channels), 0)
     at_lane = lax.broadcasted_iota(jnp.int32, (channels, channels), 1)
@@ -241,95 +250,123 @@
     rows,
     wide_hi,
     wide_lo,
+    sums,
 ):
-    deep, depth, channels, pitch, span, margin = geometry
+    deep, depth, channels, pitch, high, span, margin = geometry
+    f32 = jnp.float32
     mask = mask_ref[...]
     place = lax.axis_index("gz")
     bias1, bias2, head, bias3, bias4 = (columns_ref[:, i : i + 1] for i in range(5))
     shifts = [(b - 1) * pitch + (c - 1) for b in range(3) for c in range(3)]
-    f32 = jnp.float32
-
-    def shifted(slot, shift):
-        return stage[slot, :, pl.ds(margin + shift, span)]
-
-    def thin_columns(field):
-        high, low = split(field)
-        stage[0, :, pl.ds(margin, span)] = high
-        stage[1, :, pl.ds(margin, span)] = low
+    first_span, second_span, third_span = (
+        -(-(high - i) * pitch // LANES) * LANES for i in range(1, 4)
+    )
+    blocks = deep // depth
+
+    def put(field):
+        for slot, half in enumerate(split(field)):
+            stage[slot, :, pl.ds(margin, field.shape[1])] = half
+
+    def shifted(slot, shift, length):
+        return stage[slot, :, pl.ds(margin + shift, length)]
+
+    def thin_columns(field, length):
+        put(field)
         for t, s in enumerate(shifts):
-            h = shifted(0, s)
-            thin[pl.ds(t * deep, deep), :] = h
-            thin[pl.ds((9 + t) * deep, deep), :] = h
-            thin[pl.ds((18 + t) * deep, deep), :] = shifted(1, s)
+            h = shifted(0, s, length)
+            thin[t * deep : (t + 1) * deep, :length] = h
+            thin[(9 + t) * deep : (10 + t) * deep, :length] = h
+            thin[(18 + t) * deep : (19 + t) * deep, :length] = shifted(1, s, length)
 
     def wide_columns(z, field):
-        high, low = split(field)
-        stage[0, :, pl.ds(margin, span)] = high
-        stage[1, :, pl.ds(margin, span)] = low
-        for t, s in enumerate(shifts):
-            at = pl.ds(pl.multiple_of((z * 9 + t) * channels, channels), channels)
-            wide_hi[at, :] = shifted(0, s)
-            wide_lo[at, :] = shifted(1, s)
-
-    def banded(w_ref, start, taps):
-        at = pl.ds(pl.multiple_of(start, channels), taps)
-        rows_of = w_ref.shape[0] // 2
-        wh = w_ref[:rows_of]
-        wl = w_ref[rows_of:]
-        h = wide_hi[at, :]
-        out = jnp.dot(wh, h, preferred_element_type=f32)
-        out = out + jnp.dot(wh, wide_lo[at, :], preferred_element_type=f32)
-        return out + jnp.dot(wl, h, preferred_element_type=f32)
-
-    def gate(at, bias, hidden):
-        cand = jnp.tanh(pre[pl.ds(pl.multiple_of(at, channels), channels), :])
-        up = pre[pl.ds(pl.multiple_of(at + channels, channels), channels), :] + bias
+        length = field.shape[1]
+        put(field)
+        for c in range(3):
+            at = (z * 3 + c) * channels
+            wide_hi[at : at + channels, :length] = shifted(0, c - 1, length)
+            wide_lo[at : at + channels, :length] = shifted(1, c - 1, length)
+
+    taps = (depth + 2) * 3 * channels
+
+    def chunks(length):
+        return [(i, min(2 * LANES, length - i)) for i in range(0, length, 2 * LANES)]
+
+    def banded(w_ref, slot, start, chunk):
+        at, length = chunk
+        h = wide_hi[start : start + taps, at : at + length]
+        l = wide_lo[start : start + taps, at : at + length]
+        sums[slot, : w_ref.shape[0], pl.ds(margin + at, length)] = jnp.dot(
+            w_ref[...], jnp.concatenate([h, l, h], 0), preferred_element_type=f32
+        )
+
+    def gate(cand, up, hidden):
         fresh = 1.0 / (1.0 + jnp.exp(-up))
-        return hidden + fresh * (cand - hidden)
+        return hidden + fresh * (jnp.tanh(cand) - hidden)
 
     stage[...] = jnp.zeros_like(stage)
+    aside = jnp.zeros(sums.shape[:2] + (margin,), f32)
+    sums[:, :, :margin] = aside
+    sums[:, :, sums.shape[2] - margin :] = aside
+    edge = 3 * channels
+    zeros = jnp.zeros((edge, wide_hi.shape[1]), jnp.bfloat16)
+    for wide in (wide_hi, wide_lo):
+        wide[:edge, :] = zeros
+        wide[(deep + 1) * edge :, :] = zeros
+
     noisy = noisy_ref[...]
-    thin_columns(noisy)
-    pre[...] = jnp.dot(w1_ref[...], thin[...], preferred_element_type=f32)
-    edge = 9 * channels
-    zeros = jnp.zeros((edge, span), jnp.bfloat16)
-    for wide in (wide_hi, wide_lo):
-        wide[pl.ds(0, edge), :] = zeros
-        wide[pl.ds((deep + 1) * edge, edge), :] = zeros
-
-    def first(z, hidden):
-        hidden = gate(z * 2 * channels, bias1, hidden)
-        wide_columns(z + 1, hidden * mask)
-        return hidden
-
-    blank = jnp.zeros((channels, span), f32)
-    lax.fori_loop(0, deep, first, blank)
-
-    taps = (depth + 2) * edge
-    block_rows = depth * 2 * channels
-
-    def second(turn, hidden):
-        b = deep // depth - 1 - turn
-        pre[pl.ds(0, block_rows), :] = banded(w2_ref, b * depth * edge, taps)
+    thin_columns(noisy, first_span)
+    pre[...] = jnp.dot(w1_ref[...], thin[:, :first_span], preferred_element_type=f32)
+
+    hidden = jnp.zeros((channels, first_span), f32)
+    for z in range(deep):
+        at = z * 2 * channels
+        hidden = gate(
+            pre[at : at + channels, :],
+            pre[at + channels : at + 2 * channels, :] + bias1,
+            hidden,
+        )
+        wide_columns(z + 1, hidden * mask[:, :first_span])
+
+    def layer(slot, at, length, lift=0):
+        return sum(
+            sums[
+                slot,
+                at + b * depth * lift : at + b * depth * lift + channels,
+                pl.ds(margin + (b - 1) * pitch, length),
+            ]
+            for b in range(3)
+        )
+
+    hidden = jnp.zeros((channels, second_span), f32)
+    todo = chunks(first_span)
+    for chunk in todo:
+        banded(w2_ref, (blocks - 1) % 2, (blocks - 1) * depth * edge, chunk)
+    for b in range(blocks - 1, -1, -1):
         for zo in range(depth - 1, -1, -1):
-            hidden = gate(zo * 2 * channels, bias2, hidden)
-            rows[pl.ds(b * depth + zo, 1), :] = jnp.sum(
-                hidden * head, axis=0, keepdims=True
+            if b > 0:
+                turn = depth - 1 - zo
+                for chunk in todo[turn::depth]:
+                    banded(w2_ref, (b - 1) % 2, (b - 1) * depth * edge, chunk)
+            at = zo * 2 * channels
+            hidden = gate(
+                layer(b % 2, at, second_span, 2 * channels),
+                layer(b % 2, at + channels, second_span, 2 * channels) + bias2,
+                hidden,
             )
-        return hidden
-
-    lax.fori_loop(0, deep // depth, second, blank)
-
-    rows[...] = (noisy + rows[...]) * mask
-    finished = rows[...]
-    thin_columns(finished)
-    grown = jnp.dot(w3_ref[...], thin[...], preferred_element_type=f32)
+            z = b * depth + zo
+            rows[z : z + 1, :second_span] = jnp.sum(hidden * head, axis=0, keepdims=True)
+
+    finished = (noisy[:, :second_span] + rows[:, :second_span]) * mask[:, :second_span]
+    rows[:, :second_span] = finished
+    thin_columns(finished, third_span)
+    grown = jnp.dot(w3_ref[...], thin[:, :third_span], preferred_element_type=f32)
     for i in range(depth + 2):
         z = place * depth + i - 1
         real = jnp.where((z >= 0) & (z < deep), 1.0, 0.0)
-        layer = grown[i * channels : (i + 1) * channels]
-        wide_columns(i, jnp.maximum(layer + bias3, 0.0) * (mask * real))
-    pre[pl.ds(0, depth * channels), :] = banded(w4_ref, 0, taps)
+        features = jnp.maximum(grown[i * channels : (i + 1) * channels] + bias3, 0.0)
+        wide_columns(i, features * (mask[:, :third_span] * real))
+    for chunk in chunks(third_span):
+        banded(w4_ref, 0, 0, chunk)
 
     height, width = den_ref.shape[1:]
     for y in range(2):
@@ -338,15 +375,20 @@
             @pl.when((lax.axis_index("gy") == y) & (lax.axis_index("gx") == x))
             def _():
                 for r in range(height):
-                    lanes = pl.ds((y * HALO + r) * pitch + x * HALO, width)
-                    mine = rows[pl.ds(0, depth), lanes]
-                    for b in range(1, deep // depth):
-                        mine = jnp.where(place == b, rows[pl.ds(b * depth, depth), lanes], mine)
-                    den_ref[:, r, :] = mine
+                    row = height - 1 - r if y else r
+                    at = r * pitch + x * HALO
+                    mine = rows[:depth, pl.ds(at, width)]
+                    for b in range(1, blocks):
+                        other = rows[b * depth : (b + 1) * depth, pl.ds(at, width)]
+                        mine = jnp.where(place == b, other, mine)
+                    den_ref[:, row, :] = mine
                     for z in range(depth):
-                        seg_ref[:, z, r, :] = (
-                            pre[pl.ds(z * channels, channels), lanes] + bias4
-                        )
+                        total = bias4
+                        for b in range(3):
+                            k = (b * depth + z) * channels
+                            lanes = pl.ds(margin + at + (b - 1) * pitch, width)
+                            total = total + sums[0, k : k + channels, lanes]
+                        seg_ref[:, z, row, :] = total
 
 
 def local_body(
@@ -369,6 +411,7 @@
     high, pitch = height + HALO, width + HALO + 1
     span = -(-high * pitch // LANES) * LANES
     margin = -(-(pitch + 1) // LANES) * LANES
+    narrow = -(-(high - 1) * pitch // LANES) * LANES
 
     window = gathered(noisy)
     flat = jnp.pad(window, ((0, 0), (0, 0), (0, 1))).reshape(deep, high * pitch)
@@ -382,27 +425,33 @@
     thin_lane = np.stack(
         [lane // deep % 9, lane % deep, lane // (9 * deep)] + [lane * 0] * 5
     ).astype(np.int32)
-    thin_sub = np.stack([np.arange(27) % 9, np.arange(27) // 9], 1).astype(np.int32)
+    tap = np.arange(27)
+    thin_sub = np.stack(
+        [tap // 9, tap % 9, (2 - tap // 3 % 3) * 3 + tap % 3], 1
+    ).astype(np.int32)
     lane = np.arange(27 * channels)
-    spread = (np.arange(27)[:, None] == lane[None] // channels).astype(bf16)
+    b, a, c = lane // channels // 9, lane // channels // 3 % 3, lane // channels % 3
+    wide_lane = np.stack(
+        [a * 9 + b * 3 + c, a * 9 + (2 - b) * 3 + c] + [lane * 0] * 6
+    ).astype(np.int32)
     keep = (np.arange(channels)[:, None] == lane[None] % channels).astype(np.float32)
     lane = np.arange(2 * channels * channels)
     gather = (np.arange(2 * channels)[:, None] == lane[None] // channels).astype(bf16)
 
-    taps = (depth + 2) * 9 * channels
+    taps = 3 * (depth + 2) * 3 * channels
     in_vmem = pl.BlockSpec(memory_space=pltpu.VMEM)
     w1, w2, w3, w4, columns = pl.pallas_call(
         functools.partial(prepare, (deep, depth, channels)),
         out_shape=(
             pltpu.VMEM((deep * 2 * channels, 27 * deep), bf16),
-            pltpu.VMEM((2 * depth * 2 * channels, taps), bf16),
+            pltpu.VMEM((3 * depth * 2 * channels, taps), bf16),
             pltpu.VMEM(((depth + 2) * channels, 27 * deep), bf16),
-            pltpu.VMEM((2 * depth * channels, taps), bf16),
+            pltpu.VMEM((3 * depth * channels, taps), bf16),
             pltpu.VMEM((channels, LANES), f32),
         ),
         in_specs=[in_vmem] * 14,
         out_specs=(in_vmem,) * 5,
-        scratch_shapes=[pltpu.VMEM((depth * 2 * channels, taps), f32)],
+        scratch_shapes=[pltpu.VMEM((3 * depth * 2 * channels, taps), f32)],
         compiler_params=pltpu.CompilerParams(vmem_limit_bytes=16 * 1024 * 1024),
     )(
         first_weight,
@@ -416,7 +465,7 @@
         seg_bias_out.reshape(1, -1),
         jnp.asarray(thin_lane),
         jnp.asarray(thin_sub),
-        jnp.asarray(spread),
+        jnp.asarray(wide_lane),
         jnp.asarray(keep),
         jnp.asarray(gather),
     )
@@ -425,7 +474,7 @@
         for v in (flat, mask, w1, w2, w3, w4, columns)
     ]
     return pl.pallas_call(
-        functools.partial(kernel, (deep, depth, channels, pitch, span, margin)),
+        functools.partial(kernel, (deep, depth, channels, pitch, high, span, margin)),
         out_shape=(
             jax.ShapeDtypeStruct((depth, height, width), f32),
             jax.ShapeDtypeStruct((channels, depth, height, width), f32),
@@ -435,10 +484,11 @@
         scratch_shapes=[
             pltpu.VMEM((2, channels, span + 2 * margin), bf16),
             pltpu.VMEM((27 * deep, span), bf16),
-            pltpu.VMEM((deep * 2 * channels, span), f32),
+            pltpu.VMEM((deep * 2 * channels, narrow), f32),
             pltpu.VMEM((deep, span), f32),
-            pltpu.VMEM(((deep + 2) * 9 * channels, span), bf16),
-            pltpu.VMEM(((deep + 2) * 9 * channels, span), bf16),
+            pltpu.VMEM(((deep + 2) * 3 * channels, narrow), bf16),
+            pltpu.VMEM(((deep + 2) * 3 * channels, narrow), bf16),
+            pltpu.VMEM((2, 3 * depth * 2 * channels, narrow + 2 * margin), f32),
         ],
         compiler_params=pltpu.CompilerParams(vmem_limit_bytes=36 * 1024 * 1024),
     )(*operands)

time: 39.6 us -> 32.8 us (0.83); the launches traced: 38.8 us -> 32.6 us
  Pallas kernels: 20.9 us -> 14.5 us
    pallas_call x1, Pallas kernels: 19.2 us -> 12.7 us  [local_body(): pl.pallas_call(functools.partial(kernel, (deep, depth, channels, pitch, h...]
  transfers between devices with their start and end apart: 5 -> 5, of which waited for: 4 -> 4; matrix products, arithmetic and copies ran while one was open for 1% -> 1% of each run, Pallas kernels for 4% -> 6%
where the time goes in v3:
time: 32.8 us; the launch traced here: 32.6 us
  Pallas kernels  14.5 us (44%)
  starting transfers between devices  9.25 us (28%)
  waiting for transfers between devices  5.69 us (17%)
  local copies, waits for them, and re-layouts  1.97 us (6%)
  between operations  0.88 us (3%)
    pallas_call x1, Pallas kernels, local_body(): pl.pallas_call(functools.partial(kernel, (deep, depth, channels, pitch, h...  12.7 us
    ppermute x3, starting transfers between devices, gathered(): lax.ppermute(noisy, 'gz', [(i, (i + s) % count) for i in range(count)])  4.66 us
    ppermute x2, starting transfers between devices, swapped(): return lax.ppermute(value, axis, [(0, 1), (1, 0)])  4.6 us
    ppermute x3, waiting for transfers between devices, gathered(): lax.ppermute(noisy, 'gz', [(i, (i + s) % count) for i in range(count)])  4.14 us
    pallas_call x1, Pallas kernels, local_body(): pl.pallas_call(functools.partial(prepare, (deep, depth, channels)), out_s...  1.83 us
    unnamed x40, local copies, waits for them, and re-layouts  1.71 us
    ppermute x2, waiting for transfers between devices, swapped(): return lax.ppermute(value, axis, [(0, 1), (1, 0)])  1.55 us
  transfers between devices with their start and end apart: 5, of which 4 were waited for; matrix products, arithmetic and copies ran while one was open for 1% of the time, Pallas kernels for 6%

profile of v3, /device:TPU:1, one launch (start us, length us, event | category | flops | bytes accessed | tf_op | source)
XLA Modules:
  0.0 32.6 jit_solution(10069963572917307820)
XLA Ops:
  0.6 4.2 %collective-permute-start = (f32[4,8,128]{2,1,0:T(8,128)}, f32[4,8,128]{2,1,0:T(8,128)S(1)}, u32[]{:S(2)}, u32[]{:S(2)}) collective-permute-start(f32[4,8,128]{2,1,0:T(8,128)} %param.16), channel_id=1, source_target_pairs={{0,12},{4,0},{8,4},{12,8},{1,13},{5,1},{9,5},{13,9},{2,14},{6,2},{... | collective-permute-start | bytes 49160 | tf_op jit(solution)/shard_map/ppermute | solution.py:131
  4.8 0.5 %collective-permute-start.2 = (f32[4,8,128]{2,1,0:T(8,128)}, f32[4,8,128]{2,1,0:T(8,128)S(1)}, u32[]{:S(2)}, u32[]{:S(2)}) collective-permute-start(f32[4,8,128]{2,1,0:T(8,128)} %param.16), channel_id=1, source_target_pairs={{0,4},{4,8},{8,12},{12,0},{1,5},{5,9},{9,13},{13,1},{2,6},{6,10},{... | collective-permute-start | bytes 49160 | tf_op jit(solution)/shard_map/ppermute | solution.py:131
  5.3 0.6 %collective-permute-done = f32[4,8,128]{2,1,0:T(8,128)S(1)} collective-permute-done((f32[4,8,128]{2,1,0:T(8,128)}, f32[4,8,128]{2,1,0:T(8,128)S(1)}, u32[]{:S(2)}, u32[]{:S(2)}) %collective-permute-start) | collective-permute-done | bytes 16416 | tf_op jit(solution)/shard_map/ppermute | solution.py:131
  5.9 2.6 %collective-permute-done.1 = f32[4,8,128]{2,1,0:T(8,128)S(1)} collective-permute-done((f32[4,8,128]{2,1,0:T(8,128)}, f32[4,8,128]{2,1,0:T(8,128)S(1)}, u32[]{:S(2)}, u32[]{:S(2)}) %collective-permute-start.1) | collective-permute-done | bytes 16416 | tf_op jit(solution)/shard_map/ppermute | solution.py:131
  8.5 0.9 %collective-permute-done.2 = f32[4,8,128]{2,1,0:T(8,128)S(1)} collective-permute-done((f32[4,8,128]{2,1,0:T(8,128)}, f32[4,8,128]{2,1,0:T(8,128)S(1)}, u32[]{:S(2)}, u32[]{:S(2)}) %collective-permute-start.2) | collective-permute-done | bytes 16416 | tf_op jit(solution)/shard_map/ppermute | solution.py:131
  9.5 0.0 copy-start.13
  9.6 1.3 %collective-permute-start.3 = (f32[16,4,128]{2,1,0:T(4,128)S(1)}, f32[16,4,128]{2,1,0:T(4,128)S(1)}, u32[]{:S(2)}, u32[]{:S(2)}) collective-permute-start(f32[16,4,128]{2,1,0:T(4,128)S(1)} %rev.9), channel_id=1, source_target_pairs={{0,2},{2,0},{1,3},{3,1},{4,6},{6,4},{5,7},{7,5},{8,10},{10,8},{9,1... | collective-permute-start | bytes 98312 | tf_op jit(solution)/shard_map/ppermute | solution.py:124
  10.9 1.6 %collective-permute-done.3 = f32[16,4,128]{2,1,0:T(4,128)S(1)} collective-permute-done((f32[16,4,128]{2,1,0:T(4,128)S(1)}, f32[16,4,128]{2,1,0:T(4,128)S(1)}, u32[]{:S(2)}, u32[]{:S(2)}) %collective-permute-start.3) | collective-permute-done | bytes 32800 | tf_op jit(solution)/shard_map/ppermute | solution.py:124
  12.5 0.1 fusion
  12.6 3.3 %collective-permute-start.4 = (f32[16,12,4]{2,1,0:T(8,128)S(1)}, f32[16,12,4]{2,1,0:T(8,128)S(1)}, u32[]{:S(2)}, u32[]{:S(2)}) collective-permute-start(f32[16,12,4]{2,1,0:T(8,128)S(1)} %fusion), channel_id=1, source_target_pairs={{0,1},{1,0},{2,3},{3,2},{4,5},{5,4},{6,7},{7,6},{8,9},{9,8},{10,11... | collective-permute-start | bytes 9224 | tf_op jit(solution)/shard_map/ppermute | solution.py:124
  15.9 0.1 copy.21.w1_ref
  16.0 0.0 copy-start.2
  16.0 0.0 copy-start.3
  16.0 0.0 copy-start.4
  16.0 0.0 copy-start.5
  16.0 0.2 copy.20
  16.3 0.6 %copy-done = f32[16,16,27]{2,1,0:T(8,128)S(1)} copy-done((f32[16,16,27]{2,1,0:T(8,128)S(1)}, f32[16,16,27]{2,1,0:T(8,128)}, u32[]{:S(2)}) %copy-start) | copy-done | bytes 27672
  16.9 0.1 copy-done.6
  17.0 1.8 %shard_map.167 = (bf16[512,432]{1,0:T(8,128)(2,1)S(1)}, bf16[384,864]{1,0:T(8,128)(2,1)S(1)}, bf16[96,432]{1,0:T(8,128)(2,1)S(1)}, bf16[192,864]{1,0:T(8,128)(2,1)S(1)}, f32[16,128]{1,0:T(8,128)S(1)}) custom-call(f32[32,1,27]{2,1,0:T(1,128)S(1)} %copy.21.w1_ref, f32[1,16]{1,0:T(1,128)S(1)} %bitcast.9, f32[512,27]{1,0:T(8,128)S(1)} %bitcast.7, ...), custom_call_target="tpu_custom_call" | custom-call | tf_op jit(solution)/shard_map/pallas_call | solution.py:443
  18.8 0.1 maximum_select_fusion
  19.0 0.1 reshape.28
  19.2 0.0 copy-start.7
  19.2 0.7 %copy-done.7 = f32[1,1664]{1,0:T(1,128)S(1)} copy-done((f32[1,1664]{1,0:T(1,128)S(1)}, f32[1,1664]{1,0:T(1,128)}, u32[]{:S(2)}) %copy-start.7) | copy-done | bytes 6680
  19.9 12.7 %shard_map.168 = (f32[4,8,128]{2,1,0:T(8,128)}, f32[16,4,8,128]{3,2,1,0:T(8,128)}) custom-call(f32[16,1664]{1,0:T(8,128)S(1)} %pad.9.noisy_ref, f32[1,1664]{1,0:T(1,128)S(1)} %copy-done.7, bf16[512,432]{1,0:T(8,128)(2,1)S(1)} %get-tuple-element.7.w1_ref, bf16[384,864]{1,0:T(8,128)(2,1)S(1)} %get-tuple-element.8.w2_ref, ...), custom_call_target="tpu_custom_call" | custom-call | tf_op jit(solution)/shard_map/pallas_call | solution.py:476
  (39 shorter events, 0.2 us)
Async XLA Ops:
  0.6 5.3 %collective-permute-start = (f32[4,8,128]{2,1,0:T(8,128)}, f32[4,8,128]{2,1,0:T(8,128)S(1)}, u32[]{:S(2)}, u32[]{:S(2)}) collective-permute-start(f32[4,8,128]{2,1,0:T(8,128)} %param.16), channel_id=1, source_target_pairs={{0,12},{4,0},{8,4},{12,8},{1,13},{5,1},{9,5},{13,9},{2,14},{6,2},{... | collective-permute-start | bytes 49160 | tf_op jit(solution)/shard_map/ppermute | solution.py:131
  4.8 3.7 %collective-permute-start.1 = (f32[4,8,128]{2,1,0:T(8,128)}, f32[4,8,128]{2,1,0:T(8,128)S(1)}, u32[]{:S(2)}, u32[]{:S(2)}) collective-permute-start(f32[4,8,128]{2,1,0:T(8,128)} %param.16), channel_id=1, source_target_pairs={{0,8},{4,12},{8,0},{12,4},{1,9},{5,13},{9,1},{13,5},{2,10},{6,14},... | collective-permute-start | bytes 49160 | tf_op jit(solution)/shard_map/ppermute | solution.py:131
  4.8 4.6 %collective-permute-start.2 = (f32[4,8,128]{2,1,0:T(8,128)}, f32[4,8,128]{2,1,0:T(8,128)S(1)}, u32[]{:S(2)}, u32[]{:S(2)}) collective-permute-start(f32[4,8,128]{2,1,0:T(8,128)} %param.16), channel_id=1, source_target_pairs={{0,4},{4,8},{8,12},{12,0},{1,5},{5,9},{9,13},{13,1},{2,6},{6,10},{... | collective-permute-start | bytes 49160 | tf_op jit(solution)/shard_map/ppermute | solution.py:131
  8.5 0.9 %copy-start.14 = (f32[4,8,128]{2,1,0:T(8,128)S(1)}, f32[4,8,128]{2,1,0:T(8,128)}, u32[]{:S(2)}) copy-start(f32[4,8,128]{2,1,0:T(8,128)} %param.16) | copy-start | bytes 49156
  9.5 6.4 %copy-start.13 = (f32[32,16,27]{0,1,2:T(8,128)S(1)}, f32[32,16,27]{0,1,2:T(8,128)}, u32[]{:S(2)}) copy-start(f32[32,16,27]{0,1,2:T(8,128)} %param.19) | copy-start | bytes 165892
  9.6 2.8 %collective-permute-start.3 = (f32[16,4,128]{2,1,0:T(4,128)S(1)}, f32[16,4,128]{2,1,0:T(4,128)S(1)}, u32[]{:S(2)}, u32[]{:S(2)}) collective-permute-start(f32[16,4,128]{2,1,0:T(4,128)S(1)} %rev.9), channel_id=1, source_target_pairs={{0,2},{2,0},{1,3},{3,1},{4,6},{6,4},{5,7},{7,5},{8,10},{10,8},{9,1... | collective-permute-start | bytes 98312 | tf_op jit(solution)/shard_map/ppermute | solution.py:124
  10.9 5.0 %copy-start.15 = (f32[32,1,27]{0,1,2:T(1,128)S(1)}, f32[32,1,27]{0,1,2:T(1,128)}, u32[]{:S(2)}) copy-start(f32[32,1,27]{0,1,2:T(1,128)} %param.17) | copy-start | bytes 10372
  12.6 6.3 %collective-permute-start.4 = (f32[16,12,4]{2,1,0:T(8,128)S(1)}, f32[16,12,4]{2,1,0:T(8,128)S(1)}, u32[]{:S(2)}, u32[]{:S(2)}) collective-permute-start(f32[16,12,4]{2,1,0:T(8,128)S(1)} %fusion), channel_id=1, source_target_pairs={{0,1},{1,0},{2,3},{3,2},{4,5},{5,4},{6,7},{7,6},{8,9},{9,8},{10,11... | collective-permute-start | bytes 9224 | tf_op jit(solution)/shard_map/ppermute | solution.py:124
  16.0 0.9 %copy-start = (f32[16,16,27]{2,1,0:T(8,128)S(1)}, f32[16,16,27]{2,1,0:T(8,128)}, u32[]{:S(2)}) copy-start(f32[16,16,27]{2,1,0:T(8,128)} %param.24) | copy-start | bytes 82948
  16.0 0.9 %copy-start.1 = (bf16[32,512]{1,0:T(8,128)(2,1)S(1)}, bf16[32,512]{1,0:T(8,128)(2,1)}, u32[]{:S(2)}) copy-start(bf16[32,512]{1,0:T(8,128)(2,1)} %constant.38.clone.gather_ref) | copy-start | bytes 98308
  16.0 0.9 %copy-start.2 = (f32[16,432]{1,0:T(8,128)S(1)}, f32[16,432]{1,0:T(8,128)}, u32[]{:S(2)}) copy-start(f32[16,432]{1,0:T(8,128)} %constant.37.clone.keep_ref) | copy-start | bytes 82948
  16.0 0.9 %copy-start.3 = (s32[8,432]{1,0:T(8,128)S(1)}, s32[8,432]{1,0:T(8,128)}, u32[]{:S(2)}) copy-start(s32[8,432]{1,0:T(8,128)} %constant.36.clone.wide_lane_ref) | copy-start | bytes 41476
  16.0 0.9 %copy-start.4 = (s32[27,3]{1,0:T(8,128)S(1)}, s32[27,3]{1,0:T(8,128)}, u32[]{:S(2)}) copy-start(s32[27,3]{1,0:T(8,128)} %constant.35.clone.thin_sub_ref) | copy-start | bytes 976
  16.0 0.9 %copy-start.5 = (s32[8,432]{1,0:T(8,128)S(1)}, s32[8,432]{1,0:T(8,128)}, u32[]{:S(2)}) copy-start(s32[8,432]{1,0:T(8,128)} %constant.34.clone.thin_lane_ref) | copy-start | bytes 41476
  16.0 0.9 %copy-start.11 = (f32[16]{0:T(128)S(1)}, f32[16]{0:T(128)}, u32[]{:S(2)}) copy-start(f32[16]{0:T(128)} %param.23) | copy-start | bytes 196
  16.0 0.9 %copy-start.12 = (f32[16]{0:T(128)S(1)}, f32[16]{0:T(128)}, u32[]{:S(2)}) copy-start(f32[16]{0:T(128)} %param.25) | copy-start | bytes 196
  16.3 0.7 %copy-start.6 = (f32[16,1,27]{2,1,0:T(1,128)S(1)}, f32[16,1,27]{2,1,0:T(1,128)}, u32[]{:S(2)}) copy-start(f32[16,1,27]{2,1,0:T(1,128)} %w3_ref.1) | copy-start | bytes 5188
  16.3 0.7 %copy-start.8 = (f32[16]{0:T(128)S(1)}, f32[16]{0:T(128)}, u32[]{:S(2)}) copy-start(f32[16]{0:T(128)} %param.18) | copy-start | bytes 196
  16.3 0.7 %copy-start.9 = (f32[16]{0:T(128)S(1)}, f32[16]{0:T(128)}, u32[]{:S(2)}) copy-start(f32[16]{0:T(128)} %param.20) | copy-start | bytes 196
  16.3 0.7 %copy-start.10 = (f32[16]{0:T(128)S(1)}, f32[16]{0:T(128)}, u32[]{:S(2)}) copy-start(f32[16]{0:T(128)} %param.21) | copy-start | bytes 196
  19.2 0.7 %copy-start.7 = (f32[1,1664]{1,0:T(1,128)S(1)}, f32[1,1664]{1,0:T(1,128)}, u32[]{:S(2)}) copy-start(f32[1,1664]{1,0:T(1,128)} %constant.33.clone.mask_ref) | copy-start | bytes 19972

commit v4 on v3

--- a/solution.py
+++ b/solution.py
@@ -124,16 +124,20 @@
     return lax.ppermute(value, axis, [(0, 1), (1, 0)])
 
 
-def gathered(noisy):
+def gathered(noisy, laid_out):
     count = lax.axis_size("gz")
-    place = lax.axis_index("gz")
-    slabs = [
-        lax.ppermute(noisy, "gz", [(i, (i + s) % count) for i in range(count)])
-        for s in range(count - 1, 0, -1)
-    ] + [noisy]
-    turns = jnp.concatenate(slabs + slabs[:-1], axis=0)
-    depth = noisy.shape[0]
-    block = lax.dynamic_slice_in_dim(turns, (count - 1 - place) * depth, count * depth, 0)
+    block = noisy
+    step = 1
+    while step < count:
+        pairs = [(i, i ^ step) for i in range(count)]
+        other = lax.ppermute(block, "gz", pairs)
+        low = lax.axis_index("gz") // step % 2 == 0
+        block = jnp.where(
+            low, jnp.concatenate([block, other], 0), jnp.concatenate([other, block], 0)
+        )
+        if step == 1:
+            block, laid_out = lax.optimization_barrier((block, laid_out))
+        step *= 2
     block = jnp.where(lax.axis_index("gy") == 0, block, jnp.flip(block, 1))
     near = lax.slice_in_dim(block, block.shape[1] - HALO, None, axis=1)
     block = jnp.concatenate([block, swapped(jnp.flip(near, 1), "gy")], 1)
@@ -142,9 +146,14 @@
     low = lax.slice_in_dim(block, 0, HALO, axis=2)
     high = lax.slice_in_dim(block, size - HALO, size, axis=2)
     other = swapped(jnp.where(first, high, low), "gx")
-    return jnp.where(
-        first, jnp.concatenate([block, other], 2), jnp.concatenate([other, block], 2)
+    blank = jnp.zeros(block.shape[:2] + (1,), block.dtype)
+    window = jnp.where(
+        first,
+        jnp.concatenate([block, other, blank], 2),
+        jnp.concatenate([other, block, blank], 2),
     )
+    window = window.reshape(window.shape[0], -1)
+    return jnp.pad(window, ((0, 0), (0, -window.shape[1] % LANES))), laid_out
 
 
 def prepare(
@@ -190,7 +199,7 @@
         low = jnp.where(hit & crossed, 1.0, 0.0).astype(bf16)
         return (dot(halves[0], high) + dot(halves[1], low)).astype(bf16)
 
-    first = split(w1_ref[:, 0, :])
+    first = split(w1_ref[:, 0, :].T)
     out = 2 * channels
     for z in range(deep):
         w1_out[z * out : (z + 1) * out, :] = thin_rows(first, z)
@@ -202,28 +211,39 @@
             grow, jnp.where(inside, z, -deep)
         )
 
+    step = 3 * channels
+    part = (depth + 2) * step
+
+    def lay(pieces, w_out):
+        out = pieces[0][0].shape[0]
+        for b in range(3):
+            for i, half in enumerate((0, 0, 1)):
+                for z in range(depth):
+                    row = (b * depth + z) * out
+                    band[row : row + out, pl.ds(i * part + z * step, 3 * step)] = pieces[b][half]
+        w_out[...] = band[: w_out.shape[0], :].astype(bf16)
+
+    band[...] = jnp.zeros_like(band)
+    tall = w2_ref[...]
+    pieces = []
+    for b in range(3):
+        ahead, back = (
+            jnp.concatenate([tall[(a * 3 + k) * step : (a * 3 + k + 1) * step] for a in range(3)], 0)
+            for k in (b, 2 - b)
+        )
+        pieces.append(tuple(h.astype(f32) for h in split(jnp.where(turned, back, ahead).T)))
+    lay(pieces, w2_out)
+
+    band[: w4_out.shape[0], :] = jnp.zeros((w4_out.shape[0], 3 * part), f32)
     taps = lax.broadcasted_iota(jnp.int32, (27, wide_lane_ref.shape[1]), 0)
     spread = taps == jnp.where(turned, wide_lane_ref[1:2, :], wide_lane_ref[0:1, :])
     spread = jnp.where(spread, 1.0, 0.0).astype(bf16)
-    step = 3 * channels
-    part = (depth + 2) * step
-    band[...] = jnp.zeros_like(band)
-    for w_ref, w_out in ((w2_ref, w2_out), (w4_ref, w4_out)):
-        out = w_ref.shape[0] // channels
-        keep = jnp.concatenate([keep_ref[...]] * out, 0)
-        gather = gather_ref[:out, : out * channels]
-        flats = [
-            dot(gather, (dot(half, spread) * keep).astype(bf16)) for half in split(w_ref[...])
-        ]
-        for b in range(3):
-            for i, half in enumerate((0, 0, 1)):
-                piece = flats[half][:, b * 3 * step : (b + 1) * 3 * step]
-                for z in range(depth):
-                    row = (b * depth + z) * out
-                    band[row : row + out, pl.ds(i * part + z * step, 3 * step)] = piece
-        w_out[...] = band[: w_out.shape[0], :].astype(bf16)
-        if w_ref is w2_ref:
-            band[: w4_out.shape[0], :] = jnp.zeros((w4_out.shape[0], 3 * part), f32)
+    keep = jnp.concatenate([keep_ref[...]] * channels, 0)
+    flats = [
+        dot(gather_ref[...], (dot(half, spread) * keep).astype(bf16))
+        for half in split(w4_ref[...])
+    ]
+    lay([[f[:, b * 3 * step : (b + 1) * 3 * step] for f in flats] for b in range(3)], w4_out)
 
     at_row = lax.broadcasted_iota(jnp.int32, (channels, channels), 0)
     at_lane = lax.broadcasted_iota(jnp.int32, (channels, channels), 1)
@@ -236,7 +256,6 @@
 def kernel(
     geometry,
     noisy_ref,
-    mask_ref,
     w1_ref,
     w2_ref,
     w3_ref,
@@ -254,7 +273,11 @@
 ):
     deep, depth, channels, pitch, high, span, margin = geometry
     f32 = jnp.float32
-    mask = mask_ref[...]
+    lanes = lax.broadcasted_iota(jnp.int32, (1, span), 1)
+    blank = lanes >= high * pitch
+    for r in range(high):
+        blank = blank | (lanes == (r + 1) * pitch - 1)
+    mask = jnp.where(blank, 0.0, 1.0).astype(jnp.float32)
     place = lax.axis_index("gz")
     bias1, bias2, head, bias3, bias4 = (columns_ref[:, i : i + 1] for i in range(5))
     shifts = [(b - 1) * pitch + (c - 1) for b in range(3) for c in range(3)]
@@ -413,14 +436,7 @@
     margin = -(-(pitch + 1) // LANES) * LANES
     narrow = -(-(high - 1) * pitch // LANES) * LANES
 
-    window = gathered(noisy)
-    flat = jnp.pad(window, ((0, 0), (0, 0), (0, 1))).reshape(deep, high * pitch)
-    flat = jnp.pad(flat, ((0, 0), (0, span - high * pitch)))
-    inside = np.zeros((high, pitch), np.float32)
-    inside[:, : pitch - 1] = 1.0
-    mask = jnp.asarray(np.pad(inside.reshape(1, -1), ((0, 0), (0, span - high * pitch))))
-
-    f32, bf16, int32 = jnp.float32, jnp.bfloat16, jnp.int32
+    f32, bf16 = jnp.float32, jnp.bfloat16
     lane = np.arange(27 * deep)
     thin_lane = np.stack(
         [lane // deep % 9, lane % deep, lane // (9 * deep)] + [lane * 0] * 5
@@ -435,12 +451,12 @@
         [a * 9 + b * 3 + c, a * 9 + (2 - b) * 3 + c] + [lane * 0] * 6
     ).astype(np.int32)
     keep = (np.arange(channels)[:, None] == lane[None] % channels).astype(np.float32)
-    lane = np.arange(2 * channels * channels)
-    gather = (np.arange(2 * channels)[:, None] == lane[None] // channels).astype(bf16)
+    lane = np.arange(channels * channels)
+    gather = (np.arange(channels)[:, None] == lane[None] // channels).astype(bf16)
 
     taps = 3 * (depth + 2) * 3 * channels
     in_vmem = pl.BlockSpec(memory_space=pltpu.VMEM)
-    w1, w2, w3, w4, columns = pl.pallas_call(
+    prepared = pl.pallas_call(
         functools.partial(prepare, (deep, depth, channels)),
         out_shape=(
             pltpu.VMEM((deep * 2 * channels, 27 * deep), bf16),
@@ -453,25 +469,25 @@
         out_specs=(in_vmem,) * 5,
         scratch_shapes=[pltpu.VMEM((3 * depth * 2 * channels, taps), f32)],
         compiler_params=pltpu.CompilerParams(vmem_limit_bytes=16 * 1024 * 1024),
-    )(
-        first_weight,
+    )
+    weights = (
+        jnp.transpose(first_weight, (2, 1, 0)),
         first_bias.reshape(1, -1),
-        second_weight.reshape(-1, 27),
+        jnp.transpose(second_weight, (2, 1, 0)).reshape(-1, 2 * channels),
         second_bias.reshape(1, -1),
         head_weight.reshape(1, -1),
         seg_weight_in,
         seg_bias_in.reshape(1, -1),
         seg_weight_out.reshape(-1, 27),
         seg_bias_out.reshape(1, -1),
-        jnp.asarray(thin_lane),
-        jnp.asarray(thin_sub),
-        jnp.asarray(wide_lane),
-        jnp.asarray(keep),
-        jnp.asarray(gather),
     )
+    tables = tuple(jnp.asarray(v) for v in (thin_lane, thin_sub, wide_lane, keep, gather))
+
+    given = [pltpu.with_memory_space_constraint(v, pltpu.HBM) for v in weights + tables]
+    flat, laid_out = gathered(noisy, prepared(*given))
     operands = [
         pltpu.with_memory_space_constraint(v, pltpu.VMEM)
-        for v in (flat, mask, w1, w2, w3, w4, columns)
+        for v in (flat, *laid_out)
     ]
     return pl.pallas_call(
         functools.partial(kernel, (deep, depth, channels, pitch, high, span, margin)),
@@ -479,7 +495,7 @@
             jax.ShapeDtypeStruct((depth, height, width), f32),
             jax.ShapeDtypeStruct((channels, depth, height, width), f32),
         ),
-        in_specs=[in_vmem] * 7,
+        in_specs=[in_vmem] * 6,
         out_specs=(in_vmem,) * 2,
         scratch_shapes=[
             pltpu.VMEM((2, channels, span + 2 * margin), bf16),
@@ -497,6 +513,6 @@
 def solution(mesh):
     in_specs = (P(("win", "gz"), "gy", "gx"), P(), P(), P(), P(), P(), P(), P(), P(), P())
     out_specs = (P(("win", "gz"), "gy", "gx"), P(None, ("win", "gz"), "gy", "gx"))
-    shallow = mesh.shape["gz"] <= 4 and mesh.shape["gy"] == 2 and mesh.shape["gx"] == 2
+    shallow = mesh.shape["gz"] in (1, 2, 4) and mesh.shape["gy"] == 2 and mesh.shape["gx"] == 2
     chosen = local_body if shallow else body
     return jax.shard_map(chosen, mesh=mesh, in_specs=in_specs, out_specs=out_specs, check_vma=False)

time: 32.8 us -> 29.5 us (0.90)
  local copies, waits for them, and re-layouts: 1.97 us -> 0.3 us
  waiting for transfers between devices: 5.69 us -> 4.18 us
  Pallas kernels: 14.5 us -> 15.1 us
  starting transfers between devices: 9.25 us -> 8.8 us
    ppermute x3 -> x2, waiting for transfers between devices: 4.14 us -> 1.71 us  [gathered(): other = lax.ppermute(block, 'gz', pairs)]
    unnamed x40 -> x2, local copies, waits for them, and re-layouts: 1.71 us -> 0.01 us
    ppermute x2, waiting for transfers between devices: 1.55 us -> 2.47 us  [swapped(): return lax.ppermute(value, axis, [(0, 1), (1, 0)])]
    pallas_call x1, Pallas kernels: 1.83 us -> 2.38 us  [local_body(): flat, laid_out = gathered(noisy, prepared(*given))]
    ppermute x2, starting transfers between devices: 4.6 us -> 4.24 us  [swapped(): return lax.ppermute(value, axis, [(0, 1), (1, 0)])]
    ppermute x3 -> x2, starting transfers between devices: 4.66 us -> 4.56 us  [gathered(): other = lax.ppermute(block, 'gz', pairs)]
  transfers between devices with their start and end apart: 5 -> 4, of which waited for: 4 -> 3; matrix products, arithmetic and copies ran while one was open for 1% -> 0% of each run, Pallas kernels for 6% -> 8%
where the time goes in v4:
time: 29.5 us; the launch traced here: 29.3 us
  Pallas kernels  15.1 us (51%)
  starting transfers between devices  8.8 us (30%)
  waiting for transfers between devices  4.18 us (14%)
  between operations  0.72 us (2%)
  local copies, waits for them, and re-layouts  0.3 us (1%)
    pallas_call x1, Pallas kernels, local_body(): pl.pallas_call(functools.partial(kernel, (deep, depth, channels, pitch, h...  12.7 us
    ppermute x2, starting transfers between devices, gathered(): other = lax.ppermute(block, 'gz', pairs)  4.56 us
    ppermute x2, starting transfers between devices, swapped(): return lax.ppermute(value, axis, [(0, 1), (1, 0)])  4.24 us
    ppermute x2, waiting for transfers between devices, swapped(): return lax.ppermute(value, axis, [(0, 1), (1, 0)])  2.47 us
    pallas_call x1, Pallas kernels, local_body(): flat, laid_out = gathered(noisy, prepared(*given))  2.38 us
    ppermute x2, waiting for transfers between devices, gathered(): other = lax.ppermute(block, 'gz', pairs)  1.71 us
  transfers between devices with their start and end apart: 4, of which 3 were waited for; matrix products, arithmetic and copies ran while one was open for 0% of the time, Pallas kernels for 8%

profile of v4, /device:TPU:1, one launch (start us, length us, event | category | flops | bytes accessed | tf_op | source)
XLA Modules:
  0.0 29.3 jit_solution(5974910412900372106)
XLA Ops:
  0.6 2.2 %collective-permute-start = (f32[4,8,128]{2,1,0:T(8,128)}, f32[4,8,128]{2,1,0:T(8,128)S(1)}, u32[]{:S(2)}, u32[]{:S(2)}) collective-permute-start(f32[4,8,128]{2,1,0:T(8,128)} %param.15), channel_id=1, source_target_pairs={{0,4},{4,0},{8,12},{12,8},{1,5},{5,1},{9,13},{13,9},{2,6},{6,2},{1... | collective-permute-start | bytes 49160 | tf_op jit(solution)/shard_map/ppermute | solution.py:133
  2.8 0.0 copy-start
  2.8 2.4 %shard_map.158 = (bf16[512,432]{1,0:T(8,128)(2,1)S(1)}, bf16[384,864]{1,0:T(8,128)(2,1)S(1)}, bf16[96,432]{1,0:T(8,128)(2,1)S(1)}, bf16[192,864]{1,0:T(8,128)(2,1)S(1)}, f32[16,128]{1,0:T(8,128)S(1)}) custom-call(f32[27,1,32]{2,1,0:T(1,128)} %bitcast.13, f32[1,16]{1,0:T(1,128)} %bitcast.14, f32[432,32]{1,0:T(8,128)} %bitcast.11, f32[1,16]{1,0:T(1,128)} %bitcast.15, ...), custom_call_target="tpu_custom_call" | custom-call | tf_op jit(solution)/shard_map/pallas_call | solution.py:487
  5.2 0.0 collective-permute-done
  5.2 0.0 copy-done
  5.2 2.4 %collective-permute-start.1 = (f32[8,8,128]{2,1,0:T(8,128)S(1)}, f32[8,8,128]{2,1,0:T(8,128)S(1)}, u32[]{:S(2)}, u32[]{:S(2)}) collective-permute-start(f32[8,8,128]{2,1,0:T(8,128)S(1)} %maximum_select_fusion.2), channel_id=1, source_target_pairs={{0,8},{4,12},{8,0},{12,4},{1,9},{5,13},{9,1},{13,5},{2,10},{6,14},... | collective-permute-start | bytes 98312 | tf_op jit(solution)/shard_map/ppermute | solution.py:133
  7.6 1.7 %collective-permute-done.1 = f32[8,8,128]{2,1,0:T(8,128)S(1)} collective-permute-done((f32[8,8,128]{2,1,0:T(8,128)S(1)}, f32[8,8,128]{2,1,0:T(8,128)S(1)}, u32[]{:S(2)}, u32[]{:S(2)}) %collective-permute-start.1) | collective-permute-done | bytes 32800 | tf_op jit(solution)/shard_map/ppermute | solution.py:133
  9.4 1.3 %collective-permute-start.2 = (f32[16,4,128]{2,1,0:T(4,128)S(1)}, f32[16,4,128]{2,1,0:T(4,128)S(1)}, u32[]{:S(2)}, u32[]{:S(2)}) collective-permute-start(f32[16,4,128]{2,1,0:T(4,128)S(1)} %rev.9), channel_id=1, source_target_pairs={{0,2},{2,0},{1,3},{3,1},{4,6},{6,4},{5,7},{7,5},{8,10},{10,8},{9,1... | collective-permute-start | bytes 98312 | tf_op jit(solution)/shard_map/ppermute | solution.py:124
  10.7 1.6 %collective-permute-done.2 = f32[16,4,128]{2,1,0:T(4,128)S(1)} collective-permute-done((f32[16,4,128]{2,1,0:T(4,128)S(1)}, f32[16,4,128]{2,1,0:T(4,128)S(1)}, u32[]{:S(2)}, u32[]{:S(2)}) %collective-permute-start.2) | collective-permute-done | bytes 32800 | tf_op jit(solution)/shard_map/ppermute | solution.py:124
  12.3 0.1 fusion
  12.4 3.0 %collective-permute-start.3 = (f32[16,12,4]{2,1,0:T(8,128)S(1)}, f32[16,12,4]{2,1,0:T(8,128)S(1)}, u32[]{:S(2)}, u32[]{:S(2)}) collective-permute-start(f32[16,12,4]{2,1,0:T(8,128)S(1)} %fusion), channel_id=1, source_target_pairs={{0,1},{1,0},{2,3},{3,2},{4,5},{5,4},{6,7},{7,6},{8,9},{9,8},{10,11... | collective-permute-start | bytes 9224 | tf_op jit(solution)/shard_map/ppermute | solution.py:124
  15.3 0.1 pad.12.clone
  15.4 0.9 %collective-permute-done.3 = f32[16,12,4]{2,1,0:T(8,128)S(1)} collective-permute-done((f32[16,12,4]{2,1,0:T(8,128)S(1)}, f32[16,12,4]{2,1,0:T(8,128)S(1)}, u32[]{:S(2)}, u32[]{:S(2)}) %collective-permute-start.3) | collective-permute-done | bytes 3104 | tf_op jit(solution)/shard_map/ppermute | solution.py:124
  16.3 0.1 maximum_select_fusion
  16.5 0.1 select_n.71
  16.6 12.7 %shard_map.159 = (f32[4,8,128]{2,1,0:T(8,128)}, f32[16,4,8,128]{3,2,1,0:T(8,128)}) custom-call(f32[16,1664]{1,0:T(8,128)S(1)} %pad.4.noisy_ref, bf16[512,432]{1,0:T(8,128)(2,1)S(1)} %get-tuple-element.19.w1_ref, bf16[384,864]{1,0:T(8,128)(2,1)S(1)} %get-tuple-element.20.w2_ref, bf16[96,432]{1,0:T(8,128)(2,1)S(1)} %get-tuple-element.21.w3_ref, ...), custom_call_target="tpu_custom_call" | custom-call | tf_op jit(solution)/shard_map/pallas_call | solution.py:492
  (7 shorter events, 0.1 us)
Async XLA Ops:
  0.6 4.6 %collective-permute-start = (f32[4,8,128]{2,1,0:T(8,128)}, f32[4,8,128]{2,1,0:T(8,128)S(1)}, u32[]{:S(2)}, u32[]{:S(2)}) collective-permute-start(f32[4,8,128]{2,1,0:T(8,128)} %param.15), channel_id=1, source_target_pairs={{0,4},{4,0},{8,12},{12,8},{1,5},{5,1},{9,13},{13,9},{2,6},{6,2},{1... | collective-permute-start | bytes 49160 | tf_op jit(solution)/shard_map/ppermute | solution.py:133
  2.8 2.4 %copy-start = (f32[4,8,128]{2,1,0:T(8,128)S(1)}, f32[4,8,128]{2,1,0:T(8,128)}, u32[]{:S(2)}) copy-start(f32[4,8,128]{2,1,0:T(8,128)} %param.15) | copy-start | bytes 49156
  5.2 4.1 %collective-permute-start.1 = (f32[8,8,128]{2,1,0:T(8,128)S(1)}, f32[8,8,128]{2,1,0:T(8,128)S(1)}, u32[]{:S(2)}, u32[]{:S(2)}) collective-permute-start(f32[8,8,128]{2,1,0:T(8,128)S(1)} %maximum_select_fusion.2), channel_id=1, source_target_pairs={{0,8},{4,12},{8,0},{12,4},{1,9},{5,13},{9,1},{13,5},{2,10},{6,14},... | collective-permute-start | bytes 98312 | tf_op jit(solution)/shard_map/ppermute | solution.py:133
  9.4 2.8 %collective-permute-start.2 = (f32[16,4,128]{2,1,0:T(4,128)S(1)}, f32[16,4,128]{2,1,0:T(4,128)S(1)}, u32[]{:S(2)}, u32[]{:S(2)}) collective-permute-start(f32[16,4,128]{2,1,0:T(4,128)S(1)} %rev.9), channel_id=1, source_target_pairs={{0,2},{2,0},{1,3},{3,1},{4,6},{6,4},{5,7},{7,5},{8,10},{10,8},{9,1... | collective-permute-start | bytes 98312 | tf_op jit(solution)/shard_map/ppermute | solution.py:124
  12.4 4.0 %collective-permute-start.3 = (f32[16,12,4]{2,1,0:T(8,128)S(1)}, f32[16,12,4]{2,1,0:T(8,128)S(1)}, u32[]{:S(2)}, u32[]{:S(2)}) collective-permute-start(f32[16,12,4]{2,1,0:T(8,128)S(1)} %fusion), channel_id=1, source_target_pairs={{0,1},{1,0},{2,3},{3,2},{4,5},{5,4},{6,7},{7,6},{8,9},{9,8},{10,11... | collective-permute-start | bytes 9224 | tf_op jit(solution)/shard_map/ppermute | solution.py:124

commit v5 on v4

--- a/solution.py
+++ b/solution.py
@@ -112,7 +112,7 @@
 
 
 HALO = 4
-LANES = 128
+LANES, SUBLANES = 128, 8
 
 
 def split(value):
@@ -270,6 +270,7 @@
     wide_hi,
     wide_lo,
     sums,
+    tiles,
 ):
     deep, depth, channels, pitch, high, span, margin = geometry
     f32 = jnp.float32
@@ -285,16 +286,17 @@
         -(-(high - i) * pitch // LANES) * LANES for i in range(1, 4)
     )
     blocks = deep // depth
-
-    def put(field):
-        for slot, half in enumerate(split(field)):
-            stage[slot, :, pl.ds(margin, field.shape[1])] = half
-
-    def shifted(slot, shift, length):
-        return stage[slot, :, pl.ds(margin + shift, length)]
+    height, width = den_ref.shape[1:]
+
+    def put(field, slot):
+        for part, half in enumerate(split(field)):
+            stage[2 * slot + part, :, pl.ds(margin, field.shape[1])] = half
+
+    def shifted(part, shift, length, slot=0):
+        return stage[2 * slot + part, :, pl.ds(margin + shift, length)]
 
     def thin_columns(field, length):
-        put(field)
+        put(field, 0)
         for t, s in enumerate(shifts):
             h = shifted(0, s, length)
             thin[t * deep : (t + 1) * deep, :length] = h
@@ -302,12 +304,21 @@
             thin[(18 + t) * deep : (19 + t) * deep, :length] = shifted(1, s, length)
 
     def wide_columns(z, field):
-        length = field.shape[1]
-        put(field)
+        length, slot = field.shape[1], z % (depth + 2)
+        put(field, slot)
         for c in range(3):
             at = (z * 3 + c) * channels
-            wide_hi[at : at + channels, :length] = shifted(0, c - 1, length)
-            wide_lo[at : at + channels, :length] = shifted(1, c - 1, length)
+            wide_hi[at : at + channels, :length] = shifted(0, c - 1, length, slot)
+            wide_lo[at : at + channels, :length] = shifted(1, c - 1, length, slot)
+
+    def own_columns(z, offset):
+        for c in range(3):
+            at = (z * 3 + c) * channels
+            for r in range(height + 1):
+                lanes = slice(r * width, (r + 1) * width)
+                shift = r * pitch + offset + c - 1
+                wide_hi[at : at + channels, lanes] = shifted(0, shift, width, z)
+                wide_lo[at : at + channels, lanes] = shifted(1, shift, width, z)
 
     taps = (depth + 2) * 3 * channels
 
@@ -387,31 +398,44 @@
         z = place * depth + i - 1
         real = jnp.where((z >= 0) & (z < deep), 1.0, 0.0)
         features = jnp.maximum(grown[i * channels : (i + 1) * channels] + bias3, 0.0)
-        wide_columns(i, features * (mask[:, :third_span] * real))
-    for chunk in chunks(third_span):
+        put(features * (mask[:, :third_span] * real), i)
+
+    turned = lax.axis_index("gy") == 1
+
+    def at_row(r):
+        return jnp.where(turned, height - 1 - r, r)
+
+    for x in range(2):
+
+        @pl.when(lax.axis_index("gx") == x)
+        def _():
+            for i in range(depth + 2):
+                own_columns(i, x * HALO)
+            for r in range(height):
+                lanes = pl.ds(r * pitch + x * HALO, width)
+                mine = rows[:depth, lanes]
+                for b in range(1, deep // depth):
+                    mine = jnp.where(place == b, rows[b * depth : (b + 1) * depth, lanes], mine)
+                at = pl.multiple_of(at_row(r) * SUBLANES, SUBLANES)
+                tiles[pl.ds(at, depth), :] = mine
+
+    for z in range(depth):
+        den_ref[z] = tiles[pl.ds(z, height, stride=SUBLANES), :]
+    for chunk in chunks((height + 1) * width):
         banded(w4_ref, 0, 0, chunk)
-
-    height, width = den_ref.shape[1:]
-    for y in range(2):
-        for x in range(2):
-
-            @pl.when((lax.axis_index("gy") == y) & (lax.axis_index("gx") == x))
-            def _():
-                for r in range(height):
-                    row = height - 1 - r if y else r
-                    at = r * pitch + x * HALO
-                    mine = rows[:depth, pl.ds(at, width)]
-                    for b in range(1, blocks):
-                        other = rows[b * depth : (b + 1) * depth, pl.ds(at, width)]
-                        mine = jnp.where(place == b, other, mine)
-                    den_ref[:, row, :] = mine
-                    for z in range(depth):
-                        total = bias4
-                        for b in range(3):
-                            k = (b * depth + z) * channels
-                            lanes = pl.ds(margin + at + (b - 1) * pitch, width)
-                            total = total + sums[0, k : k + channels, lanes]
-                        seg_ref[:, z, row, :] = total
+    for z in range(depth):
+        for r in range(height):
+            total = bias4
+            for b in range(3):
+                if r + b > 0:
+                    k = (b * depth + z) * channels
+                    lanes = pl.ds(margin + (r + b - 1) * width, width)
+                    total = total + sums[0, k : k + channels, lanes]
+            at = pl.multiple_of((z * height + at_row(r)) * channels, channels)
+            tiles[pl.ds(at, channels), :] = total
+    for z in range(depth):
+        for o in range(channels):
+            seg_ref[o, z] = tiles[pl.ds(z * height * channels + o, height, stride=channels), :]
 
 
 def local_body(
@@ -498,13 +522,14 @@
         in_specs=[in_vmem] * 6,
         out_specs=(in_vmem,) * 2,
         scratch_shapes=[
-            pltpu.VMEM((2, channels, span + 2 * margin), bf16),
+            pltpu.VMEM((2 * (depth + 2), channels, span + 2 * margin), bf16),
             pltpu.VMEM((27 * deep, span), bf16),
             pltpu.VMEM((deep * 2 * channels, narrow), f32),
             pltpu.VMEM((deep, span), f32),
             pltpu.VMEM(((deep + 2) * 3 * channels, narrow), bf16),
             pltpu.VMEM(((deep + 2) * 3 * channels, narrow), bf16),
             pltpu.VMEM((2, 3 * depth * 2 * channels, narrow + 2 * margin), f32),
+            pltpu.VMEM((depth * height * channels, width), f32),
         ],
         compiler_params=pltpu.CompilerParams(vmem_limit_bytes=36 * 1024 * 1024),
     )(*operands)

time: 29.5 us -> 26.7 us (0.905)
  Pallas kernels: 15.1 us -> 12 us
    pallas_call x1, Pallas kernels: 12.7 us -> 9.63 us  [local_body(): pl.pallas_call(functools.partial(kernel, (deep, depth, channels, pitch, h...]
  transfers between devices with their start and end apart: 4 -> 4, of which waited for: 3 -> 3; matrix products, arithmetic and copies ran while one was open for 0% -> 0% of each run, Pallas kernels for 8% -> 9%
where the time goes in v5:
time: 26.7 us; the launch traced here: 26.3 us
  Pallas kernels  12 us (45%)
  starting transfers between devices  8.82 us (33%)
  waiting for transfers between devices  4.17 us (16%)
  between operations  0.72 us (3%)
  local copies, waits for them, and re-layouts  0.3 us (1%)
    pallas_call x1, Pallas kernels, local_body(): pl.pallas_call(functools.partial(kernel, (deep, depth, channels, pitch, h...  9.63 us
    ppermute x2, starting transfers between devices, gathered(): other = lax.ppermute(block, 'gz', pairs)  4.57 us
    ppermute x2, starting transfers between devices, swapped(): return lax.ppermute(value, axis, [(0, 1), (1, 0)])  4.25 us
    ppermute x2, waiting for transfers between devices, swapped(): return lax.ppermute(value, axis, [(0, 1), (1, 0)])  2.47 us
    pallas_call x1, Pallas kernels, local_body(): flat, laid_out = gathered(noisy, prepared(*given))  2.37 us
    ppermute x2, waiting for transfers between devices, gathered(): other = lax.ppermute(block, 'gz', pairs)  1.7 us
  transfers between devices with their start and end apart: 4, of which 3 were waited for; matrix products, arithmetic and copies ran while one was open for 0% of the time, Pallas kernels for 9%

profile of v5, /device:TPU:1, one launch (start us, length us, event | category | flops | bytes accessed | tf_op | source)
XLA Modules:
  0.0 26.3 jit_solution(13353995843856084648)
XLA Ops:
  0.6 2.2 %collective-permute-start = (f32[4,8,128]{2,1,0:T(8,128)}, f32[4,8,128]{2,1,0:T(8,128)S(1)}, u32[]{:S(2)}, u32[]{:S(2)}) collective-permute-start(f32[4,8,128]{2,1,0:T(8,128)} %param.15), channel_id=1, source_target_pairs={{0,4},{4,0},{8,12},{12,8},{1,5},{5,1},{9,13},{13,9},{2,6},{6,2},{1... | collective-permute-start | bytes 49160 | tf_op jit(solution)/shard_map/ppermute | solution.py:133
  2.8 0.0 copy-start
  2.8 2.4 %shard_map.158 = (bf16[512,432]{1,0:T(8,128)(2,1)S(1)}, bf16[384,864]{1,0:T(8,128)(2,1)S(1)}, bf16[96,432]{1,0:T(8,128)(2,1)S(1)}, bf16[192,864]{1,0:T(8,128)(2,1)S(1)}, f32[16,128]{1,0:T(8,128)S(1)}) custom-call(f32[27,1,32]{2,1,0:T(1,128)} %bitcast.13, f32[1,16]{1,0:T(1,128)} %bitcast.14, f32[432,32]{1,0:T(8,128)} %bitcast.11, f32[1,16]{1,0:T(1,128)} %bitcast.15, ...), custom_call_target="tpu_custom_call" | custom-call | tf_op jit(solution)/shard_map/pallas_call | solution.py:511
  5.2 0.0 collective-permute-done
  5.2 0.0 copy-done
  5.2 2.4 %collective-permute-start.1 = (f32[8,8,128]{2,1,0:T(8,128)S(1)}, f32[8,8,128]{2,1,0:T(8,128)S(1)}, u32[]{:S(2)}, u32[]{:S(2)}) collective-permute-start(f32[8,8,128]{2,1,0:T(8,128)S(1)} %maximum_select_fusion.2), channel_id=1, source_target_pairs={{0,8},{4,12},{8,0},{12,4},{1,9},{5,13},{9,1},{13,5},{2,10},{6,14},... | collective-permute-start | bytes 98312 | tf_op jit(solution)/shard_map/ppermute | solution.py:133
  7.6 1.7 %collective-permute-done.1 = f32[8,8,128]{2,1,0:T(8,128)S(1)} collective-permute-done((f32[8,8,128]{2,1,0:T(8,128)S(1)}, f32[8,8,128]{2,1,0:T(8,128)S(1)}, u32[]{:S(2)}, u32[]{:S(2)}) %collective-permute-start.1) | collective-permute-done | bytes 32800 | tf_op jit(solution)/shard_map/ppermute | solution.py:133
  9.4 1.3 %collective-permute-start.2 = (f32[16,4,128]{2,1,0:T(4,128)S(1)}, f32[16,4,128]{2,1,0:T(4,128)S(1)}, u32[]{:S(2)}, u32[]{:S(2)}) collective-permute-start(f32[16,4,128]{2,1,0:T(4,128)S(1)} %rev.9), channel_id=1, source_target_pairs={{0,2},{2,0},{1,3},{3,1},{4,6},{6,4},{5,7},{7,5},{8,10},{10,8},{9,1... | collective-permute-start | bytes 98312 | tf_op jit(solution)/shard_map/ppermute | solution.py:124
  10.7 1.6 %collective-permute-done.2 = f32[16,4,128]{2,1,0:T(4,128)S(1)} collective-permute-done((f32[16,4,128]{2,1,0:T(4,128)S(1)}, f32[16,4,128]{2,1,0:T(4,128)S(1)}, u32[]{:S(2)}, u32[]{:S(2)}) %collective-permute-start.2) | collective-permute-done | bytes 32800 | tf_op jit(solution)/shard_map/ppermute | solution.py:124
  12.3 0.1 fusion
  12.4 3.0 %collective-permute-start.3 = (f32[16,12,4]{2,1,0:T(8,128)S(1)}, f32[16,12,4]{2,1,0:T(8,128)S(1)}, u32[]{:S(2)}, u32[]{:S(2)}) collective-permute-start(f32[16,12,4]{2,1,0:T(8,128)S(1)} %fusion), channel_id=1, source_target_pairs={{0,1},{1,0},{2,3},{3,2},{4,5},{5,4},{6,7},{7,6},{8,9},{9,8},{10,11... | collective-permute-start | bytes 9224 | tf_op jit(solution)/shard_map/ppermute | solution.py:124
  15.3 0.1 pad.12.clone
  15.4 0.9 %collective-permute-done.3 = f32[16,12,4]{2,1,0:T(8,128)S(1)} collective-permute-done((f32[16,12,4]{2,1,0:T(8,128)S(1)}, f32[16,12,4]{2,1,0:T(8,128)S(1)}, u32[]{:S(2)}, u32[]{:S(2)}) %collective-permute-start.3) | collective-permute-done | bytes 3104 | tf_op jit(solution)/shard_map/ppermute | solution.py:124
  16.3 0.1 maximum_select_fusion
  16.5 0.1 select_n.71
  16.6 9.6 %shard_map.159 = (f32[4,8,128]{2,1,0:T(8,128)}, f32[16,4,8,128]{3,2,1,0:T(8,128)}) custom-call(f32[16,1664]{1,0:T(8,128)S(1)} %pad.4.noisy_ref, bf16[512,432]{1,0:T(8,128)(2,1)S(1)} %get-tuple-element.19.w1_ref, bf16[384,864]{1,0:T(8,128)(2,1)S(1)} %get-tuple-element.20.w2_ref, bf16[96,432]{1,0:T(8,128)(2,1)S(1)} %get-tuple-element.21.w3_ref, ...), custom_call_target="tpu_custom_call" | custom-call | tf_op jit(solution)/shard_map/pallas_call | solution.py:516
  (7 shorter events, 0.1 us)
Async XLA Ops:
  0.6 4.6 %collective-permute-start = (f32[4,8,128]{2,1,0:T(8,128)}, f32[4,8,128]{2,1,0:T(8,128)S(1)}, u32[]{:S(2)}, u32[]{:S(2)}) collective-permute-start(f32[4,8,128]{2,1,0:T(8,128)} %param.15), channel_id=1, source_target_pairs={{0,4},{4,0},{8,12},{12,8},{1,5},{5,1},{9,13},{13,9},{2,6},{6,2},{1... | collective-permute-start | bytes 49160 | tf_op jit(solution)/shard_map/ppermute | solution.py:133
  2.8 2.4 %copy-start = (f32[4,8,128]{2,1,0:T(8,128)S(1)}, f32[4,8,128]{2,1,0:T(8,128)}, u32[]{:S(2)}) copy-start(f32[4,8,128]{2,1,0:T(8,128)} %param.15) | copy-start | bytes 49156
  5.2 4.1 %collective-permute-start.1 = (f32[8,8,128]{2,1,0:T(8,128)S(1)}, f32[8,8,128]{2,1,0:T(8,128)S(1)}, u32[]{:S(2)}, u32[]{:S(2)}) collective-permute-start(f32[8,8,128]{2,1,0:T(8,128)S(1)} %maximum_select_fusion.2), channel_id=1, source_target_pairs={{0,8},{4,12},{8,0},{12,4},{1,9},{5,13},{9,1},{13,5},{2,10},{6,14},... | collective-permute-start | bytes 98312 | tf_op jit(solution)/shard_map/ppermute | solution.py:133
  9.4 2.8 %collective-permute-start.2 = (f32[16,4,128]{2,1,0:T(4,128)S(1)}, f32[16,4,128]{2,1,0:T(4,128)S(1)}, u32[]{:S(2)}, u32[]{:S(2)}) collective-permute-start(f32[16,4,128]{2,1,0:T(4,128)S(1)} %rev.9), channel_id=1, source_target_pairs={{0,2},{2,0},{1,3},{3,1},{4,6},{6,4},{5,7},{7,5},{8,10},{10,8},{9,1... | collective-permute-start | bytes 98312 | tf_op jit(solution)/shard_map/ppermute | solution.py:124
  12.4 4.0 %collective-permute-start.3 = (f32[16,12,4]{2,1,0:T(8,128)S(1)}, f32[16,12,4]{2,1,0:T(8,128)S(1)}, u32[]{:S(2)}, u32[]{:S(2)}) collective-permute-start(f32[16,12,4]{2,1,0:T(8,128)S(1)} %fusion), channel_id=1, source_target_pairs={{0,1},{1,0},{2,3},{3,2},{4,5},{5,4},{6,7},{7,6},{8,9},{9,8},{10,11... | collective-permute-start | bytes 9224 | tf_op jit(solution)/shard_map/ppermute | solution.py:124

commit v6 on v5

--- a/solution.py
+++ b/solution.py
@@ -112,6 +112,7 @@
 
 
 HALO = 4
+AHEAD, PACE = 8, 4
 LANES, SUBLANES = 128, 8
 
 
@@ -212,18 +213,14 @@
         )
 
     step = 3 * channels
-    part = (depth + 2) * step
 
     def lay(pieces, w_out):
         out = pieces[0][0].shape[0]
         for b in range(3):
             for i, half in enumerate((0, 0, 1)):
-                for z in range(depth):
-                    row = (b * depth + z) * out
-                    band[row : row + out, pl.ds(i * part + z * step, 3 * step)] = pieces[b][half]
+                band[b * out : (b + 1) * out, pl.ds(i * 3 * step, 3 * step)] = pieces[b][half]
         w_out[...] = band[: w_out.shape[0], :].astype(bf16)
 
-    band[...] = jnp.zeros_like(band)
     tall = w2_ref[...]
     pieces = []
     for b in range(3):
@@ -234,7 +231,6 @@
         pieces.append(tuple(h.astype(f32) for h in split(jnp.where(turned, back, ahead).T)))
     lay(pieces, w2_out)
 
-    band[: w4_out.shape[0], :] = jnp.zeros((w4_out.shape[0], 3 * part), f32)
     taps = lax.broadcasted_iota(jnp.int32, (27, wide_lane_ref.shape[1]), 0)
     spread = taps == jnp.where(turned, wide_lane_ref[1:2, :], wide_lane_ref[0:1, :])
     spread = jnp.where(spread, 1.0, 0.0).astype(bf16)
@@ -285,8 +281,9 @@
     first_span, second_span, third_span = (
         -(-(high - i) * pitch // LANES) * LANES for i in range(1, 4)
     )
-    blocks = deep // depth
     height, width = den_ref.shape[1:]
+
+    edge = 3 * channels
 
     def put(field, slot):
         for part, half in enumerate(split(field)):
@@ -320,16 +317,15 @@
                 wide_hi[at : at + channels, lanes] = shifted(0, shift, width, z)
                 wide_lo[at : at + channels, lanes] = shifted(1, shift, width, z)
 
-    taps = (depth + 2) * 3 * channels
-
     def chunks(length):
         return [(i, min(2 * LANES, length - i)) for i in range(0, length, 2 * LANES)]
 
-    def banded(w_ref, slot, start, chunk):
+    def convolve(w_ref, z, chunk):
         at, length = chunk
-        h = wide_hi[start : start + taps, at : at + length]
-        l = wide_lo[start : start + taps, at : at + length]
-        sums[slot, : w_ref.shape[0], pl.ds(margin + at, length)] = jnp.dot(
+        taps = slice(z * edge, (z + 3) * edge)
+        h = wide_hi[taps, at : at + length]
+        l = wide_lo[taps, at : at + length]
+        sums[z, : w_ref.shape[0], pl.ds(margin + at, length)] = jnp.dot(
             w_ref[...], jnp.concatenate([h, l, h], 0), preferred_element_type=f32
         )
 
@@ -338,10 +334,9 @@
         return hidden + fresh * (jnp.tanh(cand) - hidden)
 
     stage[...] = jnp.zeros_like(stage)
-    aside = jnp.zeros(sums.shape[:2] + (margin,), f32)
-    sums[:, :, :margin] = aside
-    sums[:, :, sums.shape[2] - margin :] = aside
-    edge = 3 * channels
+    before = jnp.zeros((deep, 2 * channels, margin), f32)
+    sums[:, : 2 * channels, :margin] = before
+    sums[:, 4 * channels :, margin + first_span :] = before
     zeros = jnp.zeros((edge, wide_hi.shape[1]), jnp.bfloat16)
     for wide in (wide_hi, wide_lo):
         wide[:edge, :] = zeros
@@ -349,8 +344,20 @@
 
     noisy = noisy_ref[...]
     thin_columns(noisy, first_span)
-    pre[...] = jnp.dot(w1_ref[...], thin[:, :first_span], preferred_element_type=f32)
-
+    todo = chunks(first_span)
+    part = depth * 2 * channels
+
+    def thin_block(b, chunk):
+        at, length = chunk
+        pre[b * part : (b + 1) * part, at : at + length] = jnp.dot(
+            w1_ref[b * part : (b + 1) * part, :],
+            thin[:, at : at + length],
+            preferred_element_type=f32,
+        )
+
+    for chunk in todo:
+        thin_block(0, chunk)
+    waiting = []
     hidden = jnp.zeros((channels, first_span), f32)
     for z in range(deep):
         at = z * 2 * channels
@@ -360,35 +367,33 @@
             hidden,
         )
         wide_columns(z + 1, hidden * mask[:, :first_span])
-
-    def layer(slot, at, length, lift=0):
+        if z // depth + 1 < deep // depth:
+            for chunk in todo[z % depth :: depth]:
+                thin_block(z // depth + 1, chunk)
+        if 0 < z <= AHEAD:
+            waiting += [(z - 1, chunk) for chunk in todo]
+        for _ in range(min(PACE, len(waiting))):
+            convolve(w2_ref, *waiting.pop(0))
+
+    def layer(z, at):
         return sum(
             sums[
-                slot,
-                at + b * depth * lift : at + b * depth * lift + channels,
-                pl.ds(margin + (b - 1) * pitch, length),
+                z,
+                at + b * 2 * channels : at + (b * 2 + 1) * channels,
+                pl.ds(margin + (b - 1) * pitch, second_span),
             ]
             for b in range(3)
         )
 
+    later = [(z, chunk) for z in range(deep - 1, AHEAD - 1, -1) for chunk in todo] + waiting
+    for _ in range(min(2 * len(todo), len(later))):
+        convolve(w2_ref, *later.pop(0))
     hidden = jnp.zeros((channels, second_span), f32)
-    todo = chunks(first_span)
-    for chunk in todo:
-        banded(w2_ref, (blocks - 1) % 2, (blocks - 1) * depth * edge, chunk)
-    for b in range(blocks - 1, -1, -1):
-        for zo in range(depth - 1, -1, -1):
-            if b > 0:
-                turn = depth - 1 - zo
-                for chunk in todo[turn::depth]:
-                    banded(w2_ref, (b - 1) % 2, (b - 1) * depth * edge, chunk)
-            at = zo * 2 * channels
-            hidden = gate(
-                layer(b % 2, at, second_span, 2 * channels),
-                layer(b % 2, at + channels, second_span, 2 * channels) + bias2,
-                hidden,
-            )
-            z = b * depth + zo
-            rows[z : z + 1, :second_span] = jnp.sum(hidden * head, axis=0, keepdims=True)
+    for z in range(deep - 1, -1, -1):
+        for _ in range(min(len(todo), len(later))):
+            convolve(w2_ref, *later.pop(0))
+        hidden = gate(layer(z, 0), layer(z, channels) + bias2, hidden)
+        rows[z : z + 1, :second_span] = jnp.sum(hidden * head, axis=0, keepdims=True)
 
     finished = (noisy[:, :second_span] + rows[:, :second_span]) * mask[:, :second_span]
     rows[:, :second_span] = finished
@@ -421,16 +426,16 @@
 
     for z in range(depth):
         den_ref[z] = tiles[pl.ds(z, height, stride=SUBLANES), :]
-    for chunk in chunks((height + 1) * width):
-        banded(w4_ref, 0, 0, chunk)
+    for z in range(depth):
+        for chunk in chunks((height + 1) * width):
+            convolve(w4_ref, z, chunk)
     for z in range(depth):
         for r in range(height):
             total = bias4
             for b in range(3):
                 if r + b > 0:
-                    k = (b * depth + z) * channels
                     lanes = pl.ds(margin + (r + b - 1) * width, width)
-                    total = total + sums[0, k : k + channels, lanes]
+                    total = total + sums[z, b * channels : (b + 1) * channels, lanes]
             at = pl.multiple_of((z * height + at_row(r)) * channels, channels)
             tiles[pl.ds(at, channels), :] = total
     for z in range(depth):
@@ -478,20 +483,20 @@
     lane = np.arange(channels * channels)
     gather = (np.arange(channels)[:, None] == lane[None] // channels).astype(bf16)
 
-    taps = 3 * (depth + 2) * 3 * channels
+    taps = 3 * 9 * channels
     in_vmem = pl.BlockSpec(memory_space=pltpu.VMEM)
     prepared = pl.pallas_call(
         functools.partial(prepare, (deep, depth, channels)),
         out_shape=(
             pltpu.VMEM((deep * 2 * channels, 27 * deep), bf16),
-            pltpu.VMEM((3 * depth * 2 * channels, taps), bf16),
+            pltpu.VMEM((3 * 2 * channels, taps), bf16),
             pltpu.VMEM(((depth + 2) * channels, 27 * deep), bf16),
-            pltpu.VMEM((3 * depth * channels, taps), bf16),
+            pltpu.VMEM((3 * channels, taps), bf16),
             pltpu.VMEM((channels, LANES), f32),
         ),
         in_specs=[in_vmem] * 14,
         out_specs=(in_vmem,) * 5,
-        scratch_shapes=[pltpu.VMEM((3 * depth * 2 * channels, taps), f32)],
+        scratch_shapes=[pltpu.VMEM((3 * 2 * channels, taps), f32)],
         compiler_params=pltpu.CompilerParams(vmem_limit_bytes=16 * 1024 * 1024),
     )
     weights = (
@@ -528,7 +533,7 @@
             pltpu.VMEM((deep, span), f32),
             pltpu.VMEM(((deep + 2) * 3 * channels, narrow), bf16),
             pltpu.VMEM(((deep + 2) * 3 * channels, narrow), bf16),
-            pltpu.VMEM((2, 3 * depth * 2 * channels, narrow + 2 * margin), f32),
+            pltpu.VMEM((deep, 3 * 2 * channels, narrow + 2 * margin), f32),
             pltpu.VMEM((depth * height * channels, width), f32),
         ],
         compiler_params=pltpu.CompilerParams(vmem_limit_bytes=36 * 1024 * 1024),

time: 26.7 us -> 25.1 us (0.940)
  Pallas kernels: 12 us -> 10.4 us
    pallas_call x1, Pallas kernels: 9.63 us -> 8.16 us  [local_body(): pl.pallas_call(functools.partial(kernel, (deep, depth, channels, pitch, h...]
where the time goes in v6:
time: 25.1 us; the launch traced here: 24.7 us
  Pallas kernels  10.4 us (41%)
  starting transfers between devices  8.81 us (35%)
  waiting for transfers between devices  4.17 us (17%)
  between operations  0.71 us (3%)
  local copies, waits for them, and re-layouts  0.3 us (1%)
  other arithmetic  0.26 us (1%)
    pallas_call x1, Pallas kernels, local_body(): pl.pallas_call(functools.partial(kernel, (deep, depth, channels, pitch, h...  8.16 us
    ppermute x2, starting transfers between devices, gathered(): other = lax.ppermute(block, 'gz', pairs)  4.57 us
    ppermute x2, starting transfers between devices, swapped(): return lax.ppermute(value, axis, [(0, 1), (1, 0)])  4.24 us
    ppermute x2, waiting for transfers between devices, swapped(): return lax.ppermute(value, axis, [(0, 1), (1, 0)])  2.47 us
    pallas_call x1, Pallas kernels, local_body(): flat, laid_out = gathered(noisy, prepared(*given))  2.29 us
    ppermute x2, waiting for transfers between devices, gathered(): other = lax.ppermute(block, 'gz', pairs)  1.71 us
  transfers between devices with their start and end apart: 4, of which 3 were waited for; matrix products, arithmetic and copies ran while one was open for 0% of the time, Pallas kernels for 9%

profile of v6, /device:TPU:1, one launch (start us, length us, event | category | flops | bytes accessed | tf_op | source)
XLA Modules:
  0.0 24.7 jit_solution(8770365156161625004)
XLA Ops:
  0.6 2.2 %collective-permute-start = (f32[4,8,128]{2,1,0:T(8,128)}, f32[4,8,128]{2,1,0:T(8,128)S(1)}, u32[]{:S(2)}, u32[]{:S(2)}) collective-permute-start(f32[4,8,128]{2,1,0:T(8,128)} %param.15), channel_id=1, source_target_pairs={{0,4},{4,0},{8,12},{12,8},{1,5},{5,1},{9,13},{13,9},{2,6},{6,2},{1... | collective-permute-start | bytes 49160 | tf_op jit(solution)/shard_map/ppermute | solution.py:134
  2.8 0.0 copy-start
  2.8 2.3 %shard_map.158 = (bf16[512,432]{1,0:T(8,128)(2,1)S(1)}, bf16[96,432]{1,0:T(8,128)(2,1)S(1)}, bf16[96,432]{1,0:T(8,128)(2,1)S(1)}, bf16[48,432]{1,0:T(8,128)(2,1)S(1)}, f32[16,128]{1,0:T(8,128)S(1)}) custom-call(f32[27,1,32]{2,1,0:T(1,128)} %bitcast.13, f32[1,16]{1,0:T(1,128)} %bitcast.14, f32[432,32]{1,0:T(8,128)} %bitcast.11, f32[1,16]{1,0:T(1,128)} %bitcast.15, ...), custom_call_target="tpu_custom_call" | custom-call | tf_op jit(solution)/shard_map/pallas_call | solution.py:516
  5.1 0.0 collective-permute-done
  5.1 0.0 copy-done
  5.2 2.4 %collective-permute-start.1 = (f32[8,8,128]{2,1,0:T(8,128)S(1)}, f32[8,8,128]{2,1,0:T(8,128)S(1)}, u32[]{:S(2)}, u32[]{:S(2)}) collective-permute-start(f32[8,8,128]{2,1,0:T(8,128)S(1)} %maximum_select_fusion.2), channel_id=1, source_target_pairs={{0,8},{4,12},{8,0},{12,4},{1,9},{5,13},{9,1},{13,5},{2,10},{6,14},... | collective-permute-start | bytes 98312 | tf_op jit(solution)/shard_map/ppermute | solution.py:134
  7.5 1.7 %collective-permute-done.1 = f32[8,8,128]{2,1,0:T(8,128)S(1)} collective-permute-done((f32[8,8,128]{2,1,0:T(8,128)S(1)}, f32[8,8,128]{2,1,0:T(8,128)S(1)}, u32[]{:S(2)}, u32[]{:S(2)}) %collective-permute-start.1) | collective-permute-done | bytes 32800 | tf_op jit(solution)/shard_map/ppermute | solution.py:134
  9.3 1.3 %collective-permute-start.2 = (f32[16,4,128]{2,1,0:T(4,128)S(1)}, f32[16,4,128]{2,1,0:T(4,128)S(1)}, u32[]{:S(2)}, u32[]{:S(2)}) collective-permute-start(f32[16,4,128]{2,1,0:T(4,128)S(1)} %rev.9), channel_id=1, source_target_pairs={{0,2},{2,0},{1,3},{3,1},{4,6},{6,4},{5,7},{7,5},{8,10},{10,8},{9,1... | collective-permute-start | bytes 98312 | tf_op jit(solution)/shard_map/ppermute | solution.py:125
  10.6 1.6 %collective-permute-done.2 = f32[16,4,128]{2,1,0:T(4,128)S(1)} collective-permute-done((f32[16,4,128]{2,1,0:T(4,128)S(1)}, f32[16,4,128]{2,1,0:T(4,128)S(1)}, u32[]{:S(2)}, u32[]{:S(2)}) %collective-permute-start.2) | collective-permute-done | bytes 32800 | tf_op jit(solution)/shard_map/ppermute | solution.py:125
  12.2 0.1 fusion
  12.3 3.0 %collective-permute-start.3 = (f32[16,12,4]{2,1,0:T(8,128)S(1)}, f32[16,12,4]{2,1,0:T(8,128)S(1)}, u32[]{:S(2)}, u32[]{:S(2)}) collective-permute-start(f32[16,12,4]{2,1,0:T(8,128)S(1)} %fusion), channel_id=1, source_target_pairs={{0,1},{1,0},{2,3},{3,2},{4,5},{5,4},{6,7},{7,6},{8,9},{9,8},{10,11... | collective-permute-start | bytes 9224 | tf_op jit(solution)/shard_map/ppermute | solution.py:125
  15.2 0.1 pad.12.clone
  15.3 0.9 %collective-permute-done.3 = f32[16,12,4]{2,1,0:T(8,128)S(1)} collective-permute-done((f32[16,12,4]{2,1,0:T(8,128)S(1)}, f32[16,12,4]{2,1,0:T(8,128)S(1)}, u32[]{:S(2)}, u32[]{:S(2)}) %collective-permute-start.3) | collective-permute-done | bytes 3104 | tf_op jit(solution)/shard_map/ppermute | solution.py:125
  16.2 0.1 maximum_select_fusion
  16.4 0.1 select_n.71
  16.5 8.2 %shard_map.159 = (f32[4,8,128]{2,1,0:T(8,128)}, f32[16,4,8,128]{3,2,1,0:T(8,128)}) custom-call(f32[16,1664]{1,0:T(8,128)S(1)} %pad.4.noisy_ref, bf16[512,432]{1,0:T(8,128)(2,1)S(1)} %get-tuple-element.19.w1_ref, bf16[96,432]{1,0:T(8,128)(2,1)S(1)} %get-tuple-element.20.w2_ref, bf16[96,432]{1,0:T(8,128)(2,1)S(1)} %get-tuple-element.21.w3_ref, ...), custom_call_target="tpu_custom_call" | custom-call | tf_op jit(solution)/shard_map/pallas_call | solution.py:521
  (7 shorter events, 0.1 us)
Async XLA Ops:
  0.6 4.5 %collective-permute-start = (f32[4,8,128]{2,1,0:T(8,128)}, f32[4,8,128]{2,1,0:T(8,128)S(1)}, u32[]{:S(2)}, u32[]{:S(2)}) collective-permute-start(f32[4,8,128]{2,1,0:T(8,128)} %param.15), channel_id=1, source_target_pairs={{0,4},{4,0},{8,12},{12,8},{1,5},{5,1},{9,13},{13,9},{2,6},{6,2},{1... | collective-permute-start | bytes 49160 | tf_op jit(solution)/shard_map/ppermute | solution.py:134
  2.8 2.3 %copy-start = (f32[4,8,128]{2,1,0:T(8,128)S(1)}, f32[4,8,128]{2,1,0:T(8,128)}, u32[]{:S(2)}) copy-start(f32[4,8,128]{2,1,0:T(8,128)} %param.15) | copy-start | bytes 49156
  5.2 4.1 %collective-permute-start.1 = (f32[8,8,128]{2,1,0:T(8,128)S(1)}, f32[8,8,128]{2,1,0:T(8,128)S(1)}, u32[]{:S(2)}, u32[]{:S(2)}) collective-permute-start(f32[8,8,128]{2,1,0:T(8,128)S(1)} %maximum_select_fusion.2), channel_id=1, source_target_pairs={{0,8},{4,12},{8,0},{12,4},{1,9},{5,13},{9,1},{13,5},{2,10},{6,14},... | collective-permute-start | bytes 98312 | tf_op jit(solution)/shard_map/ppermute | solution.py:134
  9.3 2.8 %collective-permute-start.2 = (f32[16,4,128]{2,1,0:T(4,128)S(1)}, f32[16,4,128]{2,1,0:T(4,128)S(1)}, u32[]{:S(2)}, u32[]{:S(2)}) collective-permute-start(f32[16,4,128]{2,1,0:T(4,128)S(1)} %rev.9), channel_id=1, source_target_pairs={{0,2},{2,0},{1,3},{3,1},{4,6},{6,4},{5,7},{7,5},{8,10},{10,8},{9,1... | collective-permute-start | bytes 98312 | tf_op jit(solution)/shard_map/ppermute | solution.py:125
  12.3 4.0 %collective-permute-start.3 = (f32[16,12,4]{2,1,0:T(8,128)S(1)}, f32[16,12,4]{2,1,0:T(8,128)S(1)}, u32[]{:S(2)}, u32[]{:S(2)}) collective-permute-start(f32[16,12,4]{2,1,0:T(8,128)S(1)} %fusion), channel_id=1, source_target_pairs={{0,1},{1,0},{2,3},{3,2},{4,5},{5,4},{6,7},{7,6},{8,9},{9,8},{10,11... | collective-permute-start | bytes 9224 | tf_op jit(solution)/shard_map/ppermute | solution.py:125

commit v7 on v6

--- a/solution.py
+++ b/solution.py
@@ -147,14 +147,12 @@
     low = lax.slice_in_dim(block, 0, HALO, axis=2)
     high = lax.slice_in_dim(block, size - HALO, size, axis=2)
     other = swapped(jnp.where(first, high, low), "gx")
-    blank = jnp.zeros(block.shape[:2] + (1,), block.dtype)
-    window = jnp.where(
+    strip = jnp.where(
         first,
-        jnp.concatenate([block, other, blank], 2),
-        jnp.concatenate([other, block, blank], 2),
-    )
-    window = window.reshape(window.shape[0], -1)
-    return jnp.pad(window, ((0, 0), (0, -window.shape[1] % LANES))), laid_out
+        jnp.concatenate([block[:, :, -2 * HALO :], other], 2),
+        jnp.concatenate([other, block[:, :, : 2 * HALO]], 2),
+    )
+    return block, strip, laid_out
 
 
 def prepare(
@@ -251,7 +249,8 @@
 
 def kernel(
     geometry,
-    noisy_ref,
+    block_ref,
+    strip_ref,
     w1_ref,
     w2_ref,
     w3_ref,
@@ -259,63 +258,70 @@
     columns_ref,
     den_ref,
     seg_ref,
-    stage,
+    lines,
     thin,
     pre,
-    rows,
+    partial,
     wide_hi,
     wide_lo,
     sums,
     tiles,
 ):
-    deep, depth, channels, pitch, high, span, margin = geometry
-    f32 = jnp.float32
-    lanes = lax.broadcasted_iota(jnp.int32, (1, span), 1)
-    blank = lanes >= high * pitch
-    for r in range(high):
-        blank = blank | (lanes == (r + 1) * pitch - 1)
-    mask = jnp.where(blank, 0.0, 1.0).astype(jnp.float32)
+    deep, depth, channels, pitch, high = geometry
+    f32, bf16 = jnp.float32, jnp.bfloat16
+    height, width = den_ref.shape[1:]
     place = lax.axis_index("gz")
+    turned = lax.axis_index("gy") == 1
     bias1, bias2, head, bias3, bias4 = (columns_ref[:, i : i + 1] for i in range(5))
-    shifts = [(b - 1) * pitch + (c - 1) for b in range(3) for c in range(3)]
-    first_span, second_span, third_span = (
-        -(-(high - i) * pitch // LANES) * LANES for i in range(1, 4)
-    )
-    height, width = den_ref.shape[1:]
-
+    lane = lax.broadcasted_iota(jnp.int32, (1, LANES), 1)
+    first_rows, second_rows, third_rows = high - 1, high - 2, high - 3
     edge = 3 * channels
 
-    def put(field, slot):
-        for part, half in enumerate(split(field)):
-            stage[2 * slot + part, :, pl.ds(margin, field.shape[1])] = half
-
-    def shifted(part, shift, length, slot=0):
-        return stage[2 * slot + part, :, pl.ds(margin + shift, length)]
-
-    def thin_columns(field, length):
-        put(field, 0)
-        for t, s in enumerate(shifts):
-            h = shifted(0, s, length)
-            thin[t * deep : (t + 1) * deep, :length] = h
-            thin[(9 + t) * deep : (10 + t) * deep, :length] = h
-            thin[(18 + t) * deep : (19 + t) * deep, :length] = shifted(1, s, length)
+    def split_strip(field):
+        return field[:, :LANES], field[:, LANES:]
+
+    def clean(field):
+        strip, main = split_strip(field)
+        return jnp.concatenate([jnp.where(lane < first_rows * pitch, strip, 0.0), main], 1)
+
+    def beside(field, c):
+        if c == 1:
+            return field
+        shift, end = (1, 0) if c == 0 else (LANES - 1, LANES - 1)
+        out = [pltpu.roll(field[:, :LANES], shift, 1)]
+        for at in range(LANES, field.shape[1], LANES):
+            moved = pltpu.roll(field[:, at : at + LANES], shift, 1)
+            out.append(jnp.where(lane == end, 0.0, moved))
+        return jnp.concatenate(out, 1)
+
+    def strip_row(strip, b):
+        if b == 1:
+            return strip
+        moved = pltpu.roll(strip, pitch if b == 0 else LANES - pitch, 1)
+        return jnp.where(lane < pitch, 0.0, moved) if b == 0 else moved
+
+    def thin_columns(fields, rows):
+        for c, field in enumerate(fields):
+            strip, main = split_strip(field)
+            for i, half in enumerate(split(main)):
+                lines[3 * i + c, :, pl.ds(LANES, main.shape[1])] = half
+            for b in range(3):
+                t = 3 * b + c
+                halves = split(strip_row(strip, b))
+                for k, i in enumerate((0, 0, 1)):
+                    at = slice((k * 9 + t) * deep, (k * 9 + t + 1) * deep)
+                    thin[at, :LANES] = halves[i]
+                    thin[at, LANES : (rows + 1) * LANES] = lines[
+                        3 * i + c, :, b * LANES : (b + rows) * LANES
+                    ]
 
     def wide_columns(z, field):
-        length, slot = field.shape[1], z % (depth + 2)
-        put(field, slot)
+        length = field.shape[1]
         for c in range(3):
             at = (z * 3 + c) * channels
-            wide_hi[at : at + channels, :length] = shifted(0, c - 1, length, slot)
-            wide_lo[at : at + channels, :length] = shifted(1, c - 1, length, slot)
-
-    def own_columns(z, offset):
-        for c in range(3):
-            at = (z * 3 + c) * channels
-            for r in range(height + 1):
-                lanes = slice(r * width, (r + 1) * width)
-                shift = r * pitch + offset + c - 1
-                wide_hi[at : at + channels, lanes] = shifted(0, shift, width, z)
-                wide_lo[at : at + channels, lanes] = shifted(1, shift, width, z)
+            h, l = split(beside(field, c))
+            wide_hi[at : at + channels, :length] = h
+            wide_lo[at : at + channels, :length] = l
 
     def chunks(length):
         return [(i, min(2 * LANES, length - i)) for i in range(0, length, 2 * LANES)]
@@ -325,25 +331,51 @@
         taps = slice(z * edge, (z + 3) * edge)
         h = wide_hi[taps, at : at + length]
         l = wide_lo[taps, at : at + length]
-        sums[z, : w_ref.shape[0], pl.ds(margin + at, length)] = jnp.dot(
-            w_ref[...], jnp.concatenate([h, l, h], 0), preferred_element_type=f32
-        )
+        out = jnp.dot(w_ref[...], jnp.concatenate([h, l, h], 0), preferred_element_type=f32)
+        n = w_ref.shape[0]
+        if at == 0:
+            sums[z, :n, :LANES] = out[:, :LANES]
+            sums[z, :n, 2 * LANES : LANES + length] = out[:, LANES:]
+        else:
+            sums[z, :n, LANES + at : LANES + at + length] = out
+
+    def layer(z, at, step, rows):
+        strip = main = 0.0
+        for b in range(3):
+            k = slice(at + b * step, at + b * step + channels)
+            strip = strip + strip_row(sums[z, k, :LANES], b)
+            main = main + sums[z, k, (b + 1) * LANES : (b + 1 + rows) * LANES]
+        return jnp.concatenate([strip, main], 1)
 
     def gate(cand, up, hidden):
         fresh = 1.0 / (1.0 + jnp.exp(-up))
         return hidden + fresh * (jnp.tanh(cand) - hidden)
 
-    stage[...] = jnp.zeros_like(stage)
-    before = jnp.zeros((deep, 2 * channels, margin), f32)
-    sums[:, : 2 * channels, :margin] = before
-    sums[:, 4 * channels :, margin + first_span :] = before
-    zeros = jnp.zeros((edge, wide_hi.shape[1]), jnp.bfloat16)
+    lines[:, :, :LANES] = jnp.zeros((6, deep, LANES), bf16)
+    sums[:, :, LANES : 2 * LANES] = jnp.zeros((deep, sums.shape[1], LANES), f32)
+    zeros = jnp.zeros((edge, wide_hi.shape[1]), bf16)
     for wide in (wide_hi, wide_lo):
         wide[:edge, :] = zeros
         wide[(deep + 1) * edge :, :] = zeros
 
-    noisy = noisy_ref[...]
-    thin_columns(noisy, first_span)
+    strips = [jnp.zeros((deep, LANES), f32)] * 3
+    for r in range(high):
+        columns = strip_ref[:, r, :]
+        columns = jnp.concatenate(
+            [columns, jnp.zeros((deep, LANES - columns.shape[1]), f32)], 1
+        )
+        here = (lane >= r * pitch) & (lane < (r + 1) * pitch)
+        for c in range(3):
+            moved = pltpu.roll(columns, (r * pitch - c) % LANES, 1)
+            strips[c] = jnp.where(here, moved, strips[c])
+    noisy = jnp.concatenate([strips[1]] + [block_ref[:, r, :] for r in range(high)], 1)
+    thin_columns(
+        [jnp.concatenate([strips[c], split_strip(beside(noisy, c))[1]], 1) for c in range(3)],
+        first_rows,
+    )
+    first_span, second_span, third_span = (
+        (n + 1) * LANES for n in (first_rows, second_rows, third_rows)
+    )
     todo = chunks(first_span)
     part = depth * 2 * channels
 
@@ -366,7 +398,7 @@
             pre[at + channels : at + 2 * channels, :] + bias1,
             hidden,
         )
-        wide_columns(z + 1, hidden * mask[:, :first_span])
+        wide_columns(z + 1, clean(hidden))
         if z // depth + 1 < deep // depth:
             for chunk in todo[z % depth :: depth]:
                 thin_block(z // depth + 1, chunk)
@@ -375,69 +407,73 @@
         for _ in range(min(PACE, len(waiting))):
             convolve(w2_ref, *waiting.pop(0))
 
-    def layer(z, at):
-        return sum(
-            sums[
-                z,
-                at + b * 2 * channels : at + (b * 2 + 1) * channels,
-                pl.ds(margin + (b - 1) * pitch, second_span),
-            ]
-            for b in range(3)
-        )
-
-    later = [(z, chunk) for z in range(deep - 1, AHEAD - 1, -1) for chunk in todo] + waiting
+    later = waiting + [(z, chunk) for z in range(deep - 1, AHEAD - 1, -1) for chunk in todo]
     for _ in range(min(2 * len(todo), len(later))):
         convolve(w2_ref, *later.pop(0))
     hidden = jnp.zeros((channels, second_span), f32)
     for z in range(deep - 1, -1, -1):
         for _ in range(min(len(todo), len(later))):
             convolve(w2_ref, *later.pop(0))
-        hidden = gate(layer(z, 0), layer(z, channels) + bias2, hidden)
-        rows[z : z + 1, :second_span] = jnp.sum(hidden * head, axis=0, keepdims=True)
-
-    finished = (noisy[:, :second_span] + rows[:, :second_span]) * mask[:, :second_span]
-    rows[:, :second_span] = finished
-    thin_columns(finished, third_span)
+        hidden = gate(
+            layer(z, 0, 2 * channels, second_rows),
+            layer(z, channels, 2 * channels, second_rows) + bias2,
+            hidden,
+        )
+        scaled = hidden * head
+        while scaled.shape[0] > SUBLANES:
+            half = scaled.shape[0] // 2
+            scaled = scaled[:half] + scaled[half:]
+        partial[z * SUBLANES : (z + 1) * SUBLANES, :] = scaled
+
+    shape = (deep, deep * SUBLANES)
+    row, column = (lax.broadcasted_iota(jnp.int32, shape, i) for i in range(2))
+    own = (column >= row * SUBLANES) & (column < (row + 1) * SUBLANES)
+    adder = jnp.where(own, 1.0, 0.0).astype(bf16)
+    change = sum(
+        jnp.dot(adder, half, preferred_element_type=f32) for half in split(partial[...])
+    )
+    finished = noisy[:, :second_span] + change
+    thin_columns([beside(finished, c) for c in range(3)], third_rows)
     grown = jnp.dot(w3_ref[...], thin[:, :third_span], preferred_element_type=f32)
     for i in range(depth + 2):
         z = place * depth + i - 1
         real = jnp.where((z >= 0) & (z < deep), 1.0, 0.0)
         features = jnp.maximum(grown[i * channels : (i + 1) * channels] + bias3, 0.0)
-        put(features * (mask[:, :third_span] * real), i)
-
-    turned = lax.axis_index("gy") == 1
+        wide_columns(i, clean(features * real))
+
+    right = lax.axis_index("gx") == 0
+    beyond = lane - jnp.where(right, width - HALO, 0)
+    border = (beyond >= 0) & (beyond < HALO)
+
+    def mended(strip, main, r):
+        at = r * pitch + HALO - 1
+        shift = jnp.where(right, (width - HALO - at) % LANES, (LANES - at) % LANES)
+        return jnp.where(border, pltpu.roll(strip, shift, 1), main)
 
     def at_row(r):
         return jnp.where(turned, height - 1 - r, r)
 
-    for x in range(2):
-
-        @pl.when(lax.axis_index("gx") == x)
-        def _():
-            for i in range(depth + 2):
-                own_columns(i, x * HALO)
-            for r in range(height):
-                lanes = pl.ds(r * pitch + x * HALO, width)
-                mine = rows[:depth, lanes]
-                for b in range(1, deep // depth):
-                    mine = jnp.where(place == b, rows[b * depth : (b + 1) * depth, lanes], mine)
-                at = pl.multiple_of(at_row(r) * SUBLANES, SUBLANES)
-                tiles[pl.ds(at, depth), :] = mine
-
+    mine = finished[:depth]
+    for b in range(1, deep // depth):
+        mine = jnp.where(place == b, finished[b * depth : (b + 1) * depth], mine)
+    mine = jnp.concatenate([mine, jnp.zeros((SUBLANES - depth, second_span), f32)], 0)
+    for r in range(height):
+        at = pl.multiple_of(at_row(r) * SUBLANES, SUBLANES)
+        tiles[pl.ds(at, SUBLANES), :] = mended(
+            mine[:, :LANES], mine[:, (r + 1) * LANES : (r + 2) * LANES], r
+        )
     for z in range(depth):
         den_ref[z] = tiles[pl.ds(z, height, stride=SUBLANES), :]
     for z in range(depth):
-        for chunk in chunks((height + 1) * width):
+        for chunk in chunks(third_span):
             convolve(w4_ref, z, chunk)
     for z in range(depth):
+        total = layer(z, 0, channels, height) + bias4
         for r in range(height):
-            total = bias4
-            for b in range(3):
-                if r + b > 0:
-                    lanes = pl.ds(margin + (r + b - 1) * width, width)
-                    total = total + sums[z, b * channels : (b + 1) * channels, lanes]
             at = pl.multiple_of((z * height + at_row(r)) * channels, channels)
-            tiles[pl.ds(at, channels), :] = total
+            tiles[pl.ds(at, channels), :] = mended(
+                total[:, :LANES], total[:, (r + 1) * LANES : (r + 2) * LANES], r
+            )
     for z in range(depth):
         for o in range(channels):
             seg_ref[o, z] = tiles[pl.ds(z * height * channels + o, height, stride=channels), :]
@@ -460,10 +496,8 @@
     place = lax.axis_index("gz")
     deep = count * depth
     channels = first_bias.shape[0]
-    high, pitch = height + HALO, width + HALO + 1
-    span = -(-high * pitch // LANES) * LANES
-    margin = -(-(pitch + 1) // LANES) * LANES
-    narrow = -(-(high - 1) * pitch // LANES) * LANES
+    high, pitch = height + HALO, 3 * HALO - 2
+    narrow = high * LANES
 
     f32, bf16 = jnp.float32, jnp.bfloat16
     lane = np.arange(27 * deep)
@@ -513,27 +547,27 @@
     tables = tuple(jnp.asarray(v) for v in (thin_lane, thin_sub, wide_lane, keep, gather))
 
     given = [pltpu.with_memory_space_constraint(v, pltpu.HBM) for v in weights + tables]
-    flat, laid_out = gathered(noisy, prepared(*given))
+    block, strip, laid_out = gathered(noisy, prepared(*given))
     operands = [
         pltpu.with_memory_space_constraint(v, pltpu.VMEM)
-        for v in (flat, *laid_out)
+        for v in (block, strip, *laid_out)
     ]
     return pl.pallas_call(
-        functools.partial(kernel, (deep, depth, channels, pitch, high, span, margin)),
+        functools.partial(kernel, (deep, depth, channels, pitch, high)),
         out_shape=(
             jax.ShapeDtypeStruct((depth, height, width), f32),
             jax.ShapeDtypeStruct((channels, depth, height, width), f32),
         ),
-        in_specs=[in_vmem] * 6,
+        in_specs=[in_vmem] * 7,
         out_specs=(in_vmem,) * 2,
         scratch_shapes=[
-            pltpu.VMEM((2 * (depth + 2), channels, span + 2 * margin), bf16),
-            pltpu.VMEM((27 * deep, span), bf16),
+            pltpu.VMEM((6, deep, (high + 1) * LANES), bf16),
+            pltpu.VMEM((27 * deep, narrow), bf16),
             pltpu.VMEM((deep * 2 * channels, narrow), f32),
-            pltpu.VMEM((deep, span), f32),
+            pltpu.VMEM((deep * SUBLANES, narrow - LANES), f32),
             pltpu.VMEM(((deep + 2) * 3 * channels, narrow), bf16),
             pltpu.VMEM(((deep + 2) * 3 * channels, narrow), bf16),
-            pltpu.VMEM((deep, 3 * 2 * channels, narrow + 2 * margin), f32),
+            pltpu.VMEM((deep, 3 * 2 * channels, narrow + LANES), f32),
             pltpu.VMEM((depth * height * channels, width), f32),
         ],
         compiler_params=pltpu.CompilerParams(vmem_limit_bytes=36 * 1024 * 1024),

time: 25.1 us -> 23.9 us (0.952)
  Pallas kernels: 10.4 us -> 9.35 us
    pallas_call x1, Pallas kernels: 8.16 us -> 7.07 us  [local_body(): pl.pallas_call(functools.partial(kernel, (deep, depth, channels, pitch, h...]
  transfers between devices with their start and end apart: 4 -> 4, of which waited for: 3 -> 3; matrix products, arithmetic and copies ran while one was open for 0% -> 0% of each run, Pallas kernels for 9% -> 10%
where the time goes in v7:
time: 23.9 us; the launch traced here: 23.4 us
  Pallas kernels  9.35 us (39%)
  starting transfers between devices  8.81 us (37%)
  waiting for transfers between devices  4.13 us (17%)
  between operations  0.72 us (3%)
  other arithmetic  0.36 us (2%)
    pallas_call x1, Pallas kernels, local_body(): pl.pallas_call(functools.partial(kernel, (deep, depth, channels, pitch, h...  7.07 us
    ppermute x2, starting transfers between devices, gathered(): other = lax.ppermute(block, 'gz', pairs)  4.57 us
    ppermute x2, starting transfers between devices, swapped(): return lax.ppermute(value, axis, [(0, 1), (1, 0)])  4.24 us
    ppermute x2, waiting for transfers between devices, swapped(): return lax.ppermute(value, axis, [(0, 1), (1, 0)])  2.42 us
    pallas_call x1, Pallas kernels, local_body(): block, strip, laid_out = gathered(noisy, prepared(*given))  2.29 us
    ppermute x2, waiting for transfers between devices, gathered(): other = lax.ppermute(block, 'gz', pairs)  1.71 us
  transfers between devices with their start and end apart: 4, of which 3 were waited for; matrix products, arithmetic and copies ran while one was open for 0% of the time, Pallas kernels for 10%

profile of v7, /device:TPU:1, one launch (start us, length us, event | category | flops | bytes accessed | tf_op | source)
XLA Modules:
  0.0 23.4 jit_solution(12883315407904325810)
XLA Ops:
  0.6 2.2 %collective-permute-start = (f32[4,8,128]{2,1,0:T(8,128)}, f32[4,8,128]{2,1,0:T(8,128)S(1)}, u32[]{:S(2)}, u32[]{:S(2)}) collective-permute-start(f32[4,8,128]{2,1,0:T(8,128)} %param.15), channel_id=1, source_target_pairs={{0,4},{4,0},{8,12},{12,8},{1,5},{5,1},{9,13},{13,9},{2,6},{6,2},{1... | collective-permute-start | bytes 49160 | tf_op jit(solution)/shard_map/ppermute | solution.py:134
  2.8 0.0 copy-start
  2.8 2.3 %shard_map.158 = (bf16[512,432]{1,0:T(8,128)(2,1)S(1)}, bf16[96,432]{1,0:T(8,128)(2,1)S(1)}, bf16[96,432]{1,0:T(8,128)(2,1)S(1)}, bf16[48,432]{1,0:T(8,128)(2,1)S(1)}, f32[16,128]{1,0:T(8,128)S(1)}) custom-call(f32[27,1,32]{2,1,0:T(1,128)} %bitcast.12, f32[1,16]{1,0:T(1,128)} %bitcast.13, f32[432,32]{1,0:T(8,128)} %bitcast.10, f32[1,16]{1,0:T(1,128)} %bitcast.14, ...), custom_call_target="tpu_custom_call" | custom-call | tf_op jit(solution)/shard_map/pallas_call | solution.py:550
  5.1 0.0 collective-permute-done
  5.1 0.0 copy-done
  5.2 2.4 %collective-permute-start.1 = (f32[8,8,128]{2,1,0:T(8,128)S(1)}, f32[8,8,128]{2,1,0:T(8,128)S(1)}, u32[]{:S(2)}, u32[]{:S(2)}) collective-permute-start(f32[8,8,128]{2,1,0:T(8,128)S(1)} %maximum_select_fusion.2), channel_id=1, source_target_pairs={{0,8},{4,12},{8,0},{12,4},{1,9},{5,13},{9,1},{13,5},{2,10},{6,14},... | collective-permute-start | bytes 98312 | tf_op jit(solution)/shard_map/ppermute | solution.py:134
  7.5 1.7 %collective-permute-done.1 = f32[8,8,128]{2,1,0:T(8,128)S(1)} collective-permute-done((f32[8,8,128]{2,1,0:T(8,128)S(1)}, f32[8,8,128]{2,1,0:T(8,128)S(1)}, u32[]{:S(2)}, u32[]{:S(2)}) %collective-permute-start.1) | collective-permute-done | bytes 32800 | tf_op jit(solution)/shard_map/ppermute | solution.py:134
  9.3 1.3 %collective-permute-start.2 = (f32[16,4,128]{2,1,0:T(4,128)S(1)}, f32[16,4,128]{2,1,0:T(4,128)S(1)}, u32[]{:S(2)}, u32[]{:S(2)}) collective-permute-start(f32[16,4,128]{2,1,0:T(4,128)S(1)} %rev.9), channel_id=1, source_target_pairs={{0,2},{2,0},{1,3},{3,1},{4,6},{6,4},{5,7},{7,5},{8,10},{10,8},{9,1... | collective-permute-start | bytes 98312 | tf_op jit(solution)/shard_map/ppermute | solution.py:125
  10.6 1.6 %collective-permute-done.2 = f32[16,4,128]{2,1,0:T(4,128)S(1)} collective-permute-done((f32[16,4,128]{2,1,0:T(4,128)S(1)}, f32[16,4,128]{2,1,0:T(4,128)S(1)}, u32[]{:S(2)}, u32[]{:S(2)}) %collective-permute-start.2) | collective-permute-done | bytes 32800 | tf_op jit(solution)/shard_map/ppermute | solution.py:125
  12.2 0.1 fusion.2
  12.3 3.0 %collective-permute-start.3 = (f32[16,12,4]{2,1,0:T(8,128)S(1)}, f32[16,12,4]{2,1,0:T(8,128)S(1)}, u32[]{:S(2)}, u32[]{:S(2)}) collective-permute-start(f32[16,12,4]{2,1,0:T(8,128)S(1)} %fusion.2), channel_id=1, source_target_pairs={{0,1},{1,0},{2,3},{3,2},{4,5},{5,4},{6,7},{7,6},{8,9},{9,8},{10,11... | collective-permute-start | bytes 9224 | tf_op jit(solution)/shard_map/ppermute | solution.py:125
  15.2 0.1 fusion.4
  15.4 0.9 %collective-permute-done.3 = f32[16,12,4]{2,1,0:T(8,128)S(1)} collective-permute-done((f32[16,12,4]{2,1,0:T(8,128)S(1)}, f32[16,12,4]{2,1,0:T(8,128)S(1)}, u32[]{:S(2)}, u32[]{:S(2)}) %collective-permute-start.3) | collective-permute-done | bytes 3104 | tf_op jit(solution)/shard_map/ppermute | solution.py:125
  16.2 0.1 maximum_select_fusion.strip_ref
  16.4 7.1 %shard_map.159 = (f32[4,8,128]{2,1,0:T(8,128)}, f32[16,4,8,128]{3,2,1,0:T(8,128)}) custom-call(f32[16,12,128]{2,1,0:T(8,128)S(1)} %pad_maximum_fusion.block_ref, f32[16,12,12]{2,1,0:T(8,128)S(1)} %maximum_select_fusion.strip_ref, bf16[512,432]{1,0:T(8,128)(2,1)S(1)} %get-tuple-element.19.w1_ref, bf16[96,432]{1,0:T(8,128)(2,1)S(1)} %get-tuple-element.20.w2_ref, ...), custom_call_target="tpu_custom_call" | custom-call | tf_op jit(solution)/shard_map/pallas_call | solution.py:555
  (7 shorter events, 0.1 us)
Async XLA Ops:
  0.6 4.5 %collective-permute-start = (f32[4,8,128]{2,1,0:T(8,128)}, f32[4,8,128]{2,1,0:T(8,128)S(1)}, u32[]{:S(2)}, u32[]{:S(2)}) collective-permute-start(f32[4,8,128]{2,1,0:T(8,128)} %param.15), channel_id=1, source_target_pairs={{0,4},{4,0},{8,12},{12,8},{1,5},{5,1},{9,13},{13,9},{2,6},{6,2},{1... | collective-permute-start | bytes 49160 | tf_op jit(solution)/shard_map/ppermute | solution.py:134
  2.8 2.3 %copy-start = (f32[4,8,128]{2,1,0:T(8,128)S(1)}, f32[4,8,128]{2,1,0:T(8,128)}, u32[]{:S(2)}) copy-start(f32[4,8,128]{2,1,0:T(8,128)} %param.15) | copy-start | bytes 49156
  5.2 4.1 %collective-permute-start.1 = (f32[8,8,128]{2,1,0:T(8,128)S(1)}, f32[8,8,128]{2,1,0:T(8,128)S(1)}, u32[]{:S(2)}, u32[]{:S(2)}) collective-permute-start(f32[8,8,128]{2,1,0:T(8,128)S(1)} %maximum_select_fusion.2), channel_id=1, source_target_pairs={{0,8},{4,12},{8,0},{12,4},{1,9},{5,13},{9,1},{13,5},{2,10},{6,14},... | collective-permute-start | bytes 98312 | tf_op jit(solution)/shard_map/ppermute | solution.py:134
  9.3 2.8 %collective-permute-start.2 = (f32[16,4,128]{2,1,0:T(4,128)S(1)}, f32[16,4,128]{2,1,0:T(4,128)S(1)}, u32[]{:S(2)}, u32[]{:S(2)}) collective-permute-start(f32[16,4,128]{2,1,0:T(4,128)S(1)} %rev.9), channel_id=1, source_target_pairs={{0,2},{2,0},{1,3},{3,1},{4,6},{6,4},{5,7},{7,5},{8,10},{10,8},{9,1... | collective-permute-start | bytes 98312 | tf_op jit(solution)/shard_map/ppermute | solution.py:125
  12.3 4.0 %collective-permute-start.3 = (f32[16,12,4]{2,1,0:T(8,128)S(1)}, f32[16,12,4]{2,1,0:T(8,128)S(1)}, u32[]{:S(2)}, u32[]{:S(2)}) collective-permute-start(f32[16,12,4]{2,1,0:T(8,128)S(1)} %fusion.2), channel_id=1, source_target_pairs={{0,1},{1,0},{2,3},{3,2},{4,5},{5,4},{6,7},{7,6},{8,9},{9,8},{10,11... | collective-permute-start | bytes 9224 | tf_op jit(solution)/shard_map/ppermute | solution.py:125

commit v8 on v7

--- a/solution.py
+++ b/solution.py
@@ -188,21 +188,22 @@
 
     tap_lane, z_lane, part_lane = (thin_lane_ref[i : i + 1, :] for i in range(3))
     a_sub, tap_ahead, tap_turned = (thin_sub_ref[:, i : i + 1] for i in range(3))
-    same = tap_lane == jnp.where(turned, tap_turned, tap_ahead)
-    crossed = part_lane == 1
-    reach = z_lane - a_sub + 1
-
-    def thin_rows(halves, z):
-        hit = same & (reach == z)
-        high = jnp.where(hit & ~crossed, 1.0, 0.0).astype(bf16)
-        low = jnp.where(hit & crossed, 1.0, 0.0).astype(bf16)
-        return (dot(halves[0], high) + dot(halves[1], low)).astype(bf16)
-
-    first = split(w1_ref[:, 0, :].T)
+    same = tap_lane + 9 * (part_lane & 1) == jnp.where(turned, tap_turned, tap_ahead)
+    reach = jnp.where(same, z_lane - a_sub + 1, -2 * deep)
+
+    def paired(weight):
+        blank = jnp.zeros((weight.shape[0], thin_sub_ref.shape[0] // 2 - weight.shape[1]), f32)
+        high, low = (half.astype(f32) for half in split(weight))
+        return jnp.concatenate([high, blank, low, blank], 1).astype(bf16)
+
+    def thin_rows(pair, z):
+        return dot(pair, jnp.where(reach == z, 1.0, 0.0).astype(bf16)).astype(bf16)
+
+    first = paired(w1_ref[:, 0, :].T)
     out = 2 * channels
     for z in range(deep):
         w1_out[z * out : (z + 1) * out, :] = thin_rows(first, z)
-    grow = split(w3_ref[:, 0, :])
+    grow = paired(w3_ref[:, 0, :])
     for i in range(depth + 2):
         z = place + i - 1
         inside = (z >= 0) & (z < deep)
@@ -233,9 +234,9 @@
     spread = taps == jnp.where(turned, wide_lane_ref[1:2, :], wide_lane_ref[0:1, :])
     spread = jnp.where(spread, 1.0, 0.0).astype(bf16)
     keep = jnp.concatenate([keep_ref[...]] * channels, 0)
+    both = dot(jnp.concatenate(split(w4_ref[...]), 0), spread)
     flats = [
-        dot(gather_ref[...], (dot(half, spread) * keep).astype(bf16))
-        for half in split(w4_ref[...])
+        dot(gather_ref[...], (half * keep).astype(bf16)) for half in jnp.split(both, 2, 0)
     ]
     lay([[f[:, b * 3 * step : (b + 1) * 3 * step] for f in flats] for b in range(3)], w4_out)
 
@@ -284,14 +285,14 @@
         strip, main = split_strip(field)
         return jnp.concatenate([jnp.where(lane < first_rows * pitch, strip, 0.0), main], 1)
 
-    def beside(field, c):
+    def beside(field, c, first=0):
         if c == 1:
             return field
         shift, end = (1, 0) if c == 0 else (LANES - 1, LANES - 1)
-        out = [pltpu.roll(field[:, :LANES], shift, 1)]
-        for at in range(LANES, field.shape[1], LANES):
+        out = []
+        for at in range(0, field.shape[1], LANES):
             moved = pltpu.roll(field[:, at : at + LANES], shift, 1)
-            out.append(jnp.where(lane == end, 0.0, moved))
+            out.append(jnp.where(lane == end, 0.0, moved) if first + at > 0 else moved)
         return jnp.concatenate(out, 1)
 
     def strip_row(strip, b):
@@ -315,13 +316,13 @@
                         3 * i + c, :, b * LANES : (b + rows) * LANES
                     ]
 
-    def wide_columns(z, field):
-        length = field.shape[1]
+    def wide_columns(z, field, first=0):
+        lanes = slice(first, first + field.shape[1])
         for c in range(3):
             at = (z * 3 + c) * channels
-            h, l = split(beside(field, c))
-            wide_hi[at : at + channels, :length] = h
-            wide_lo[at : at + channels, :length] = l
+            h, l = split(beside(field, c, first))
+            wide_hi[at : at + channels, lanes] = h
+            wide_lo[at : at + channels, lanes] = l
 
     def chunks(length):
         return [(i, min(2 * LANES, length - i)) for i in range(0, length, 2 * LANES)]
@@ -434,12 +435,29 @@
     )
     finished = noisy[:, :second_span] + change
     thin_columns([beside(finished, c) for c in range(3)], third_rows)
-    grown = jnp.dot(w3_ref[...], thin[:, :third_span], preferred_element_type=f32)
-    for i in range(depth + 2):
-        z = place * depth + i - 1
-        real = jnp.where((z >= 0) & (z < deep), 1.0, 0.0)
-        features = jnp.maximum(grown[i * channels : (i + 1) * channels] + bias3, 0.0)
-        wide_columns(i, clean(features * real))
+
+    def grow(chunk):
+        at, length = chunk
+        return jnp.dot(w3_ref[...], thin[:, at : at + length], preferred_element_type=f32)
+
+    def spread(chunk, grown):
+        for i in range(depth + 2):
+            z = place * depth + i - 1
+            real = jnp.where((z >= 0) & (z < deep), 1.0, 0.0)
+            features = jnp.maximum(grown[i * channels : (i + 1) * channels] + bias3, 0.0)
+            features = features * real
+            wide_columns(i, features if chunk[0] else clean(features), chunk[0])
+
+    todo = chunks(third_span)
+    grown = {}
+    for k in range(len(todo) + 2):
+        if k < len(todo):
+            grown[k] = grow(todo[k])
+        if 0 <= k - 1 < len(todo):
+            spread(todo[k - 1], grown[k - 1])
+        if k >= 2:
+            for z in range(depth):
+                convolve(w4_ref, z, todo[k - 2])
 
     right = lax.axis_index("gx") == 0
     beyond = lane - jnp.where(right, width - HALO, 0)
@@ -464,9 +482,6 @@
         )
     for z in range(depth):
         den_ref[z] = tiles[pl.ds(z, height, stride=SUBLANES), :]
-    for z in range(depth):
-        for chunk in chunks(third_span):
-            convolve(w4_ref, z, chunk)
     for z in range(depth):
         total = layer(z, 0, channels, height) + bias4
         for r in range(height):
@@ -505,8 +520,14 @@
         [lane // deep % 9, lane % deep, lane // (9 * deep)] + [lane * 0] * 5
     ).astype(np.int32)
     tap = np.arange(27)
+    ahead, back = tap % 9, (2 - tap // 3 % 3) * 3 + tap % 3
+    never = np.full(5, -1)
     thin_sub = np.stack(
-        [tap // 9, tap % 9, (2 - tap // 3 % 3) * 3 + tap % 3], 1
+        [
+            np.concatenate([low, never, high, never])
+            for low, high in ((tap // 9, tap // 9), (ahead, ahead + 9), (back, back + 9))
+        ],
+        1,
     ).astype(np.int32)
     lane = np.arange(27 * channels)
     b, a, c = lane // channels // 9, lane // channels // 3 % 3, lane // channels % 3

time: 23.9 us -> 23.5 us (0.983)
  Pallas kernels: 9.35 us -> 8.95 us
  starting transfers between devices: 8.81 us -> 9.18 us
  waiting for transfers between devices: 4.13 us -> 3.78 us
    ppermute x2, starting transfers between devices: 4.24 us -> 4.62 us  [swapped(): return lax.ppermute(value, axis, [(0, 1), (1, 0)])]
    ppermute x2, waiting for transfers between devices: 1.71 us -> 1.36 us  [gathered(): other = lax.ppermute(block, 'gz', pairs)]
    pallas_call x1, Pallas kernels: 2.29 us -> 2 us  [local_body(): block, strip, laid_out = gathered(noisy, prepared(*given))]
  transfers between devices with their start and end apart: 4 -> 4, of which waited for: 3 -> 3; matrix products, arithmetic and copies ran while one was open for 0% -> 0% of each run, Pallas kernels for 10% -> 9%
where the time goes in v8:
time: 23.5 us; the launch traced here: 23.1 us
  starting transfers between devices  9.18 us (39%)
  Pallas kernels  8.95 us (38%)
  waiting for transfers between devices  3.78 us (16%)
  between operations  0.71 us (3%)
  other arithmetic  0.36 us (2%)
    pallas_call x1, Pallas kernels, local_body(): pl.pallas_call(functools.partial(kernel, (deep, depth, channels, pitch, h...  6.95 us
    ppermute x2, starting transfers between devices, swapped(): return lax.ppermute(value, axis, [(0, 1), (1, 0)])  4.62 us
    ppermute x2, starting transfers between devices, gathered(): other = lax.ppermute(block, 'gz', pairs)  4.56 us
    ppermute x2, waiting for transfers between devices, swapped(): return lax.ppermute(value, axis, [(0, 1), (1, 0)])  2.42 us
    pallas_call x1, Pallas kernels, local_body(): block, strip, laid_out = gathered(noisy, prepared(*given))  2 us
    ppermute x2, waiting for transfers between devices, gathered(): other = lax.ppermute(block, 'gz', pairs)  1.36 us
  transfers between devices with their start and end apart: 4, of which 3 were waited for; matrix products, arithmetic and copies ran while one was open for 0% of the time, Pallas kernels for 9%

profile of v8, /device:TPU:1, one launch (start us, length us, event | category | flops | bytes accessed | tf_op | source)
XLA Modules:
  0.0 23.1 jit_solution(15205808952220244815)
XLA Ops:
  0.6 2.2 %collective-permute-start = (f32[4,8,128]{2,1,0:T(8,128)}, f32[4,8,128]{2,1,0:T(8,128)S(1)}, u32[]{:S(2)}, u32[]{:S(2)}) collective-permute-start(f32[4,8,128]{2,1,0:T(8,128)} %param.15), channel_id=1, source_target_pairs={{0,4},{4,0},{8,12},{12,8},{1,5},{5,1},{9,13},{13,9},{2,6},{6,2},{1... | collective-permute-start | bytes 49160 | tf_op jit(solution)/shard_map/ppermute | solution.py:134
  2.8 0.0 copy-start
  2.8 2.0 %shard_map.158 = (bf16[512,432]{1,0:T(8,128)(2,1)S(1)}, bf16[96,432]{1,0:T(8,128)(2,1)S(1)}, bf16[96,432]{1,0:T(8,128)(2,1)S(1)}, bf16[48,432]{1,0:T(8,128)(2,1)S(1)}, f32[16,128]{1,0:T(8,128)S(1)}) custom-call(f32[27,1,32]{2,1,0:T(1,128)} %bitcast.12, f32[1,16]{1,0:T(1,128)} %bitcast.13, f32[432,32]{1,0:T(8,128)} %bitcast.10, f32[1,16]{1,0:T(1,128)} %bitcast.14, ...), custom_call_target="tpu_custom_call" | custom-call | tf_op jit(solution)/shard_map/pallas_call | solution.py:571
  4.8 0.0 collective-permute-done
  4.8 0.0 copy-done
  4.9 2.4 %collective-permute-start.1 = (f32[8,8,128]{2,1,0:T(8,128)S(1)}, f32[8,8,128]{2,1,0:T(8,128)S(1)}, u32[]{:S(2)}, u32[]{:S(2)}) collective-permute-start(f32[8,8,128]{2,1,0:T(8,128)S(1)} %maximum_select_fusion.2), channel_id=1, source_target_pairs={{0,8},{4,12},{8,0},{12,4},{1,9},{5,13},{9,1},{13,5},{2,10},{6,14},... | collective-permute-start | bytes 98312 | tf_op jit(solution)/shard_map/ppermute | solution.py:134
  7.2 1.4 %collective-permute-done.1 = f32[8,8,128]{2,1,0:T(8,128)S(1)} collective-permute-done((f32[8,8,128]{2,1,0:T(8,128)S(1)}, f32[8,8,128]{2,1,0:T(8,128)S(1)}, u32[]{:S(2)}, u32[]{:S(2)}) %collective-permute-start.1) | collective-permute-done | bytes 32800 | tf_op jit(solution)/shard_map/ppermute | solution.py:134
  8.7 1.3 %collective-permute-start.2 = (f32[16,4,128]{2,1,0:T(4,128)S(1)}, f32[16,4,128]{2,1,0:T(4,128)S(1)}, u32[]{:S(2)}, u32[]{:S(2)}) collective-permute-start(f32[16,4,128]{2,1,0:T(4,128)S(1)} %rev.9), channel_id=1, source_target_pairs={{0,2},{2,0},{1,3},{3,1},{4,6},{6,4},{5,7},{7,5},{8,10},{10,8},{9,1... | collective-permute-start | bytes 98312 | tf_op jit(solution)/shard_map/ppermute | solution.py:125
  10.0 1.6 %collective-permute-done.2 = f32[16,4,128]{2,1,0:T(4,128)S(1)} collective-permute-done((f32[16,4,128]{2,1,0:T(4,128)S(1)}, f32[16,4,128]{2,1,0:T(4,128)S(1)}, u32[]{:S(2)}, u32[]{:S(2)}) %collective-permute-start.2) | collective-permute-done | bytes 32800 | tf_op jit(solution)/shard_map/ppermute | solution.py:125
  11.5 0.1 fusion.2
  11.6 3.3 %collective-permute-start.3 = (f32[16,12,4]{2,1,0:T(8,128)S(1)}, f32[16,12,4]{2,1,0:T(8,128)S(1)}, u32[]{:S(2)}, u32[]{:S(2)}) collective-permute-start(f32[16,12,4]{2,1,0:T(8,128)S(1)} %fusion.2), channel_id=1, source_target_pairs={{0,1},{1,0},{2,3},{3,2},{4,5},{5,4},{6,7},{7,6},{8,9},{9,8},{10,11... | collective-permute-start | bytes 9224 | tf_op jit(solution)/shard_map/ppermute | solution.py:125
  15.0 0.1 fusion.4
  15.1 0.9 %collective-permute-done.3 = f32[16,12,4]{2,1,0:T(8,128)S(1)} collective-permute-done((f32[16,12,4]{2,1,0:T(8,128)S(1)}, f32[16,12,4]{2,1,0:T(8,128)S(1)}, u32[]{:S(2)}, u32[]{:S(2)}) %collective-permute-start.3) | collective-permute-done | bytes 3104 | tf_op jit(solution)/shard_map/ppermute | solution.py:125
  16.0 0.1 maximum_select_fusion.strip_ref
  16.1 7.0 %shard_map.159 = (f32[4,8,128]{2,1,0:T(8,128)}, f32[16,4,8,128]{3,2,1,0:T(8,128)}) custom-call(f32[16,12,128]{2,1,0:T(8,128)S(1)} %pad_maximum_fusion.block_ref, f32[16,12,12]{2,1,0:T(8,128)S(1)} %maximum_select_fusion.strip_ref, bf16[512,432]{1,0:T(8,128)(2,1)S(1)} %get-tuple-element.19.w1_ref, bf16[96,432]{1,0:T(8,128)(2,1)S(1)} %get-tuple-element.20.w2_ref, ...), custom_call_target="tpu_custom_call" | custom-call | tf_op jit(solution)/shard_map/pallas_call | solution.py:576
  (7 shorter events, 0.1 us)
Async XLA Ops:
  0.6 4.2 %collective-permute-start = (f32[4,8,128]{2,1,0:T(8,128)}, f32[4,8,128]{2,1,0:T(8,128)S(1)}, u32[]{:S(2)}, u32[]{:S(2)}) collective-permute-start(f32[4,8,128]{2,1,0:T(8,128)} %param.15), channel_id=1, source_target_pairs={{0,4},{4,0},{8,12},{12,8},{1,5},{5,1},{9,13},{13,9},{2,6},{6,2},{1... | collective-permute-start | bytes 49160 | tf_op jit(solution)/shard_map/ppermute | solution.py:134
  2.8 2.0 %copy-start = (f32[4,8,128]{2,1,0:T(8,128)S(1)}, f32[4,8,128]{2,1,0:T(8,128)}, u32[]{:S(2)}) copy-start(f32[4,8,128]{2,1,0:T(8,128)} %param.15) | copy-start | bytes 49156
  4.9 3.7 %collective-permute-start.1 = (f32[8,8,128]{2,1,0:T(8,128)S(1)}, f32[8,8,128]{2,1,0:T(8,128)S(1)}, u32[]{:S(2)}, u32[]{:S(2)}) collective-permute-start(f32[8,8,128]{2,1,0:T(8,128)S(1)} %maximum_select_fusion.2), channel_id=1, source_target_pairs={{0,8},{4,12},{8,0},{12,4},{1,9},{5,13},{9,1},{13,5},{2,10},{6,14},... | collective-permute-start | bytes 98312 | tf_op jit(solution)/shard_map/ppermute | solution.py:134
  8.7 2.8 %collective-permute-start.2 = (f32[16,4,128]{2,1,0:T(4,128)S(1)}, f32[16,4,128]{2,1,0:T(4,128)S(1)}, u32[]{:S(2)}, u32[]{:S(2)}) collective-permute-start(f32[16,4,128]{2,1,0:T(4,128)S(1)} %rev.9), channel_id=1, source_target_pairs={{0,2},{2,0},{1,3},{3,1},{4,6},{6,4},{5,7},{7,5},{8,10},{10,8},{9,1... | collective-permute-start | bytes 98312 | tf_op jit(solution)/shard_map/ppermute | solution.py:125
  11.6 4.3 %collective-permute-start.3 = (f32[16,12,4]{2,1,0:T(8,128)S(1)}, f32[16,12,4]{2,1,0:T(8,128)S(1)}, u32[]{:S(2)}, u32[]{:S(2)}) collective-permute-start(f32[16,12,4]{2,1,0:T(8,128)S(1)} %fusion.2), channel_id=1, source_target_pairs={{0,1},{1,0},{2,3},{3,2},{4,5},{5,4},{6,7},{7,6},{8,9},{9,8},{10,11... | collective-permute-start | bytes 9224 | tf_op jit(solution)/shard_map/ppermute | solution.py:125

commit v9 on v8

--- a/solution.py
+++ b/solution.py
@@ -378,7 +378,8 @@
         (n + 1) * LANES for n in (first_rows, second_rows, third_rows)
     )
     todo = chunks(first_span)
-    part = depth * 2 * channels
+    share = min(2 * depth, deep)
+    part = share * 2 * channels
 
     def thin_block(b, chunk):
         at, length = chunk
@@ -400,9 +401,9 @@
             hidden,
         )
         wide_columns(z + 1, clean(hidden))
-        if z // depth + 1 < deep // depth:
-            for chunk in todo[z % depth :: depth]:
-                thin_block(z // depth + 1, chunk)
+        if z // share + 1 < deep // share:
+            for chunk in todo[z % share :: share]:
+                thin_block(z // share + 1, chunk)
         if 0 < z <= AHEAD:
             waiting += [(z - 1, chunk) for chunk in todo]
         for _ in range(min(PACE, len(waiting))):

time: 23.5 us -> 23.1 us (0.983)
  Pallas kernels: 8.95 us -> 8.56 us
    pallas_call x1, Pallas kernels: 6.95 us -> 6.56 us  [local_body(): pl.pallas_call(functools.partial(kernel, (deep, depth, channels, pitch, h...]
where the time goes in v9:
time: 23.1 us; the launch traced here: 22.7 us
  starting transfers between devices  9.18 us (40%)
  Pallas kernels  8.56 us (37%)
  waiting for transfers between devices  3.78 us (16%)
  between operations  0.71 us (3%)
  other arithmetic  0.36 us (2%)
    pallas_call x1, Pallas kernels, local_body(): pl.pallas_call(functools.partial(kernel, (deep, depth, channels, pitch, h...  6.56 us
    ppermute x2, starting transfers between devices, swapped(): return lax.ppermute(value, axis, [(0, 1), (1, 0)])  4.62 us
    ppermute x2, starting transfers between devices, gathered(): other = lax.ppermute(block, 'gz', pairs)  4.56 us
    ppermute x2, waiting for transfers between devices, swapped(): return lax.ppermute(value, axis, [(0, 1), (1, 0)])  2.42 us
    pallas_call x1, Pallas kernels, local_body(): block, strip, laid_out = gathered(noisy, prepared(*given))  2 us
    ppermute x2, waiting for transfers between devices, gathered(): other = lax.ppermute(block, 'gz', pairs)  1.36 us
  transfers between devices with their start and end apart: 4, of which 3 were waited for; matrix products, arithmetic and copies ran while one was open for 0% of the time, Pallas kernels for 9%

profile of v9, /device:TPU:1, one launch (start us, length us, event | category | flops | bytes accessed | tf_op | source)
XLA Modules:
  0.0 22.7 jit_solution(2190653396256579850)
XLA Ops:
  0.6 2.2 %collective-permute-start = (f32[4,8,128]{2,1,0:T(8,128)}, f32[4,8,128]{2,1,0:T(8,128)S(1)}, u32[]{:S(2)}, u32[]{:S(2)}) collective-permute-start(f32[4,8,128]{2,1,0:T(8,128)} %param.15), channel_id=1, source_target_pairs={{0,4},{4,0},{8,12},{12,8},{1,5},{5,1},{9,13},{13,9},{2,6},{6,2},{1... | collective-permute-start | bytes 49160 | tf_op jit(solution)/shard_map/ppermute | solution.py:134
  2.8 0.0 copy-start
  2.8 2.0 %shard_map.158 = (bf16[512,432]{1,0:T(8,128)(2,1)S(1)}, bf16[96,432]{1,0:T(8,128)(2,1)S(1)}, bf16[96,432]{1,0:T(8,128)(2,1)S(1)}, bf16[48,432]{1,0:T(8,128)(2,1)S(1)}, f32[16,128]{1,0:T(8,128)S(1)}) custom-call(f32[27,1,32]{2,1,0:T(1,128)} %bitcast.12, f32[1,16]{1,0:T(1,128)} %bitcast.13, f32[432,32]{1,0:T(8,128)} %bitcast.10, f32[1,16]{1,0:T(1,128)} %bitcast.14, ...), custom_call_target="tpu_custom_call" | custom-call | tf_op jit(solution)/shard_map/pallas_call | solution.py:572
  4.8 0.0 collective-permute-done
  4.8 0.0 copy-done
  4.9 2.4 %collective-permute-start.1 = (f32[8,8,128]{2,1,0:T(8,128)S(1)}, f32[8,8,128]{2,1,0:T(8,128)S(1)}, u32[]{:S(2)}, u32[]{:S(2)}) collective-permute-start(f32[8,8,128]{2,1,0:T(8,128)S(1)} %maximum_select_fusion.2), channel_id=1, source_target_pairs={{0,8},{4,12},{8,0},{12,4},{1,9},{5,13},{9,1},{13,5},{2,10},{6,14},... | collective-permute-start | bytes 98312 | tf_op jit(solution)/shard_map/ppermute | solution.py:134
  7.2 1.4 %collective-permute-done.1 = f32[8,8,128]{2,1,0:T(8,128)S(1)} collective-permute-done((f32[8,8,128]{2,1,0:T(8,128)S(1)}, f32[8,8,128]{2,1,0:T(8,128)S(1)}, u32[]{:S(2)}, u32[]{:S(2)}) %collective-permute-start.1) | collective-permute-done | bytes 32800 | tf_op jit(solution)/shard_map/ppermute | solution.py:134
  8.7 1.3 %collective-permute-start.2 = (f32[16,4,128]{2,1,0:T(4,128)S(1)}, f32[16,4,128]{2,1,0:T(4,128)S(1)}, u32[]{:S(2)}, u32[]{:S(2)}) collective-permute-start(f32[16,4,128]{2,1,0:T(4,128)S(1)} %rev.9), channel_id=1, source_target_pairs={{0,2},{2,0},{1,3},{3,1},{4,6},{6,4},{5,7},{7,5},{8,10},{10,8},{9,1... | collective-permute-start | bytes 98312 | tf_op jit(solution)/shard_map/ppermute | solution.py:125
  10.0 1.6 %collective-permute-done.2 = f32[16,4,128]{2,1,0:T(4,128)S(1)} collective-permute-done((f32[16,4,128]{2,1,0:T(4,128)S(1)}, f32[16,4,128]{2,1,0:T(4,128)S(1)}, u32[]{:S(2)}, u32[]{:S(2)}) %collective-permute-start.2) | collective-permute-done | bytes 32800 | tf_op jit(solution)/shard_map/ppermute | solution.py:125
  11.5 0.1 fusion.2
  11.6 3.3 %collective-permute-start.3 = (f32[16,12,4]{2,1,0:T(8,128)S(1)}, f32[16,12,4]{2,1,0:T(8,128)S(1)}, u32[]{:S(2)}, u32[]{:S(2)}) collective-permute-start(f32[16,12,4]{2,1,0:T(8,128)S(1)} %fusion.2), channel_id=1, source_target_pairs={{0,1},{1,0},{2,3},{3,2},{4,5},{5,4},{6,7},{7,6},{8,9},{9,8},{10,11... | collective-permute-start | bytes 9224 | tf_op jit(solution)/shard_map/ppermute | solution.py:125
  15.0 0.1 fusion.4
  15.1 0.9 %collective-permute-done.3 = f32[16,12,4]{2,1,0:T(8,128)S(1)} collective-permute-done((f32[16,12,4]{2,1,0:T(8,128)S(1)}, f32[16,12,4]{2,1,0:T(8,128)S(1)}, u32[]{:S(2)}, u32[]{:S(2)}) %collective-permute-start.3) | collective-permute-done | bytes 3104 | tf_op jit(solution)/shard_map/ppermute | solution.py:125
  16.0 0.1 maximum_select_fusion.strip_ref
  16.1 6.6 %shard_map.159 = (f32[4,8,128]{2,1,0:T(8,128)}, f32[16,4,8,128]{3,2,1,0:T(8,128)}) custom-call(f32[16,12,128]{2,1,0:T(8,128)S(1)} %pad_maximum_fusion.block_ref, f32[16,12,12]{2,1,0:T(8,128)S(1)} %maximum_select_fusion.strip_ref, bf16[512,432]{1,0:T(8,128)(2,1)S(1)} %get-tuple-element.19.w1_ref, bf16[96,432]{1,0:T(8,128)(2,1)S(1)} %get-tuple-element.20.w2_ref, ...), custom_call_target="tpu_custom_call" | custom-call | tf_op jit(solution)/shard_map/pallas_call | solution.py:577
  (7 shorter events, 0.1 us)
Async XLA Ops:
  0.6 4.2 %collective-permute-start = (f32[4,8,128]{2,1,0:T(8,128)}, f32[4,8,128]{2,1,0:T(8,128)S(1)}, u32[]{:S(2)}, u32[]{:S(2)}) collective-permute-start(f32[4,8,128]{2,1,0:T(8,128)} %param.15), channel_id=1, source_target_pairs={{0,4},{4,0},{8,12},{12,8},{1,5},{5,1},{9,13},{13,9},{2,6},{6,2},{1... | collective-permute-start | bytes 49160 | tf_op jit(solution)/shard_map/ppermute | solution.py:134
  2.8 2.0 %copy-start = (f32[4,8,128]{2,1,0:T(8,128)S(1)}, f32[4,8,128]{2,1,0:T(8,128)}, u32[]{:S(2)}) copy-start(f32[4,8,128]{2,1,0:T(8,128)} %param.15) | copy-start | bytes 49156
  4.9 3.7 %collective-permute-start.1 = (f32[8,8,128]{2,1,0:T(8,128)S(1)}, f32[8,8,128]{2,1,0:T(8,128)S(1)}, u32[]{:S(2)}, u32[]{:S(2)}) collective-permute-start(f32[8,8,128]{2,1,0:T(8,128)S(1)} %maximum_select_fusion.2), channel_id=1, source_target_pairs={{0,8},{4,12},{8,0},{12,4},{1,9},{5,13},{9,1},{13,5},{2,10},{6,14},... | collective-permute-start | bytes 98312 | tf_op jit(solution)/shard_map/ppermute | solution.py:134
  8.7 2.8 %collective-permute-start.2 = (f32[16,4,128]{2,1,0:T(4,128)S(1)}, f32[16,4,128]{2,1,0:T(4,128)S(1)}, u32[]{:S(2)}, u32[]{:S(2)}) collective-permute-start(f32[16,4,128]{2,1,0:T(4,128)S(1)} %rev.9), channel_id=1, source_target_pairs={{0,2},{2,0},{1,3},{3,1},{4,6},{6,4},{5,7},{7,5},{8,10},{10,8},{9,1... | collective-permute-start | bytes 98312 | tf_op jit(solution)/shard_map/ppermute | solution.py:125
  11.6 4.3 %collective-permute-start.3 = (f32[16,12,4]{2,1,0:T(8,128)S(1)}, f32[16,12,4]{2,1,0:T(8,128)S(1)}, u32[]{:S(2)}, u32[]{:S(2)}) collective-permute-start(f32[16,12,4]{2,1,0:T(8,128)S(1)} %fusion.2), channel_id=1, source_target_pairs={{0,1},{1,0},{2,3},{3,2},{4,5},{5,4},{6,7},{7,6},{8,9},{9,8},{10,11... | collective-permute-start | bytes 9224 | tf_op jit(solution)/shard_map/ppermute | solution.py:125

commit v10 on v9

--- a/solution.py
+++ b/solution.py
@@ -325,7 +325,7 @@
             wide_lo[at : at + channels, lanes] = l
 
     def chunks(length):
-        return [(i, min(2 * LANES, length - i)) for i in range(0, length, 2 * LANES)]
+        return [(i, min(4 * LANES, length - i)) for i in range(0, length, 4 * LANES)]
 
     def convolve(w_ref, z, chunk):
         at, length = chunk

time: 23.1 us -> 23 us (level)
  no operation moved by 1% of the time
where the time goes in v10:
time: 23 us; the launch traced here: 22.6 us
  starting transfers between devices  9.18 us (40%)
  Pallas kernels  8.48 us (37%)
  waiting for transfers between devices  3.78 us (16%)
  between operations  0.71 us (3%)
  other arithmetic  0.36 us (2%)
    pallas_call x1, Pallas kernels, local_body(): pl.pallas_call(functools.partial(kernel, (deep, depth, channels, pitch, h...  6.49 us
    ppermute x2, starting transfers between devices, swapped(): return lax.ppermute(value, axis, [(0, 1), (1, 0)])  4.62 us
    ppermute x2, starting transfers between devices, gathered(): other = lax.ppermute(block, 'gz', pairs)  4.56 us
    ppermute x2, waiting for transfers between devices, swapped(): return lax.ppermute(value, axis, [(0, 1), (1, 0)])  2.42 us
    pallas_call x1, Pallas kernels, local_body(): block, strip, laid_out = gathered(noisy, prepared(*given))  2 us
    ppermute x2, waiting for transfers between devices, gathered(): other = lax.ppermute(block, 'gz', pairs)  1.36 us
  transfers between devices with their start and end apart: 4, of which 3 were waited for; matrix products, arithmetic and copies ran while one was open for 0% of the time, Pallas kernels for 9%

profile of v10, /device:TPU:1, one launch (start us, length us, event | category | flops | bytes accessed | tf_op | source)
XLA Modules:
  0.0 22.6 jit_solution(6304779295394727885)
XLA Ops:
  0.6 2.2 %collective-permute-start = (f32[4,8,128]{2,1,0:T(8,128)}, f32[4,8,128]{2,1,0:T(8,128)S(1)}, u32[]{:S(2)}, u32[]{:S(2)}) collective-permute-start(f32[4,8,128]{2,1,0:T(8,128)} %param.15), channel_id=1, source_target_pairs={{0,4},{4,0},{8,12},{12,8},{1,5},{5,1},{9,13},{13,9},{2,6},{6,2},{1... | collective-permute-start | bytes 49160 | tf_op jit(solution)/shard_map/ppermute | solution.py:134
  2.8 0.0 copy-start
  2.8 2.0 %shard_map.158 = (bf16[512,432]{1,0:T(8,128)(2,1)S(1)}, bf16[96,432]{1,0:T(8,128)(2,1)S(1)}, bf16[96,432]{1,0:T(8,128)(2,1)S(1)}, bf16[48,432]{1,0:T(8,128)(2,1)S(1)}, f32[16,128]{1,0:T(8,128)S(1)}) custom-call(f32[27,1,32]{2,1,0:T(1,128)} %bitcast.12, f32[1,16]{1,0:T(1,128)} %bitcast.13, f32[432,32]{1,0:T(8,128)} %bitcast.10, f32[1,16]{1,0:T(1,128)} %bitcast.14, ...), custom_call_target="tpu_custom_call" | custom-call | tf_op jit(solution)/shard_map/pallas_call | solution.py:572
  4.8 0.0 collective-permute-done
  4.8 0.0 copy-done
  4.9 2.4 %collective-permute-start.1 = (f32[8,8,128]{2,1,0:T(8,128)S(1)}, f32[8,8,128]{2,1,0:T(8,128)S(1)}, u32[]{:S(2)}, u32[]{:S(2)}) collective-permute-start(f32[8,8,128]{2,1,0:T(8,128)S(1)} %maximum_select_fusion.2), channel_id=1, source_target_pairs={{0,8},{4,12},{8,0},{12,4},{1,9},{5,13},{9,1},{13,5},{2,10},{6,14},... | collective-permute-start | bytes 98312 | tf_op jit(solution)/shard_map/ppermute | solution.py:134
  7.2 1.4 %collective-permute-done.1 = f32[8,8,128]{2,1,0:T(8,128)S(1)} collective-permute-done((f32[8,8,128]{2,1,0:T(8,128)S(1)}, f32[8,8,128]{2,1,0:T(8,128)S(1)}, u32[]{:S(2)}, u32[]{:S(2)}) %collective-permute-start.1) | collective-permute-done | bytes 32800 | tf_op jit(solution)/shard_map/ppermute | solution.py:134
  8.7 1.3 %collective-permute-start.2 = (f32[16,4,128]{2,1,0:T(4,128)S(1)}, f32[16,4,128]{2,1,0:T(4,128)S(1)}, u32[]{:S(2)}, u32[]{:S(2)}) collective-permute-start(f32[16,4,128]{2,1,0:T(4,128)S(1)} %rev.9), channel_id=1, source_target_pairs={{0,2},{2,0},{1,3},{3,1},{4,6},{6,4},{5,7},{7,5},{8,10},{10,8},{9,1... | collective-permute-start | bytes 98312 | tf_op jit(solution)/shard_map/ppermute | solution.py:125
  10.0 1.6 %collective-permute-done.2 = f32[16,4,128]{2,1,0:T(4,128)S(1)} collective-permute-done((f32[16,4,128]{2,1,0:T(4,128)S(1)}, f32[16,4,128]{2,1,0:T(4,128)S(1)}, u32[]{:S(2)}, u32[]{:S(2)}) %collective-permute-start.2) | collective-permute-done | bytes 32800 | tf_op jit(solution)/shard_map/ppermute | solution.py:125
  11.5 0.1 fusion.2
  11.6 3.3 %collective-permute-start.3 = (f32[16,12,4]{2,1,0:T(8,128)S(1)}, f32[16,12,4]{2,1,0:T(8,128)S(1)}, u32[]{:S(2)}, u32[]{:S(2)}) collective-permute-start(f32[16,12,4]{2,1,0:T(8,128)S(1)} %fusion.2), channel_id=1, source_target_pairs={{0,1},{1,0},{2,3},{3,2},{4,5},{5,4},{6,7},{7,6},{8,9},{9,8},{10,11... | collective-permute-start | bytes 9224 | tf_op jit(solution)/shard_map/ppermute | solution.py:125
  15.0 0.1 fusion.4
  15.1 0.9 %collective-permute-done.3 = f32[16,12,4]{2,1,0:T(8,128)S(1)} collective-permute-done((f32[16,12,4]{2,1,0:T(8,128)S(1)}, f32[16,12,4]{2,1,0:T(8,128)S(1)}, u32[]{:S(2)}, u32[]{:S(2)}) %collective-permute-start.3) | collective-permute-done | bytes 3104 | tf_op jit(solution)/shard_map/ppermute | solution.py:125
  16.0 0.1 maximum_select_fusion.strip_ref
  16.1 6.5 %shard_map.159 = (f32[4,8,128]{2,1,0:T(8,128)}, f32[16,4,8,128]{3,2,1,0:T(8,128)}) custom-call(f32[16,12,128]{2,1,0:T(8,128)S(1)} %pad_maximum_fusion.block_ref, f32[16,12,12]{2,1,0:T(8,128)S(1)} %maximum_select_fusion.strip_ref, bf16[512,432]{1,0:T(8,128)(2,1)S(1)} %get-tuple-element.19.w1_ref, bf16[96,432]{1,0:T(8,128)(2,1)S(1)} %get-tuple-element.20.w2_ref, ...), custom_call_target="tpu_custom_call" | custom-call | tf_op jit(solution)/shard_map/pallas_call | solution.py:577
  (7 shorter events, 0.1 us)
Async XLA Ops:
  0.6 4.2 %collective-permute-start = (f32[4,8,128]{2,1,0:T(8,128)}, f32[4,8,128]{2,1,0:T(8,128)S(1)}, u32[]{:S(2)}, u32[]{:S(2)}) collective-permute-start(f32[4,8,128]{2,1,0:T(8,128)} %param.15), channel_id=1, source_target_pairs={{0,4},{4,0},{8,12},{12,8},{1,5},{5,1},{9,13},{13,9},{2,6},{6,2},{1... | collective-permute-start | bytes 49160 | tf_op jit(solution)/shard_map/ppermute | solution.py:134
  2.8 2.0 %copy-start = (f32[4,8,128]{2,1,0:T(8,128)S(1)}, f32[4,8,128]{2,1,0:T(8,128)}, u32[]{:S(2)}) copy-start(f32[4,8,128]{2,1,0:T(8,128)} %param.15) | copy-start | bytes 49156
  4.9 3.7 %collective-permute-start.1 = (f32[8,8,128]{2,1,0:T(8,128)S(1)}, f32[8,8,128]{2,1,0:T(8,128)S(1)}, u32[]{:S(2)}, u32[]{:S(2)}) collective-permute-start(f32[8,8,128]{2,1,0:T(8,128)S(1)} %maximum_select_fusion.2), channel_id=1, source_target_pairs={{0,8},{4,12},{8,0},{12,4},{1,9},{5,13},{9,1},{13,5},{2,10},{6,14},... | collective-permute-start | bytes 98312 | tf_op jit(solution)/shard_map/ppermute | solution.py:134
  8.7 2.8 %collective-permute-start.2 = (f32[16,4,128]{2,1,0:T(4,128)S(1)}, f32[16,4,128]{2,1,0:T(4,128)S(1)}, u32[]{:S(2)}, u32[]{:S(2)}) collective-permute-start(f32[16,4,128]{2,1,0:T(4,128)S(1)} %rev.9), channel_id=1, source_target_pairs={{0,2},{2,0},{1,3},{3,1},{4,6},{6,4},{5,7},{7,5},{8,10},{10,8},{9,1... | collective-permute-start | bytes 98312 | tf_op jit(solution)/shard_map/ppermute | solution.py:125
  11.6 4.3 %collective-permute-start.3 = (f32[16,12,4]{2,1,0:T(8,128)S(1)}, f32[16,12,4]{2,1,0:T(8,128)S(1)}, u32[]{:S(2)}, u32[]{:S(2)}) collective-permute-start(f32[16,12,4]{2,1,0:T(8,128)S(1)} %fusion.2), channel_id=1, source_target_pairs={{0,1},{1,0},{2,3},{3,2},{4,5},{5,4},{6,7},{7,6},{8,9},{9,8},{10,11... | collective-permute-start | bytes 9224 | tf_op jit(solution)/shard_map/ppermute | solution.py:125
